TPU v7x, 512 devices: a whole 4x4x16 slice. The times are simulated.
512 devices in a mesh: grp: 4 (over y), clu: 128 (over x, z, core).
Axes of the slice: x: 4, y: 4, z: 16, core: 2. Of those that a mesh axis runs over, the one named last changes fastest.
Arguments:
- forces: bfloat16 [3, 32768, 512], P(None, 'clu'), may hold values from -6 to 6
- order: int32 [32768], P('clu'), may hold values from 0 to 32767, as said below
- bases: bfloat16 [2, 32, 3, 32768], P(None, None, None, 'clu'), may hold values from -0.21875 to 0.21875
- near_tiles: bfloat16 [128, 8, 768, 768], P('clu', 'grp'), may hold values from -0.078125 to 0.078125
- near_col: int32 [128, 8], P('clu', 'grp'), may hold values from 0 to 127, as said below
- far_basis: bfloat16 [128, 64, 32, 768], P('clu', 'grp'), may hold values from -0.03125 to 0.03125
- far_coupling: bfloat16 [128, 64, 32, 32], P('clu', 'grp'), may hold values from -1 to 1
- far_scale: float32 [128, 64], P('clu', 'grp'), may hold values from 0.5 to 2
- far_rank: int32 [128, 64], P('clu', 'grp'), may hold values from 8 to 32
- far_target: int32 [128, 64], P('clu', 'grp'), may hold values from 0 to 5, as said below
Outputs:
- velocity: float32 [3, 32768, 512], P(None, 'clu', 'grp')
Inputs may be any that keep to these rules, and one draw needn't show every extreme that they name: `order`: A permutation of the bead numbers; the 256 positions of row block c hold beads of chain blocks c - 1, c and c + 1 only, counted cyclically, exactly 64 of them from chain block c - 1 and exactly 64 from chain block c + 1. `near_col`: each near tile's column block lies within two blocks of its row block, counted cyclically. `far_target`: level l takes indices 2 ** (l + 1) - 2 to 2 ** (l + 2) - 3; the named cluster never contains the block's own row block.
All inputs are finite; a program needn't handle non-finite values.
Results may differ from a plain program's by a relative error of at most 0.0025.
Values may be sent and summed in bfloat16 or wider, within the bound.
No kernel may reach another device: no remote copies, remote signals or barrier semaphores. Data moves between devices by JAX's collectives and lax.ppermute only.
A program may use at most 64 MiB of HBM per device.

v0:
```python
import jax
import jax.numpy as jnp
from jax import lax
from jax.sharding import Mesh
from jax.sharding import PartitionSpec as P

CLU = ("clu_0", "clu_1", "clu_2")


def with_halo(cells, sides, width):
    for axis, dim in sides:
        count = lax.axis_size(axis)
        head = lax.slice_in_dim(cells, 0, width, axis=dim)
        tail = lax.slice_in_dim(cells, cells.shape[dim] - width, cells.shape[dim], axis=dim)
        cells = jnp.concatenate(
            [
                lax.ppermute(tail, axis, [(i, (i + 1) % count) for i in range(count)]),
                cells,
                lax.ppermute(head, axis, [((i + 1) % count, i) for i in range(count)]),
            ],
            axis=dim,
        )
    return cells


def from_behind(shard, axis, by):
    size = lax.axis_size(axis)
    return lax.ppermute(shard, axis, [(i, (i + by) % size) for i in range(size)])


def cut_along(shard, dim, size):
    before, after = (shard.shape[:dim], shard.shape[dim + 1 :])
    return jnp.moveaxis(shard.reshape(*before, size, -1, *after), dim, 0)


def sent_and_summed(shard, axis, dim):
    tiles = cut_along(shard, dim, lax.axis_size(axis))
    arrived = lax.all_to_all(tiles, axis, split_axis=0, concat_axis=0, tiled=True)
    return arrived.sum(axis=0)


def sum_in_two_steps(shard, axes, dim):
    far, near = axes
    own = sent_and_summed(cut_along(shard, dim, lax.axis_size(far)), near, dim + 1)
    return jnp.sum(lax.all_to_all(own, far, 0, 0, tiled=True), axis=0)


def padded_to(lines, size):
    spare = -len(lines) % size
    return jnp.pad(lines, [(0, spare)] + [(0, 0)] * (lines.ndim - 1))


def copy_for_each(shard, axis):
    copies = jnp.broadcast_to(shard, (lax.axis_size(axis), *shard.shape))
    return lax.all_to_all(copies, axis, split_axis=0, concat_axis=0, tiled=True)


def laid_out(tiles, dim):
    shape = list(tiles.shape[1:])
    shape[dim] *= tiles.shape[0]
    return jnp.moveaxis(tiles, 0, dim).reshape(shape)


def gathered_by_axis(shard, axes, dim):
    far, near = axes
    leading = copy_for_each(shard, far)
    tiles = jnp.swapaxes(copy_for_each(leading, near), 0, 1)
    return laid_out(tiles.reshape(-1, *shard.shape), dim)


def nested_sum(shard, axes):
    lines = shard.reshape(-1)
    own = sum_in_two_steps(
        padded_to(lines, lax.axis_size(axes[0]) * lax.axis_size(axes[1])), axes, 0
    )
    whole = gathered_by_axis(own, axes, 0)
    return whole[: len(lines)].reshape(shard.shape)


def nearby_forces(local_forces, order, clusters, own_index):
    tile_len = order.shape[0]
    extended = with_halo(local_forces, ((CLU, 1),), tile_len)
    start = (own_index - 1) * tile_len
    positions = jnp.mod(order - start, clusters * tile_len)
    own_block = jnp.take(extended, positions, axis=1)
    pieces = {0: own_block}
    for offset in (-2, -1, 1, 2):
        pieces[offset] = from_behind(own_block, CLU, -offset)
    return jnp.concatenate([pieces[offset] for offset in (-2, -1, 0, 1, 2)], axis=1)


def on_device(
    forces,
    order,
    bases,
    near_tiles,
    near_col,
    far_basis,
    far_coupling,
    far_scale,
    far_rank,
    far_target,
):
    clusters = lax.axis_size(CLU)
    own_index = lax.axis_index(CLU)
    tile_len = order.shape[0]
    columns = forces.shape[2]
    nearby = nearby_forces(forces, order, clusters, own_index)
    own_forces = nearby[:, 2 * tile_len : 3 * tile_len, :].reshape(3 * tile_len, columns)
    tiles = near_tiles[0]
    positions = jnp.mod(near_col[0] - own_index + 2, clusters)
    partial_value = jnp.zeros((3 * tile_len, columns), jnp.float32)
    for slot in range(tiles.shape[0]):
        column_block = lax.dynamic_slice_in_dim(
            nearby, positions[slot] * tile_len, tile_len, 1
        ).reshape(3 * tile_len, columns)
        partial_value = partial_value + jnp.dot(
            tiles[slot], column_block, preferred_element_type=jnp.float32
        )
    levels = bases.shape[0]
    rank = bases.shape[1]
    flat_bases = bases.reshape(levels * rank, 3 * tile_len)
    pieces = jnp.dot(flat_bases, own_forces, preferred_element_type=jnp.float32).reshape(
        levels, rank, columns
    )
    coarse_count = 2 ** (levels + 1) - 2
    slots = jnp.arange(coarse_count, dtype=jnp.int32)
    table = jnp.zeros((coarse_count, rank, columns), jnp.float32)
    for level in range(levels):
        count = 2 ** (level + 1)
        members = clusters // count
        target_slot = count - 2 + own_index // members
        table = table + (slots == target_slot).astype(jnp.float32)[:, None, None] * pieces[level]
    table = nested_sum(table, (("clu_0", "clu_1"), "clu_2"))
    targets = far_target[0]
    far_count = targets.shape[0]
    selector = (targets[:, None] == slots[None, :]).astype(jnp.float32)
    picked = jnp.dot(
        selector, table.reshape(coarse_count, rank * columns), precision=lax.Precision.HIGHEST
    ).reshape(far_count, rank, columns)
    keeping = (jnp.arange(rank, dtype=jnp.int32)[None, :] < far_rank[0][:, None]).astype(
        jnp.float32
    )
    masked = picked * keeping[:, :, None]
    coupled = jnp.einsum(
        "brs,bsn->brn", far_coupling[0].astype(jnp.float32), masked, precision=lax.Precision.HIGHEST
    )
    coupled = (coupled * far_scale[0][:, None, None]).astype(jnp.bfloat16)
    far_part = lax.dot_general(
        far_basis[0].reshape(far_count * rank, 3 * tile_len),
        coupled.reshape(far_count * rank, columns),
        (((0,), (0,)), ((), ())),
        preferred_element_type=jnp.float32,
    )
    partial_value = (partial_value + far_part).reshape(3, tile_len, columns)
    return sent_and_summed(partial_value, "grp", 2)


def solution(mesh):
    torus = Mesh(
        mesh.devices.reshape(mesh.shape["grp"], 4, 16, 2), ("grp", "clu_0", "clu_1", "clu_2")
    )
    in_specs = (
        P(None, CLU, None),
        P(CLU),
        P(None, None, None, CLU),
        P(CLU, "grp", None, None),
        P(CLU, "grp"),
        P(CLU, "grp", None, None),
        P(CLU, "grp", None, None),
        P(CLU, "grp"),
        P(CLU, "grp"),
        P(CLU, "grp"),
    )
    out_specs = P(None, CLU, "grp")
    return jax.shard_map(
        on_device, mesh=torus, in_specs=in_specs, out_specs=out_specs, check_vma=False
    )
```

profile of v0, /device:TPU:32, one launch (start us, length us, event | category | flops | bytes accessed | tf_op | source)
XLA Modules:
  0.0 153.2 jit_solution(1615564462221036528)
XLA Ops:
  0.0 0.0 copy-start
  0.0 2.0 %collective-permute-start = (bf16[3,256,512]{2,1,0:T(8,128)(2,1)}, bf16[3,256,512]{2,1,0:T(8,128)(2,1)S(1)}, u32[]{:S(2)}, u32[]{:S(2)}) collective-permute-start(bf16[3,256,512]{2,1,0:T(8,128)(2,1)} %param.10), channel_id=1, source_target_pairs={{0,1},{1,2},{2,3},{3,4},{4,5},{5,6},{6,7},{7,8},{8,9},{9,10},{10,1... | collective-permute-start | bytes 2359304 | tf_op jit(solution)/shard_map/ppermute | solution.py:17
  2.1 3.6 %collective-permute-start.1 = (bf16[3,256,512]{2,1,0:T(8,128)(2,1)}, bf16[3,256,512]{2,1,0:T(8,128)(2,1)S(1)}, u32[]{:S(2)}, u32[]{:S(2)}) collective-permute-start(bf16[3,256,512]{2,1,0:T(8,128)(2,1)} %param.10), channel_id=1, source_target_pairs={{1,0},{2,1},{3,2},{4,3},{5,4},{6,5},{7,6},{8,7},{9,8},{10,9},{11,1... | collective-permute-start | bytes 2359304 | tf_op jit(solution)/shard_map/ppermute | solution.py:19
  5.7 1.8 %copy.45 = bf16[3,256,512]{2,0,1:T(4,128)(2,1)S(1)} copy(bf16[3,256,512]{2,1,0:T(8,128)(2,1)} %param.10) | data formatting | bytes 1572864 | tf_op args[0]
  7.6 1.0 copy.58
  8.6 0.7 compare_and_fusion
  9.3 4.3 %collective-permute-done = bf16[3,256,512]{2,1,0:T(8,128)(2,1)S(1)} collective-permute-done((bf16[3,256,512]{2,1,0:T(8,128)(2,1)}, bf16[3,256,512]{2,1,0:T(8,128)(2,1)S(1)}, u32[]{:S(2)}, u32[]{:S(2)}) %collective-permute-start) | collective-permute-done | bytes 786464 | tf_op jit(solution)/shard_map/ppermute | solution.py:17
  13.6 0.7 copy.44
  14.3 1.2 collective-permute-done.1
  15.5 0.7 copy.46
  16.2 8.6 %pad_maximum_fusion = bf16[3,768,512]{2,0,1:T(4,128)(2,1)} fusion(bf16[3,256,512]{2,0,1:T(4,128)(2,1)S(1)} %copy.46, bf16[3,256,512]{2,0,1:T(4,128)(2,1)S(1)} %copy.45, bf16[3,256,512]{2,0,1:T(4,128)(2,1)S(1)} %copy.44), kind=kLoop, calls=%fused_computation.1 | loop fusion | flops 2359296 | bytes 4718592 | tf_op jit(solution)/shard_map/concatenate | solution.py:15
  24.8 3.4 %gather_fusion = bf16[256,3,512]{2,1,0:T(4,128)(2,1)S(1)} fusion(bf16[3,768,512]{2,0,1:T(4,128)(2,1)} %pad_maximum_fusion, s32[1024]{0:T(1024)S(1)} %pad_clamp_fusion), kind=kCustom, calls=%fused_computation | custom fusion | bytes 1573888 | tf_op jit(solution)/shard_map/jit(_take)/gather | solution.py:85
  28.3 1.0 select_bitcast_fusion
  29.3 0.2 copy.47
  29.5 0.0 copy-start.7
  29.5 0.0 copy-start.5
  29.5 3.8 %collective-permute-start.2 = (bf16[3,256,512]{2,1,0:T(8,128)(2,1)S(1)}, bf16[3,256,512]{2,1,0:T(8,128)(2,1)}, u32[]{:S(2)}, u32[]{:S(2)}) collective-permute-start(bf16[3,256,512]{2,1,0:T(8,128)(2,1)S(1)} %copy.47), channel_id=1, source_target_pairs={{0,2},{1,3},{2,4},{3,5},{4,6},{5,7},{6,8},{7,9},{8,10},{9,11},{10,... | collective-permute-start | bytes 2359304 | tf_op jit(solution)/shard_map/ppermute | solution.py:28
  33.4 0.2 convolution_bitcast_fusion
  33.6 0.1 multiply_add_fusion
  33.7 0.3 add.74
  34.1 5.4 %all_to_all.33 = f32[2,64,768]{2,1,0:T(8,128)S(1)} all-to-all(f32[2,64,768]{2,1,0:T(8,128)S(1)} %copy.59), channel_id=1, replica_groups=mesh['grp'=4,'clu_0'=4,'clu_1'=16,'clu_2'=2] {'clu_2'}, dimensions={0} | all-to-all | bytes 786432 | tf_op jit(solution)/shard_map/all_to_all | solution.py:38
  39.4 0.8 all_to_all.22
  40.3 16.9 %all-to-all-start.1 = ((f32[64,1,768]{2,1,0:T(1,128)}), f32[64,1,768]{2,1,0:T(1,128)}, u32[]{:S(2)}, u32[]{:S(2)}) async-start(f32[64,1,768]{2,1,0:T(1,128)} %all_to_all.22), calls=%async_computation.1 | async-start | bytes 393216 | tf_op jit(solution)/shard_map/all_to_all | solution.py:45
  57.2 1.9 %collective-permute-start.3 = (bf16[3,256,512]{2,1,0:T(8,128)(2,1)S(1)}, bf16[3,256,512]{2,1,0:T(8,128)(2,1)S(1)}, u32[]{:S(2)}, u32[]{:S(2)}) collective-permute-start(bf16[3,256,512]{2,1,0:T(8,128)(2,1)S(1)} %copy.47), channel_id=1, source_target_pairs={{0,1},{1,2},{2,3},{3,4},{4,5},{5,6},{6,7},{7,8},{8,9},{9,10},{10,1... | collective-permute-start | bytes 2359304 | tf_op jit(solution)/shard_map/ppermute | solution.py:28
  59.2 0.7 fusion.16
  61.1 0.0 copy-done.5
  61.1 3.6 %collective-permute-start.4 = (bf16[3,256,512]{2,1,0:T(8,128)(2,1)S(1)}, bf16[3,256,512]{2,1,0:T(8,128)(2,1)}, u32[]{:S(2)}, u32[]{:S(2)}) collective-permute-start(bf16[3,256,512]{2,1,0:T(8,128)(2,1)S(1)} %copy.47), channel_id=1, source_target_pairs={{0,127},{1,0},{2,1},{3,2},{4,3},{5,4},{6,5},{7,6},{8,7},{9,8},{10,... | collective-permute-start | bytes 2359304 | tf_op jit(solution)/shard_map/ppermute | solution.py:28
  64.8 5.8 %collective-permute-start.5 = (bf16[3,256,512]{2,1,0:T(8,128)(2,1)S(1)}, bf16[3,256,512]{2,1,0:T(8,128)(2,1)}, u32[]{:S(2)}, u32[]{:S(2)}) collective-permute-start(bf16[3,256,512]{2,1,0:T(8,128)(2,1)S(1)} %copy.47), channel_id=1, source_target_pairs={{0,126},{1,127},{2,0},{3,1},{4,2},{5,3},{6,4},{7,5},{8,6},{9,7},{1... | collective-permute-start | bytes 2359304 | tf_op jit(solution)/shard_map/ppermute | solution.py:28
  70.5 4.5 %all-to-all-done.1 = f32[64,1,768]{2,1,0:T(1,128)} async-done(((f32[64,1,768]{2,1,0:T(1,128)}), f32[64,1,768]{2,1,0:T(1,128)}, u32[]{:S(2)}, u32[]{:S(2)}) %all-to-all-start.1) | async-done | bytes 196640 | tf_op jit(solution)/shard_map/all_to_all | solution.py:45
  75.0 1.1 reduce_sum.28
  76.1 0.8 broadcast_in_dim.26
  76.9 8.8 %all-to-all-start.2 = ((f32[64,1,768]{2,1,0:T(1,128)}), f32[64,1,768]{2,1,0:T(1,128)}, u32[]{:S(2)}, u32[]{:S(2)}) async-start(f32[64,1,768]{2,1,0:T(1,128)} %broadcast_in_dim.26), calls=%async_computation.2 | async-start | bytes 393216 | tf_op jit(solution)/shard_map/all_to_all | solution.py:55
  85.6 0.0 collective-permute-done.2
  85.6 1.8 %copy_dynamic-update-slice_fusion.3 = bf16[3,1280,512]{2,0,1:T(4,128)(2,1)S(1)} fusion(bf16[3,256,512]{2,1,0:T(8,128)(2,1)} %collective-permute-done.2), kind=kLoop, calls=%fused_computation.17 | loop fusion | bytes 1835008
  87.5 0.0 collective-permute-done.3
  87.5 0.7 copy_dynamic-update-slice_fusion.2
  88.2 1.2 constant_dynamic-update-slice_fusion
  89.4 0.0 collective-permute-done.4
  89.4 1.9 %copy_dynamic-update-slice_fusion.1 = bf16[3,1280,512]{2,0,1:T(4,128)(2,1)S(1)} fusion(bf16[3,1280,512]{2,0,1:T(4,128)(2,1)S(1)} %constant_dynamic-update-slice_fusion, bf16[3,256,512]{2,1,0:T(8,128)(2,1)} %collective-permute-done.4), kind=kLoop, calls=%fused_computation.15 | loop fusion | bytes 1835008
  91.3 6.8 %collective-permute-done.5 = bf16[3,256,512]{2,1,0:T(8,128)(2,1)} collective-permute-done((bf16[3,256,512]{2,1,0:T(8,128)(2,1)S(1)}, bf16[3,256,512]{2,1,0:T(8,128)(2,1)}, u32[]{:S(2)}, u32[]{:S(2)}) %collective-permute-start.5) | collective-permute-done | bytes 786464 | tf_op jit(solution)/shard_map/ppermute | solution.py:28
  98.1 1.9 %copy_dynamic-update-slice_fusion = bf16[3,1280,512]{2,0,1:T(4,128)(2,1)S(1)} fusion(bf16[3,1280,512]{2,0,1:T(4,128)(2,1)S(1)} %copy_dynamic-update-slice_fusion.1, bf16[3,256,512]{2,1,0:T(8,128)(2,1)} %collective-permute-done.5), kind=kLoop, calls=%fused_computation.14 | loop fusion | bytes 1835008 | tf_op jit(solution)/shard_map/concatenate | solution.py:89
  100.0 0.0 copy-start.6
  100.0 0.7 constant_dynamic-slice_fusion
  100.8 0.2 copy.56
  101.0 0.2 copy.55
  101.1 0.6 copy-done.6
  101.7 0.8 fusion.1
  102.5 0.0 copy-start.4
  102.5 2.0 %fusion.3 = f32[512,768]{1,0:T(8,128)} fusion(bf16[768,512]{1,0:T(8,128)(2,1)S(1)} %bitcast.61, bf16[1,2,768,768]{3,2,1,0:T(8,128)(2,1)S(1)} %copy-done.6), kind=kOutput, calls=%fused_computation.8 | convolution fusion | flops 603979776 | bytes 3538944 | tf_op jit(solution)/shard_map/dot_general | solution.py:117
  104.5 7.9 %all-to-all-done.2 = f32[64,1,768]{2,1,0:T(1,128)} async-done(((f32[64,1,768]{2,1,0:T(1,128)}), f32[64,1,768]{2,1,0:T(1,128)}, u32[]{:S(2)}, u32[]{:S(2)}) %all-to-all-start.2) | async-done | bytes 196640 | tf_op jit(solution)/shard_map/all_to_all | solution.py:55
  112.5 0.9 copy.73
  113.5 4.0 %all_to_all.34 = f32[2,64,768]{2,1,0:T(8,128)S(1)} all-to-all(f32[2,64,768]{2,1,0:T(8,128)S(1)} %broadcast_in_dim.27), channel_id=1, replica_groups=mesh['grp'=4,'clu_0'=4,'clu_1'=16,'clu_2'=2] {'clu_2'}, dimensions={0} | all-to-all | bytes 786432 | tf_op jit(solution)/shard_map/all_to_all | solution.py:55
  117.5 0.3 copy.60
  117.8 0.3 reshape_reshape_reshape_reshape.3
  118.1 0.0 copy-start.1
  118.1 0.0 copy-done.4
  118.2 0.7 convolution_multiply_fusion.1
  118.9 1.3 fusion
  120.2 1.8 %add_bitcast_fusion = f32[768,512]{0,1:T(8,128)} fusion(f32[512,768]{1,0:T(8,128)S(1)} %copy-done.1, f32[512,768]{1,0:T(8,128)S(1)} %fusion.1, bf16[512,512]{1,0:T(8,128)(2,1)S(1)} %bitcast.56, bf16[512,768]{1,0:T(8,128)(2,1)S(1)} %bitcast.53), kind=kOutput, calls=%fused_computation.2 | convolution fusion | flops 403439616 | bytes 6029312 | tf_op jit(solution)/shard_map/dot_general | solution.py:149
  122.0 1.9 %copy.62 = f32[768,512]{1,0:T(8,128)S(1)} copy(f32[768,512]{0,1:T(8,128)} %add_bitcast_fusion) | data formatting | bytes 3145728 | tf_op jit(solution)/shard_map/add | solution.py:155
  123.9 1.7 %reshape_reshape.4 = f32[3,256,4,128]{3,2,1,0:T(4,128)} reshape(f32[768,512]{1,0:T(8,128)S(1)} %copy.62) | data formatting | bytes 3145728 | tf_op jit(solution)/shard_map/reshape;reshape | solution.py:33
  125.5 1.6 %copy.63 = f32[4,3,256,128]{3,2,1,0:T(8,128)S(1)} copy(f32[4,3,256,128]{3,0,2,1:T(4,128)} %bitcast.54) | data formatting | bytes 3145728 | tf_op jit(solution)/shard_map/transpose | solution.py:33
  127.1 25.3 %all_to_all.35 = f32[4,3,256,128]{3,2,1,0:T(8,128)S(1)} all-to-all(f32[4,3,256,128]{3,2,1,0:T(8,128)S(1)} %copy.63), channel_id=1, replica_groups=mesh['grp'=4,'clu_0'=4,'clu_1'=16,'clu_2'=2] {'grp'}, dimensions={0} | all-to-all | bytes 3145728 | tf_op jit(solution)/shard_map/all_to_all | solution.py:38
  152.4 0.9 reduce_sum.29
  (16 shorter events, 0.1 us)
Async XLA Ops:
  0.0 120.2 %copy-start = (bf16[1,16,32,768]{3,2,1,0:T(8,128)(2,1)S(1)}, bf16[1,16,32,768]{3,2,1,0:T(8,128)(2,1)}, u32[]{:S(2)}) copy-start(bf16[1,16,32,768]{3,2,1,0:T(8,128)(2,1)} %param.15) | copy-start | bytes 2359300
  0.0 13.6 %collective-permute-start = (bf16[3,256,512]{2,1,0:T(8,128)(2,1)}, bf16[3,256,512]{2,1,0:T(8,128)(2,1)S(1)}, u32[]{:S(2)}, u32[]{:S(2)}) collective-permute-start(bf16[3,256,512]{2,1,0:T(8,128)(2,1)} %param.10), channel_id=1, source_target_pairs={{0,1},{1,2},{2,3},{3,4},{4,5},{5,6},{6,7},{7,8},{8,9},{9,10},{10,1... | collective-permute-start | bytes 2359304 | tf_op jit(solution)/shard_map/ppermute | solution.py:17
  2.1 13.5 %collective-permute-start.1 = (bf16[3,256,512]{2,1,0:T(8,128)(2,1)}, bf16[3,256,512]{2,1,0:T(8,128)(2,1)S(1)}, u32[]{:S(2)}, u32[]{:S(2)}) collective-permute-start(bf16[3,256,512]{2,1,0:T(8,128)(2,1)} %param.10), channel_id=1, source_target_pairs={{1,0},{2,1},{3,2},{4,3},{5,4},{6,5},{7,6},{8,7},{9,8},{10,9},{11,1... | collective-permute-start | bytes 2359304 | tf_op jit(solution)/shard_map/ppermute | solution.py:19
  29.5 29.6 %copy-start.7 = (s32[1,2]{1,0:T(1,128)S(1)}, s32[1,2]{1,0:T(1,128)}, u32[]{:S(2)}) copy-start(s32[1,2]{1,0:T(1,128)} %param.14) | copy-start | bytes 28
  29.5 31.6 %copy-start.5 = (s32[1,16]{1,0:T(1,128)S(1)}, s32[1,16]{1,0:T(1,128)}, u32[]{:S(2)}) copy-start(s32[1,16]{1,0:T(1,128)} %param.18) | copy-start | bytes 196
  29.5 56.1 %collective-permute-start.2 = (bf16[3,256,512]{2,1,0:T(8,128)(2,1)S(1)}, bf16[3,256,512]{2,1,0:T(8,128)(2,1)}, u32[]{:S(2)}, u32[]{:S(2)}) collective-permute-start(bf16[3,256,512]{2,1,0:T(8,128)(2,1)S(1)} %copy.47), channel_id=1, source_target_pairs={{0,2},{1,3},{2,4},{3,5},{4,6},{5,7},{6,8},{7,9},{8,10},{9,11},{10,... | collective-permute-start | bytes 2359304 | tf_op jit(solution)/shard_map/ppermute | solution.py:28
  40.3 34.8 %all-to-all-start.1 = ((f32[64,1,768]{2,1,0:T(1,128)}), f32[64,1,768]{2,1,0:T(1,128)}, u32[]{:S(2)}, u32[]{:S(2)}) async-start(f32[64,1,768]{2,1,0:T(1,128)} %all_to_all.22), calls=%async_computation.1 | async-start | bytes 393216 | tf_op jit(solution)/shard_map/all_to_all | solution.py:45
  57.2 30.3 %collective-permute-start.3 = (bf16[3,256,512]{2,1,0:T(8,128)(2,1)S(1)}, bf16[3,256,512]{2,1,0:T(8,128)(2,1)S(1)}, u32[]{:S(2)}, u32[]{:S(2)}) collective-permute-start(bf16[3,256,512]{2,1,0:T(8,128)(2,1)S(1)} %copy.47), channel_id=1, source_target_pairs={{0,1},{1,2},{2,3},{3,4},{4,5},{5,6},{6,7},{7,8},{8,9},{9,10},{10,1... | collective-permute-start | bytes 2359304 | tf_op jit(solution)/shard_map/ppermute | solution.py:28
  61.1 28.3 %collective-permute-start.4 = (bf16[3,256,512]{2,1,0:T(8,128)(2,1)S(1)}, bf16[3,256,512]{2,1,0:T(8,128)(2,1)}, u32[]{:S(2)}, u32[]{:S(2)}) collective-permute-start(bf16[3,256,512]{2,1,0:T(8,128)(2,1)S(1)} %copy.47), channel_id=1, source_target_pairs={{0,127},{1,0},{2,1},{3,2},{4,3},{5,4},{6,5},{7,6},{8,7},{9,8},{10,... | collective-permute-start | bytes 2359304 | tf_op jit(solution)/shard_map/ppermute | solution.py:28
  64.8 33.4 %collective-permute-start.5 = (bf16[3,256,512]{2,1,0:T(8,128)(2,1)S(1)}, bf16[3,256,512]{2,1,0:T(8,128)(2,1)}, u32[]{:S(2)}, u32[]{:S(2)}) collective-permute-start(bf16[3,256,512]{2,1,0:T(8,128)(2,1)S(1)} %copy.47), channel_id=1, source_target_pairs={{0,126},{1,127},{2,0},{3,1},{4,2},{5,3},{6,4},{7,5},{8,6},{9,7},{1... | collective-permute-start | bytes 2359304 | tf_op jit(solution)/shard_map/ppermute | solution.py:28
  76.9 35.6 %all-to-all-start.2 = ((f32[64,1,768]{2,1,0:T(1,128)}), f32[64,1,768]{2,1,0:T(1,128)}, u32[]{:S(2)}, u32[]{:S(2)}) async-start(f32[64,1,768]{2,1,0:T(1,128)} %broadcast_in_dim.26), calls=%async_computation.2 | async-start | bytes 393216 | tf_op jit(solution)/shard_map/all_to_all | solution.py:55
  100.0 1.7 %copy-start.6 = (bf16[1,2,768,768]{3,2,1,0:T(8,128)(2,1)S(1)}, bf16[1,2,768,768]{3,2,1,0:T(8,128)(2,1)}, u32[]{:S(2)}) copy-start(bf16[1,2,768,768]{3,2,1,0:T(8,128)(2,1)} %param.13) | copy-start | bytes 7077892
  102.5 15.6 %copy-start.4 = (s32[1,16]{1,0:T(1,128)S(1)}, s32[1,16]{1,0:T(1,128)}, u32[]{:S(2)}) copy-start(s32[1,16]{1,0:T(1,128)} %param.19) | copy-start | bytes 196
  104.5 14.3 %copy-start.2 = (bf16[1,16,32,32]{3,2,1,0:T(8,128)(2,1)S(1)}, bf16[1,16,32,32]{3,2,1,0:T(8,128)(2,1)}, u32[]{:S(2)}) copy-start(bf16[1,16,32,32]{3,2,1,0:T(8,128)(2,1)} %param.16) | copy-start | bytes 98308
  104.5 14.3 %copy-start.3 = (f32[1,16]{1,0:T(1,128)S(1)}, f32[1,16]{1,0:T(1,128)}, u32[]{:S(2)}) copy-start(f32[1,16]{1,0:T(1,128)} %param.17) | copy-start | bytes 196
  118.1 2.0 %copy-start.1 = (f32[512,768]{1,0:T(8,128)S(1)}, f32[512,768]{1,0:T(8,128)}, u32[]{:S(2)}) copy-start(f32[512,768]{1,0:T(8,128)} %fusion.3) | copy-start | bytes 4718596
where the time goes:
time: 154 us; the launch traced here: 153 us
  starting transfers between devices  46.5 us (30%)
  blocking collectives  34.7 us (23%)
  local copies, waits for them, and re-layouts  25 us (16%)
  waiting for transfers between devices  24.8 us (16%)
  other arithmetic  13.7 us (9%)
  matrix products  6.85 us (4%)
  between operations  1.71 us (1%)
    all_to_all x2, blocking collectives, sent_and_summed(): lax.all_to_all(tiles, axis, split_axis=0, concat_axis=0, tiled=True)  30.6 us
    all_to_all x1, starting transfers between devices, sum_in_two_steps(): return jnp.sum(lax.all_to_all(own, far, 0, 0, tiled=True), axis=0)  16.9 us
    ppermute x4, starting transfers between devices, from_behind(): lax.ppermute(shard, axis, [(i, (i + by) % size) for i in range(size)])  15.1 us
    unnamed x23, local copies, waits for them, and re-layouts  8.78 us
    all_to_all x1, starting transfers between devices, copy_for_each(): return lax.all_to_all(copies, axis, split_axis=0, concat_axis=0, tiled=True)  8.75 us
    concatenate x1, other arithmetic, with_halo(): jnp.concatenate([lax.ppermute(tail, axis, [(i, (i + 1) % count) for i in...  8.65 us
    all_to_all x1, waiting for transfers between devices, copy_for_each(): return lax.all_to_all(copies, axis, split_axis=0, concat_axis=0, tiled=True)  7.94 us
    ppermute x4, waiting for transfers between devices, from_behind(): lax.ppermute(shard, axis, [(i, (i + by) % size) for i in range(size)])  6.84 us
  transfers between devices with their start and end apart: 8, of which 5 were waited for; matrix products, arithmetic and copies ran while one was open for 12% of the time, Pallas kernels for 0%

commit v1 on v0

v1 whole, which is shorter than its diff:
```python
import functools

import jax
import jax.numpy as jnp
from jax import lax
from jax.experimental import pallas as pl
from jax.experimental.pallas import tpu as pltpu
from jax.sharding import Mesh
from jax.sharding import PartitionSpec as P

CLU = ("clu_0", "clu_1", "clu_2")
PAD = 16
F32 = jnp.float32
BF16 = jnp.bfloat16
VMEM = pl.BlockSpec(memory_space=pltpu.VMEM)
SMEM = pl.BlockSpec(memory_space=pltpu.SMEM)
ANY = pl.BlockSpec(memory_space=pl.ANY)


def params(mib):
    return pltpu.CompilerParams(vmem_limit_bytes=mib * 2**20)


def iota(shape, dim):
    return lax.broadcasted_iota(jnp.int32, shape, dim)


def dot(a, b):
    return jnp.dot(a, b, preferred_element_type=F32)


def as_column(row):
    size = row.shape[1]
    square = (size, size)
    spread = jnp.where(iota(square, 0) == iota(square, 1), jnp.broadcast_to(row, square), 0.0)
    return jnp.sum(spread, axis=1, keepdims=True)


def count_before(mask):
    size = mask.shape[1]
    square = (size, size)
    upto = (iota(square, 0) <= iota(square, 1)).astype(F32).astype(BF16)
    rows = jnp.broadcast_to(mask, (16, size)).astype(BF16)
    return dot(rows, upto)[:1] - 1.0


def chosen(column, width):
    shape = (column.shape[0], width)
    return (jnp.broadcast_to(column, shape) == iota(shape, 1).astype(F32)).astype(F32).astype(BF16)


def dress_kernel(sc, rel_ref, forces_ref, block_ref, halo_ref):
    rows, columns = forces_ref.shape
    size = rel_ref.shape[1]
    part = halo_ref.shape[1]
    start = pl.multiple_of(sc[1] * part, part)
    halo_ref[:rows] = forces_ref[:, pl.ds(start, part)]
    block_ref[:rows] = forces_ref[...]
    rel = rel_ref[...]
    high = (rel >= size).astype(jnp.int32) + (rel >= 2 * size).astype(jnp.int32)
    low = (rel - high * size).astype(F32)
    high = high.astype(F32)
    line = iota((PAD, columns), 0)
    spare = jnp.zeros((1, columns - size), F32)
    wide = [jnp.concatenate([v, spare], axis=1) for v in (low, high)]
    block_ref[rows:] = jnp.where(
        line == 0, wide[0], jnp.where(line == 1, wide[1], 0.0)
    ).astype(BF16)
    line = iota((PAD, part), 0)
    tail = jnp.zeros((PAD, part), F32)
    at = 0
    for v in (low, high):
        for i in range(size // part):
            tail = jnp.where(line == at, v[:, i * part : (i + 1) * part], tail)
            at += 1
    halo_ref[rows:] = tail.astype(BF16)


def pieces_kernel(sc, halo_ref, own_ref, pair_ref, bases_ref, keep_ref, send_ref, thin_ref):
    levels, comps, rank, size = bases_ref.shape
    rows = comps * size
    part = halo_ref.shape[1]
    quarter = size // 4
    core = sc[0]
    start = pl.multiple_of(sc[1] * part, part)
    tail = own_ref[rows:].astype(F32)
    low, high = tail[0:1, :size], tail[1:2, :size]
    seat = jnp.where(core == 0, high, 2.0 - high)
    pick = chosen(as_column(seat * size + low), 3 * size)
    sums = [jnp.zeros((rank, part), F32) for _ in range(levels)]
    for comp in range(comps):
        span = slice(comp * size, (comp + 1) * size)
        got = dot(pick[:, :size], halo_ref[span])
        got += dot(pick[:, size : 2 * size], own_ref[span, pl.ds(start, part)])
        got += dot(pick[:, 2 * size :], pair_ref[span, pl.ds(start, part)])
        got = got.astype(BF16)
        for level in range(levels):
            sums[level] += dot(bases_ref[level, comp], got)
    keep_ref[...] = jnp.where(core == 0, sums[0], sums[1])
    send_ref[...] = jnp.where(core == 0, sums[1], sums[0])
    tail = halo_ref[rows:].astype(F32)
    per = size // part
    low = jnp.concatenate([tail[i : i + 1] for i in range(per)], axis=1)
    high = jnp.concatenate([tail[per + i : per + i + 1] for i in range(per)], axis=1)
    mine = high == jnp.where(core == 0, 2.0, 0.0)
    place = count_before(mine.astype(F32))
    shape = (quarter, size)
    seats = jnp.broadcast_to(jnp.where(mine, place, -1.0), shape)
    into = (seats == iota(shape, 0).astype(F32)).astype(F32).astype(BF16)
    pack = dot(into, chosen(as_column(low), size)).astype(BF16)
    for comp in range(comps):
        thin_ref[comp] = dot(pack, own_ref[comp * size : (comp + 1) * size]).astype(BF16)


def far_kernel(slot, keeps, scale, basis_ref, coupling_ref, weights_ref, high_ref, low_ref):
    blocks, rank, _ = coupling_ref.shape
    width = high_ref.shape[1]
    lane = iota((rank, width), 1)
    for b in range(blocks):
        first = slot[b] * rank
        tile = coupling_ref[b].astype(F32) * scale[b]
        tile = jnp.concatenate([tile] * (width // rank), axis=1)
        tile = jnp.where((lane >= first) & (lane < first + keeps[b]), tile, 0.0)
        high = tile.astype(BF16)
        high_ref[b * rank : (b + 1) * rank] = high
        low_ref[b * rank : (b + 1) * rank] = (tile - high.astype(F32)).astype(BF16)
    dims = (((0,), (0,)), ((), ()))
    total = lax.dot_general(basis_ref[...], high_ref[...], dims, preferred_element_type=F32)
    total += lax.dot_general(basis_ref[...], low_ref[...], dims, preferred_element_type=F32)
    for i in range(weights_ref.shape[0]):
        weights_ref[i] = total


def near_kernel(
    sc, tiles_ref, thin, near_z, pair_far, own, pair, far_z, pair_near,
    split_ref, mine_ref, window, blocks, sems,
):
    count, rows, _ = tiles_ref.shape
    columns = own.shape[1]
    size = rows // 3
    quarter = thin.shape[1]
    groups, _, part = split_ref.shape
    core, group = sc[0], sc[1]
    seats = (thin, near_z, pair_far, own, pair, far_z, pair_near)
    for j in range(count):
        off = jnp.where(core == 0, sc[2 + j], -sc[2 + j])
        for o in range(-2, 3):

            @pl.when(off == o)
            def _(j=j, o=o):
                for w in range(3):
                    source = seats[o + 2 + w]
                    if o + w == -2:
                        for comp in range(3):
                            pltpu.make_async_copy(
                                source.at[comp],
                                window.at[j, w, pl.ds(comp * size, quarter)],
                                sems.at[j, w, comp],
                            ).start()
                            window[j, w, comp * size + quarter : (comp + 1) * size] = jnp.zeros(
                                (size - quarter, columns), BF16
                            )
                    else:
                        pltpu.make_async_copy(source, window.at[j, w], sems.at[j, w, 0]).start()

    for j in range(count):
        off = jnp.where(core == 0, sc[2 + j], -sc[2 + j])
        edge = off == -2
        for w in range(1, 3):
            pltpu.make_async_copy(own, window.at[j, w], sems.at[j, w, 0]).wait()

        @pl.when(edge)
        def _(j=j):
            for comp in range(3):
                pltpu.make_async_copy(
                    thin.at[comp], window.at[j, 0, pl.ds(comp * size, quarter)], sems.at[j, 0, comp]
                ).wait()

        @pl.when(jnp.logical_not(edge))
        def _(j=j):
            pltpu.make_async_copy(own, window.at[j, 0], sems.at[j, 0, 0]).wait()

        tail = window[j, 1, rows:].astype(F32)
        low, high = tail[0:1, :size], tail[1:2, :size]
        seat = jnp.where(core == 0, high, 2.0 - high)
        first = seat == 0.0
        place = count_before(first.astype(F32))
        low = jnp.where(jnp.logical_and(first, edge), place, low)
        pick = chosen(as_column(seat * size + low), 3 * size)
        for comp in range(3):
            span = slice(comp * size, (comp + 1) * size)
            got = dot(pick[:, :size], window[j, 0, span])
            for w in range(1, 3):
                got += dot(pick[:, w * size : (w + 1) * size], window[j, w, span])
            blocks[j, span] = got.astype(BF16)
    for r in range(3):
        span = slice(r * size, (r + 1) * size)
        total = dot(tiles_ref[0, span], blocks[0])
        for j in range(1, count):
            total += dot(tiles_ref[j, span], blocks[j])
        for i in range(groups):
            piece = total[:, i * part : (i + 1) * part]
            split_ref[i, span] = piece.astype(BF16)

            @pl.when(group == i)
            def _(piece=piece, span=span):
                mine_ref[span] = piece


def last_kernel(sc, arrived_ref, mine_ref, weights_ref, sums_ref, out_ref, table_ref):
    groups = arrived_ref.shape[0]
    count, rank, _ = sums_ref.shape
    planes = count // 2
    group, plane = sc[1], sc[2]
    half = planes // 2
    other = jnp.where(plane < half, half, 0)
    coarse = sums_ref[2 * other]
    for i in range(1, half):
        coarse += sums_ref[2 * (other + i)]
    table_ref[:rank] = coarse
    for i in range(1, planes):
        at = lax.rem(plane + i, planes)
        table_ref[i * rank : (i + 1) * rank] = sums_ref[2 * at + 1]
    weights = weights_ref[0]
    for i in range(1, groups):
        weights += weights_ref[i]
    total = mine_ref[...] + jnp.dot(
        weights, table_ref[...], precision=lax.Precision.HIGHEST, preferred_element_type=F32
    )
    for i in range(groups):
        total += jnp.where(group == i, 0.0, arrived_ref[i].astype(F32))
    out_ref[...] = total


def shape_of(dims, dtype):
    return jax.ShapeDtypeStruct(dims, dtype)


def on_device(
    forces, order, bases, near_tiles, near_col, far_basis, far_coupling, far_scale, far_rank, far_target
):
    clusters = lax.axis_size(CLU)
    planes = lax.axis_size("clu_0")
    steps = lax.axis_size("clu_1")
    groups = lax.axis_size("grp")
    own_index = lax.axis_index(CLU)
    plane = lax.axis_index("clu_0")
    core = lax.axis_index("clu_2")
    group = lax.axis_index("grp")
    size = order.shape[0]
    comps, _, columns = forces.shape
    rows = comps * size
    part = columns // groups
    levels, rank = bases.shape[:2]
    count = near_tiles.shape[1]
    far_count = far_target.shape[1]
    width = planes * rank

    def swapped(v):
        return lax.ppermute(v, "clu_2", [(0, 1), (1, 0)])

    def swapped_by(v, by):
        pairs = [(i, (i + by if i % 2 else i - by) % clusters) for i in range(clusters)]
        return lax.ppermute(v, CLU, pairs)

    def from_near(v):
        pairs = [(i, (i - 2 if i % 2 else i + 2) % clusters) for i in range(clusters)]
        return lax.ppermute(v, CLU, pairs)

    def from_far(v):
        pairs = [(i, (i + 2 if i % 2 else i - 2) % clusters) for i in range(clusters)]
        return lax.ppermute(v, CLU, pairs)

    def spread(v, axis, copies):
        many = jnp.broadcast_to(v, (copies, *v.shape))
        return lax.all_to_all(many, axis, split_axis=0, concat_axis=0, tiled=True)

    offsets = jnp.mod(near_col[0] - own_index + 2, clusters) - 2
    sc = jnp.concatenate([jnp.stack([core, group]), offsets]).astype(jnp.int32)
    rel = jnp.mod(order - (own_index - 1) * size, clusters * size).reshape(1, size)
    block, halo = pl.pallas_call(
        dress_kernel,
        out_shape=(shape_of((rows + PAD, columns), BF16), shape_of((rows + PAD, part), BF16)),
        in_specs=[SMEM, VMEM, VMEM],
        out_specs=(VMEM, VMEM),
        compiler_params=params(16),
        name="dress",
    )(sc, rel, forces.reshape(rows, columns))
    halo = swapped_by(halo, 1)
    pair = swapped(block)
    near_z = from_near(block)
    far_z = from_far(block)

    keep, send, thin = pl.pallas_call(
        pieces_kernel,
        out_shape=(
            shape_of((rank, part), F32),
            shape_of((rank, part), F32),
            shape_of((comps, size // 4, columns), BF16),
        ),
        in_specs=[SMEM, VMEM, VMEM, VMEM, VMEM],
        out_specs=(VMEM, VMEM, VMEM),
        compiler_params=params(16),
        name="pieces",
    )(sc, halo, block, pair, bases.transpose(0, 2, 1, 3))
    level_sum = keep + swapped(send)
    level_sum = jnp.sum(spread(level_sum, "clu_1", steps), axis=0)
    sums = spread(level_sum, ("clu_0", "clu_2"), planes * 2)
    thin = swapped_by(thin, 3)

    target = far_target[0]
    slot = jnp.where(target < 2, 0, jnp.mod(target - 2 - plane, planes)).astype(jnp.int32)
    weights = pl.pallas_call(
        far_kernel,
        out_shape=shape_of((groups, rows, width), F32),
        in_specs=[SMEM, SMEM, SMEM, VMEM, VMEM],
        out_specs=VMEM,
        scratch_shapes=[pltpu.VMEM((far_count * rank, width), BF16)] * 2,
        compiler_params=params(16),
        name="far_weights",
    )(slot, far_rank[0], far_scale[0], far_basis.reshape(far_count * rank, rows), far_coupling[0])
    weights = lax.all_to_all(weights, "grp", split_axis=0, concat_axis=0, tiled=True)

    pair_near = swapped(near_z)
    pair_far = swapped(far_z)
    split, mine = pl.pallas_call(
        near_kernel,
        out_shape=(shape_of((groups, rows, part), BF16), shape_of((rows, part), F32)),
        in_specs=[SMEM, VMEM] + [ANY] * 7,
        out_specs=(VMEM, VMEM),
        scratch_shapes=[
            pltpu.VMEM((count, 3, rows + PAD, columns), BF16),
            pltpu.VMEM((count, rows, columns), BF16),
            pltpu.SemaphoreType.DMA((count, 3, 3)),
        ],
        compiler_params=params(32),
        name="near",
    )(sc, near_tiles[0], thin, near_z, pair_far, block, pair, far_z, pair_near)
    arrived = lax.all_to_all(split, "grp", split_axis=0, concat_axis=0, tiled=True)
    velocity = pl.pallas_call(
        last_kernel,
        out_shape=shape_of((rows, part), F32),
        in_specs=[SMEM, VMEM, VMEM, VMEM, VMEM],
        out_specs=VMEM,
        scratch_shapes=[pltpu.VMEM((width, part), F32)],
        compiler_params=params(16),
        name="last",
    )(jnp.stack([core, group, plane]).astype(jnp.int32), arrived, mine, weights, sums)
    return velocity.reshape(comps, size, part)


def solution(mesh):
    clusters = mesh.shape["clu"]
    torus = Mesh(
        mesh.devices.reshape(mesh.shape["grp"], 4, clusters // 8, 2),
        ("grp", "clu_0", "clu_1", "clu_2"),
    )
    in_specs = (
        P(None, CLU, None),
        P(CLU),
        P(None, None, None, CLU),
        P(CLU, "grp", None, None),
        P(CLU, "grp"),
        P(CLU, "grp", None, None),
        P(CLU, "grp", None, None),
        P(CLU, "grp"),
        P(CLU, "grp"),
        P(CLU, "grp"),
    )
    return jax.shard_map(
        on_device, mesh=torus, in_specs=in_specs, out_specs=P(None, CLU, "grp"), check_vma=False
    )
```

time: 154 us -> 113 us (0.73)
  the two profiles are of different devices: /device:TPU:32 before, /device:TPU:34 now
where the time goes in v1:
time: 113 us
  starting transfers between devices  49.7 us (44%)
  waiting for transfers between devices  39.5 us (35%)
  Pallas kernels  12.5 us (11%)
  local copies, waits for them, and re-layouts  8.1 us (7%)
  other arithmetic  2.5 us (2%)
    all_to_all x2, starting transfers between devices, spread(): return lax.all_to_all(many, axis, split_axis=0, concat_axis=0, tiled=True)  21.1 us
    all_to_all x1, waiting for transfers between devices, on_device(): lax.all_to_all(split, 'grp', split_axis=0, concat_axis=0, tiled=True)  12.6 us
    all_to_all x2, waiting for transfers between devices, spread(): return lax.all_to_all(many, axis, split_axis=0, concat_axis=0, tiled=True)  10.4 us
    ppermute x4, starting transfers between devices, swapped(): return lax.ppermute(v, 'clu_2', [(0, 1), (1, 0)])  8.76 us
    unnamed x26, local copies, waits for them, and re-layouts  6.71 us
    ppermute x1, waiting for transfers between devices, from_far(): return lax.ppermute(v, CLU, pairs)  6.71 us
    ppermute x2, starting transfers between devices, swapped_by(): return lax.ppermute(v, CLU, pairs)  5.95 us
    pallas_call x1, Pallas kernels, on_device(): pl.pallas_call(near_kernel, out_shape=(shape_of((groups, rows, part), BF1...  5.77 us
  transfers between devices with their start and end apart: 12, of which 6 were waited for; matrix products, arithmetic and copies ran while one was open for 2% of the time, Pallas kernels for 7%

profile of v1, /device:TPU:34, one launch (start us, length us, event | category | flops | bytes accessed | tf_op | source)
XLA Modules:
  0.0 112.5 jit_solution(15681517802043466097)
XLA Ops:
  0.0 0.7 fusion.1
  0.7 0.7 and_select_fusion.1
  1.4 0.1 pad_add_fusion.1.sc
  1.4 0.0 copy-start.3
  1.4 1.1 %copy-done.3 = bf16[3,256,512]{2,1,0:T(8,128)(2,1)S(1)} copy-done((bf16[3,256,512]{2,1,0:T(8,128)(2,1)S(1)}, bf16[3,256,512]{2,1,0:T(8,128)(2,1)}, u32[]{:S(2)}) %copy-start.3) | copy-done | bytes 786456
  2.6 0.0 copy-start.12
  2.6 0.0 copy-start.8
  2.6 0.0 copy-start.9
  2.6 0.6 dress.1
  3.2 0.0 copy-start.1
  3.2 0.0 copy-start.6
  3.2 2.1 %collective-permute-start.1 = (bf16[784,512]{1,0:T(8,128)(2,1)S(1)}, bf16[784,512]{1,0:T(8,128)(2,1)S(1)}, u32[]{:S(2)}, u32[]{:S(2)}) collective-permute-start(bf16[784,512]{1,0:T(8,128)(2,1)S(1)} %get-tuple-element.13.own_ref.own), channel_id=1, source_target_pairs={{0,1},{1,0},{2,3},{3,2},{4,5},{5,4},{6,7},{7,6},{8,9},{9,8},{10,11... | collective-permute-start | bytes 2408456 | tf_op jit(solution)/shard_map/ppermute | solution.py:260
  5.3 2.1 %collective-permute-start = (bf16[784,128]{1,0:T(8,128)(2,1)S(1)}, bf16[784,128]{1,0:T(8,128)(2,1)S(1)}, u32[]{:S(2)}, u32[]{:S(2)}) collective-permute-start(bf16[784,128]{1,0:T(8,128)(2,1)S(1)} %get-tuple-element.12), channel_id=1, source_target_pairs={{0,127},{1,2},{2,1},{3,4},{4,3},{5,6},{6,5},{7,8},{8,7},{9,10},{10... | collective-permute-start | bytes 602120 | tf_op jit(solution)/shard_map/ppermute | solution.py:264
  7.4 4.9 %collective-permute-done.halo_ref = bf16[784,128]{1,0:T(8,128)(2,1)S(1)} collective-permute-done((bf16[784,128]{1,0:T(8,128)(2,1)S(1)}, bf16[784,128]{1,0:T(8,128)(2,1)S(1)}, u32[]{:S(2)}, u32[]{:S(2)}) %collective-permute-start) | collective-permute-done | bytes 200736 | tf_op jit(solution)/shard_map/ppermute | solution.py:264
  12.3 0.0 collective-permute-done.1.pair_ref.pair
  12.3 0.0 copy-start.7
  12.3 0.9 copy-done.7
  13.2 1.8 %pieces.1 = (f32[32,128]{1,0:T(8,128)S(1)}, f32[32,128]{1,0:T(8,128)S(1)}, bf16[3,64,512]{2,1,0:T(8,128)(2,1)S(1)}) custom-call(s32[4]{0:T(128)S(1)} %pad_add_fusion.1.sc, bf16[784,128]{1,0:T(8,128)(2,1)S(1)} %collective-permute-done.halo_ref, bf16[784,512]{1,0:T(8,128)(2,1)S(1)} %get-tuple-element.13.own_ref.own, ...), custom_call_target="tpu_custom_call" | custom-call | tf_op jit(solution)/shard_map/pieces/pallas_call | solution.py:294
  15.0 0.0 copy-start.10
  15.0 0.7 copy-done.10
  15.7 2.4 %collective-permute-start.7 = (f32[32,128]{1,0:T(8,128)S(1)}, f32[32,128]{1,0:T(8,128)S(1)}, u32[]{:S(2)}, u32[]{:S(2)}) collective-permute-start(f32[32,128]{1,0:T(8,128)S(1)} %get-tuple-element.18), channel_id=1, source_target_pairs={{0,1},{1,0},{2,3},{3,2},{4,5},{5,4},{6,7},{7,6},{8,9},{9,8},{10,11... | collective-permute-start | bytes 49160 | tf_op jit(solution)/shard_map/ppermute | solution.py:260
  18.1 0.8 collective-permute-done.7
  18.9 0.7 broadcast_in_dim.11
  19.6 16.3 %all-to-all-start.2 = ((f32[16,32,128]{2,1,0:T(8,128)}), f32[16,32,128]{2,1,0:T(8,128)S(1)}, u32[]{:S(2)}, u32[]{:S(2)}) async-start(f32[16,32,128]{2,1,0:T(8,128)} %broadcast_in_dim.11), calls=%async_computation.2 | async-start | bytes 524288 | tf_op jit(solution)/shard_map/all_to_all | solution.py:276
  35.9 2.0 %collective-permute-start.4 = (bf16[784,512]{1,0:T(8,128)(2,1)S(1)}, bf16[784,512]{1,0:T(8,128)(2,1)}, u32[]{:S(2)}, u32[]{:S(2)}) collective-permute-start(bf16[784,512]{1,0:T(8,128)(2,1)S(1)} %get-tuple-element.13.own_ref.own), channel_id=1, source_target_pairs={{0,126},{1,3},{2,0},{3,5},{4,2},{5,7},{6,4},{7,9},{8,6},{9,11},{10... | collective-permute-start | bytes 2408456 | tf_op jit(solution)/shard_map/ppermute | solution.py:272
  37.9 3.8 %collective-permute-start.3 = (bf16[784,512]{1,0:T(8,128)(2,1)S(1)}, bf16[784,512]{1,0:T(8,128)(2,1)}, u32[]{:S(2)}, u32[]{:S(2)}) collective-permute-start(bf16[784,512]{1,0:T(8,128)(2,1)S(1)} %get-tuple-element.13.own_ref.own), channel_id=1, source_target_pairs={{0,2},{1,127},{2,4},{3,1},{4,6},{5,3},{6,8},{7,5},{8,10},{9,7},{10... | collective-permute-start | bytes 2408456 | tf_op jit(solution)/shard_map/ppermute | solution.py:268
  41.7 0.0 copy-done.12
  41.8 0.0 copy-done.8
  41.8 0.0 copy-done.9
  41.8 0.0 copy-done.1
  41.8 0.0 copy-done.6
  41.8 2.6 %far_weights.1 = f32[4,768,128]{2,1,0:T(8,128)} custom-call(s32[16]{0:T(128)S(1)} %bitcast_select_fusion.slot, s32[16]{0:T(128)S(1)} %bitcast.24, f32[16]{0:T(128)S(1)} %bitcast.25, bf16[512,768]{1,0:T(8,128)(2,1)S(1)} %bitcast.19, bf16[16,32,32]{2,1,0:T(8,128)(2,1)S(1)} %bitcast.21), custom_call_target="tpu_custom_call" | custom-call | tf_op jit(solution)/shard_map/far_weights/pallas_call | solution.py:313
  44.4 10.4 %all-to-all-done.2 = f32[16,32,128]{2,1,0:T(8,128)S(1)} async-done(((f32[16,32,128]{2,1,0:T(8,128)}), f32[16,32,128]{2,1,0:T(8,128)S(1)}, u32[]{:S(2)}, u32[]{:S(2)}) %all-to-all-start.2) | async-done | bytes 262176 | tf_op jit(solution)/shard_map/all_to_all | solution.py:276
  54.8 0.0 copy-start.11
  54.8 0.7 copy-done.11
  55.5 4.5 %all-to-all-start.1 = ((f32[4,768,128]{2,1,0:T(8,128)}), f32[4,768,128]{2,1,0:T(8,128)S(1)}, u32[]{:S(2)}, u32[]{:S(2)}) async-start(f32[4,768,128]{2,1,0:T(8,128)} %far_weights.1), calls=%async_computation.1 | async-start | bytes 3145728 | tf_op jit(solution)/shard_map/all_to_all | solution.py:322
  60.0 6.7 %collective-permute-done.4.far_z = bf16[784,512]{1,0:T(8,128)(2,1)} collective-permute-done((bf16[784,512]{1,0:T(8,128)(2,1)S(1)}, bf16[784,512]{1,0:T(8,128)(2,1)}, u32[]{:S(2)}, u32[]{:S(2)}) %collective-permute-start.4) | collective-permute-done | bytes 802848 | tf_op jit(solution)/shard_map/ppermute | solution.py:272
  66.7 1.9 %collective-permute-start.5 = (bf16[784,512]{1,0:T(8,128)(2,1)}, bf16[784,512]{1,0:T(8,128)(2,1)}, u32[]{:S(2)}, u32[]{:S(2)}) collective-permute-start(bf16[784,512]{1,0:T(8,128)(2,1)} %collective-permute-done.4.far_z), channel_id=1, source_target_pairs={{0,1},{1,0},{2,3},{3,2},{4,5},{5,4},{6,7},{7,6},{8,9},{9,8},{10,11... | collective-permute-start | bytes 2408456 | tf_op jit(solution)/shard_map/ppermute | solution.py:260
  68.6 0.0 collective-permute-done.3.near_z
  68.6 2.4 %collective-permute-start.6 = (bf16[784,512]{1,0:T(8,128)(2,1)}, bf16[784,512]{1,0:T(8,128)(2,1)}, u32[]{:S(2)}, u32[]{:S(2)}) collective-permute-start(bf16[784,512]{1,0:T(8,128)(2,1)} %collective-permute-done.3.near_z), channel_id=1, source_target_pairs={{0,1},{1,0},{2,3},{3,2},{4,5},{5,4},{6,7},{7,6},{8,9},{9,8},{10,11... | collective-permute-start | bytes 2408456 | tf_op jit(solution)/shard_map/ppermute | solution.py:260
  71.0 3.8 %collective-permute-start.2 = (bf16[3,64,512]{2,1,0:T(8,128)(2,1)}, bf16[3,64,512]{2,1,0:T(8,128)(2,1)S(1)}, u32[]{:S(2)}, u32[]{:S(2)}) collective-permute-start(bf16[3,64,512]{2,1,0:T(8,128)(2,1)} %copy-done.10), channel_id=1, source_target_pairs={{0,125},{1,4},{2,127},{3,6},{4,1},{5,8},{6,3},{7,10},{8,5},{9,12},... | collective-permute-start | bytes 589832 | tf_op jit(solution)/shard_map/ppermute | solution.py:264
  74.8 1.0 reduce_sum.9
  75.8 4.0 %all-to-all-done.1.weights_ref = f32[4,768,128]{2,1,0:T(8,128)S(1)} async-done(((f32[4,768,128]{2,1,0:T(8,128)}), f32[4,768,128]{2,1,0:T(8,128)S(1)}, u32[]{:S(2)}, u32[]{:S(2)}) %all-to-all-start.1) | async-done | bytes 1572896 | tf_op jit(solution)/shard_map/all_to_all | solution.py:322
  79.8 0.7 broadcast_in_dim.12
  80.5 4.8 %all-to-all-start.3 = ((f32[8,32,128]{2,1,0:T(8,128)}), f32[8,32,128]{2,1,0:T(8,128)S(1)}, u32[]{:S(2)}, u32[]{:S(2)}) async-start(f32[8,32,128]{2,1,0:T(8,128)} %broadcast_in_dim.12), calls=%async_computation.3 | async-start | bytes 262144 | tf_op jit(solution)/shard_map/all_to_all | solution.py:276
  85.3 0.0 collective-permute-done.2.thin
  85.3 0.0 collective-permute-done.5.pair_far
  85.3 0.0 collective-permute-done.6.pair_near
  85.3 0.0 copy-start
  85.4 1.7 %copy-done = bf16[1,2,768,768]{3,2,1,0:T(8,128)(2,1)S(1)} copy-done((bf16[1,2,768,768]{3,2,1,0:T(8,128)(2,1)S(1)}, bf16[1,2,768,768]{3,2,1,0:T(8,128)(2,1)}, u32[]{:S(2)}) %copy-start) | copy-done | bytes 2359320
  87.0 5.8 %near.1 = (bf16[4,768,128]{2,1,0:T(8,128)(2,1)S(1)}, f32[768,128]{1,0:T(8,128)S(1)}) custom-call(s32[4]{0:T(128)S(1)} %pad_add_fusion.1.sc, bf16[2,768,768]{2,1,0:T(8,128)(2,1)S(1)} %bitcast.18, bf16[3,64,512]{2,1,0:T(8,128)(2,1)S(1)} %collective-permute-done.2.thin, bf16[784,512]{1,0:T(8,128)(2,1)} %collective-permute-done.3.near_z, ...), custom_call_target="tpu_custom_call" | custom-call | tf_op jit(solution)/shard_map/near/pallas_call | solution.py:326
  92.8 0.0 copy-start.2
  92.8 0.9 copy-done.2
  93.7 0.0 copy-start.4
  93.7 0.7 copy-done.4
  94.4 0.0 all-to-all-done.3.sums_ref
  94.4 0.0 copy-start.5
  94.4 3.6 %all-to-all-start = ((bf16[4,768,128]{2,1,0:T(8,128)(2,1)}), bf16[4,768,128]{2,1,0:T(8,128)(2,1)S(1)}, u32[]{:S(2)}, u32[]{:S(2)}) async-start(bf16[4,768,128]{2,1,0:T(8,128)(2,1)} %copy-done.2), calls=%async_computation | async-start | bytes 1572864 | tf_op jit(solution)/shard_map/all_to_all | solution.py:339
  98.1 0.1 pad_add_fusion.sc
  98.1 12.6 %all-to-all-done.arrived_ref = bf16[4,768,128]{2,1,0:T(8,128)(2,1)S(1)} async-done(((bf16[4,768,128]{2,1,0:T(8,128)(2,1)}), bf16[4,768,128]{2,1,0:T(8,128)(2,1)S(1)}, u32[]{:S(2)}, u32[]{:S(2)}) %all-to-all-start) | async-done | bytes 786464 | tf_op jit(solution)/shard_map/all_to_all | solution.py:339
  110.7 0.0 copy-done.5
  110.7 1.8 %last.1 = f32[768,128]{1,0:T(8,128)} custom-call(s32[3]{0:T(128)S(1)} %pad_add_fusion.sc, bf16[4,768,128]{2,1,0:T(8,128)(2,1)S(1)} %all-to-all-done.arrived_ref, f32[768,128]{1,0:T(8,128)S(1)} %copy-done.5, f32[4,768,128]{2,1,0:T(8,128)S(1)} %all-to-all-done.1.weights_ref, f32[8,32,128]{2,1,0:T(8,128)S(1)} %all-to-all-done.3.sums_ref), custom_call_target="tpu_custom_call" | custom-call | tf_op jit(solution)/shard_map/last/pallas_call | solution.py:340
  (2 shorter events, 0.0 us)
Async XLA Ops:
  1.4 1.1 %copy-start.3 = (bf16[3,256,512]{2,1,0:T(8,128)(2,1)S(1)}, bf16[3,256,512]{2,1,0:T(8,128)(2,1)}, u32[]{:S(2)}) copy-start(bf16[3,256,512]{2,1,0:T(8,128)(2,1)} %param.10) | copy-start | bytes 2359300
  2.6 39.2 %copy-start.12 = (s32[1,16]{1,0:T(1,128)S(1)}, s32[1,16]{1,0:T(1,128)}, u32[]{:S(2)}) copy-start(s32[1,16]{1,0:T(1,128)} %param.19) | copy-start | bytes 196
  2.6 39.2 %copy-start.8 = (s32[1,16]{1,0:T(1,128)S(1)}, s32[1,16]{1,0:T(1,128)}, u32[]{:S(2)}) copy-start(s32[1,16]{1,0:T(1,128)} %param.18) | copy-start | bytes 196
  2.6 39.2 %copy-start.9 = (f32[1,16]{1,0:T(1,128)S(1)}, f32[1,16]{1,0:T(1,128)}, u32[]{:S(2)}) copy-start(f32[1,16]{1,0:T(1,128)} %param.17) | copy-start | bytes 196
  3.2 38.6 %copy-start.1 = (bf16[1,16,32,768]{3,2,1,0:T(8,128)(2,1)S(1)}, bf16[1,16,32,768]{3,2,1,0:T(8,128)(2,1)}, u32[]{:S(2)}) copy-start(bf16[1,16,32,768]{3,2,1,0:T(8,128)(2,1)} %param.15) | copy-start | bytes 2359300
  3.2 38.6 %copy-start.6 = (bf16[1,16,32,32]{3,2,1,0:T(8,128)(2,1)S(1)}, bf16[1,16,32,32]{3,2,1,0:T(8,128)(2,1)}, u32[]{:S(2)}) copy-start(bf16[1,16,32,32]{3,2,1,0:T(8,128)(2,1)} %param.16) | copy-start | bytes 98308
  3.2 9.1 %collective-permute-start.1 = (bf16[784,512]{1,0:T(8,128)(2,1)S(1)}, bf16[784,512]{1,0:T(8,128)(2,1)S(1)}, u32[]{:S(2)}, u32[]{:S(2)}) collective-permute-start(bf16[784,512]{1,0:T(8,128)(2,1)S(1)} %get-tuple-element.13.own_ref.own), channel_id=1, source_target_pairs={{0,1},{1,0},{2,3},{3,2},{4,5},{5,4},{6,7},{7,6},{8,9},{9,8},{10,11... | collective-permute-start | bytes 2408456 | tf_op jit(solution)/shard_map/ppermute | solution.py:260
  5.3 7.0 %collective-permute-start = (bf16[784,128]{1,0:T(8,128)(2,1)S(1)}, bf16[784,128]{1,0:T(8,128)(2,1)S(1)}, u32[]{:S(2)}, u32[]{:S(2)}) collective-permute-start(bf16[784,128]{1,0:T(8,128)(2,1)S(1)} %get-tuple-element.12), channel_id=1, source_target_pairs={{0,127},{1,2},{2,1},{3,4},{4,3},{5,6},{6,5},{7,8},{8,7},{9,10},{10... | collective-permute-start | bytes 602120 | tf_op jit(solution)/shard_map/ppermute | solution.py:264
  12.3 0.9 copy-start.7
  15.0 0.7 copy-start.10
  15.7 3.2 %collective-permute-start.7 = (f32[32,128]{1,0:T(8,128)S(1)}, f32[32,128]{1,0:T(8,128)S(1)}, u32[]{:S(2)}, u32[]{:S(2)}) collective-permute-start(f32[32,128]{1,0:T(8,128)S(1)} %get-tuple-element.18), channel_id=1, source_target_pairs={{0,1},{1,0},{2,3},{3,2},{4,5},{5,4},{6,7},{7,6},{8,9},{9,8},{10,11... | collective-permute-start | bytes 49160 | tf_op jit(solution)/shard_map/ppermute | solution.py:260
  19.6 35.2 %all-to-all-start.2 = ((f32[16,32,128]{2,1,0:T(8,128)}), f32[16,32,128]{2,1,0:T(8,128)S(1)}, u32[]{:S(2)}, u32[]{:S(2)}) async-start(f32[16,32,128]{2,1,0:T(8,128)} %broadcast_in_dim.11), calls=%async_computation.2 | async-start | bytes 524288 | tf_op jit(solution)/shard_map/all_to_all | solution.py:276
  35.9 30.8 %collective-permute-start.4 = (bf16[784,512]{1,0:T(8,128)(2,1)S(1)}, bf16[784,512]{1,0:T(8,128)(2,1)}, u32[]{:S(2)}, u32[]{:S(2)}) collective-permute-start(bf16[784,512]{1,0:T(8,128)(2,1)S(1)} %get-tuple-element.13.own_ref.own), channel_id=1, source_target_pairs={{0,126},{1,3},{2,0},{3,5},{4,2},{5,7},{6,4},{7,9},{8,6},{9,11},{10... | collective-permute-start | bytes 2408456 | tf_op jit(solution)/shard_map/ppermute | solution.py:272
  37.9 30.7 %collective-permute-start.3 = (bf16[784,512]{1,0:T(8,128)(2,1)S(1)}, bf16[784,512]{1,0:T(8,128)(2,1)}, u32[]{:S(2)}, u32[]{:S(2)}) collective-permute-start(bf16[784,512]{1,0:T(8,128)(2,1)S(1)} %get-tuple-element.13.own_ref.own), channel_id=1, source_target_pairs={{0,2},{1,127},{2,4},{3,1},{4,6},{5,3},{6,8},{7,5},{8,10},{9,7},{10... | collective-permute-start | bytes 2408456 | tf_op jit(solution)/shard_map/ppermute | solution.py:268
  54.8 0.7 copy-start.11
  55.5 24.4 %all-to-all-start.1 = ((f32[4,768,128]{2,1,0:T(8,128)}), f32[4,768,128]{2,1,0:T(8,128)S(1)}, u32[]{:S(2)}, u32[]{:S(2)}) async-start(f32[4,768,128]{2,1,0:T(8,128)} %far_weights.1), calls=%async_computation.1 | async-start | bytes 3145728 | tf_op jit(solution)/shard_map/all_to_all | solution.py:322
  66.7 18.7 %collective-permute-start.5 = (bf16[784,512]{1,0:T(8,128)(2,1)}, bf16[784,512]{1,0:T(8,128)(2,1)}, u32[]{:S(2)}, u32[]{:S(2)}) collective-permute-start(bf16[784,512]{1,0:T(8,128)(2,1)} %collective-permute-done.4.far_z), channel_id=1, source_target_pairs={{0,1},{1,0},{2,3},{3,2},{4,5},{5,4},{6,7},{7,6},{8,9},{9,8},{10,11... | collective-permute-start | bytes 2408456 | tf_op jit(solution)/shard_map/ppermute | solution.py:260
  68.6 16.7 %collective-permute-start.6 = (bf16[784,512]{1,0:T(8,128)(2,1)}, bf16[784,512]{1,0:T(8,128)(2,1)}, u32[]{:S(2)}, u32[]{:S(2)}) collective-permute-start(bf16[784,512]{1,0:T(8,128)(2,1)} %collective-permute-done.3.near_z), channel_id=1, source_target_pairs={{0,1},{1,0},{2,3},{3,2},{4,5},{5,4},{6,7},{7,6},{8,9},{9,8},{10,11... | collective-permute-start | bytes 2408456 | tf_op jit(solution)/shard_map/ppermute | solution.py:260
  71.0 14.3 %collective-permute-start.2 = (bf16[3,64,512]{2,1,0:T(8,128)(2,1)}, bf16[3,64,512]{2,1,0:T(8,128)(2,1)S(1)}, u32[]{:S(2)}, u32[]{:S(2)}) collective-permute-start(bf16[3,64,512]{2,1,0:T(8,128)(2,1)} %copy-done.10), channel_id=1, source_target_pairs={{0,125},{1,4},{2,127},{3,6},{4,1},{5,8},{6,3},{7,10},{8,5},{9,12},... | collective-permute-start | bytes 589832 | tf_op jit(solution)/shard_map/ppermute | solution.py:264
  80.5 13.9 %all-to-all-start.3 = ((f32[8,32,128]{2,1,0:T(8,128)}), f32[8,32,128]{2,1,0:T(8,128)S(1)}, u32[]{:S(2)}, u32[]{:S(2)}) async-start(f32[8,32,128]{2,1,0:T(8,128)} %broadcast_in_dim.12), calls=%async_computation.3 | async-start | bytes 262144 | tf_op jit(solution)/shard_map/all_to_all | solution.py:276
  85.3 1.7 %copy-start = (bf16[1,2,768,768]{3,2,1,0:T(8,128)(2,1)S(1)}, bf16[1,2,768,768]{3,2,1,0:T(8,128)(2,1)}, u32[]{:S(2)}) copy-start(bf16[1,2,768,768]{3,2,1,0:T(8,128)(2,1)} %param.13) | copy-start | bytes 7077892
  92.8 0.9 copy-start.2
  93.7 0.7 copy-start.4
  94.4 16.3 %copy-start.5 = (f32[768,128]{1,0:T(8,128)S(1)}, f32[768,128]{1,0:T(8,128)}, u32[]{:S(2)}) copy-start(f32[768,128]{1,0:T(8,128)} %copy-done.4) | copy-start | bytes 1179652
  94.4 16.3 %all-to-all-start = ((bf16[4,768,128]{2,1,0:T(8,128)(2,1)}), bf16[4,768,128]{2,1,0:T(8,128)(2,1)S(1)}, u32[]{:S(2)}, u32[]{:S(2)}) async-start(bf16[4,768,128]{2,1,0:T(8,128)(2,1)} %copy-done.2), calls=%async_computation | async-start | bytes 1572864 | tf_op jit(solution)/shard_map/all_to_all | solution.py:339

commit v2 on v1

v2 whole, which is shorter than its diff:
```python
import functools

import jax
import jax.numpy as jnp
from jax import lax
from jax.experimental import pallas as pl
from jax.experimental.pallas import tpu as pltpu
from jax.sharding import Mesh
from jax.sharding import PartitionSpec as P

CLU = ("clu_0", "clu_1", "clu_2")
PAD = 16
F32 = jnp.float32
BF16 = jnp.bfloat16
VMEM = pl.BlockSpec(memory_space=pltpu.VMEM)
SMEM = pl.BlockSpec(memory_space=pltpu.SMEM)
ANY = pl.BlockSpec(memory_space=pl.ANY)
HBM = pl.BlockSpec(memory_space=pltpu.MemorySpace.HBM)


def params(mib):
    return pltpu.CompilerParams(vmem_limit_bytes=mib * 2**20)


def iota(shape, dim):
    return lax.broadcasted_iota(jnp.int32, shape, dim)


def dot(a, b):
    return jnp.dot(a, b, preferred_element_type=F32)


def as_column(row):
    size = row.shape[1]
    square = (size, size)
    spread = jnp.where(iota(square, 0) == iota(square, 1), jnp.broadcast_to(row, square), 0.0)
    return jnp.sum(spread, axis=1, keepdims=True)


def count_before(mask):
    size = mask.shape[1]
    square = (size, size)
    upto = (iota(square, 0) <= iota(square, 1)).astype(F32).astype(BF16)
    rows = jnp.broadcast_to(mask, (16, size)).astype(BF16)
    return dot(rows, upto)[:1] - 1.0


def chosen(column, width):
    shape = (column.shape[0], width)
    return (jnp.broadcast_to(column, shape) == iota(shape, 1).astype(F32)).astype(F32).astype(BF16)


def rows_of(v, width):
    return [v[:, i : i + width] for i in range(0, v.shape[1], width)]


def stacked(lines, width):
    at = iota((PAD, width), 0)
    out = jnp.zeros((PAD, width), F32)
    for i, v in enumerate(lines):
        if v.shape[1] < width:
            v = jnp.concatenate([v, jnp.zeros((1, width - v.shape[1]), F32)], axis=1)
        out = jnp.where(at == i, v, out)
    return out.astype(BF16)


def dress_kernel(clusters, sc, order_ref, forces, bases, block_ref, halo_ref, base_ref, sems):
    rows, columns = forces.shape
    comps, rank, size = base_ref.shape
    part = halo_ref.shape[1]
    start = pl.multiple_of(sc[1] * part, part)
    copies = [
        pltpu.make_async_copy(bases.at[1 - sc[0]], base_ref, sems.at[2]),
        pltpu.make_async_copy(forces.at[:, pl.ds(start, part)], halo_ref.at[pl.ds(0, rows)], sems.at[0]),
        pltpu.make_async_copy(forces, block_ref.at[pl.ds(0, rows)], sems.at[1]),
    ]
    for copy in copies:
        copy.start()
    rel = order_ref[...] - (sc[3] - 1) * size
    rel = jnp.where(rel < 0, rel + clusters * size, rel)
    rel = jnp.where(rel >= clusters * size, rel - clusters * size, rel)
    high = (rel >= size).astype(jnp.int32) + (rel >= 2 * size).astype(jnp.int32)
    low = (rel - high * size).astype(F32)
    high = high.astype(F32)
    block_ref[rows : rows + PAD] = stacked([low, high], columns)
    halo_ref[rows:] = stacked(rows_of(low, part) + rows_of(high, part), part)
    copies[0].wait()
    half = rank // 2
    for comp in range(comps):
        at = rows + PAD + comp * half
        block_ref[at : at + half, :size] = base_ref[comp, :half]
        block_ref[at : at + half, size : 2 * size] = base_ref[comp, half:]
    copies[1].wait()
    copies[2].wait()


def pieces_kernel(
    sc, order_ref, first_ref, last_ref, own_ref, pair_ref, bases_ref, after, many_ref, thin_ref, orders_ref
):
    del after
    _, comps, rank, size = bases_ref.shape
    rows = comps * size
    part = first_ref.shape[1]
    quarter = size // 4
    half = rank // 2
    per = size // part
    core = sc[0]
    start = pl.multiple_of(sc[1] * part, part)

    def narrow(ref):
        tail = ref[rows:].astype(F32)
        return [
            jnp.concatenate([tail[at + i : at + i + 1] for i in range(per)], axis=1) for at in (0, per)
        ]

    pair_tail = pair_ref[rows : rows + PAD].astype(F32)
    own_order = order_ref[...].astype(F32)
    orders = [
        narrow(first_ref),
        [own_order[0:1, :size], own_order[1:2, :size]],
        [pair_tail[0:1, :size], pair_tail[1:2, :size]],
        narrow(last_ref),
    ]
    for i, (low, high) in enumerate(orders):
        orders_ref[2 * i : 2 * i + 1] = low
        orders_ref[2 * i + 1 : 2 * i + 2] = high

    def pick_of(low, high):
        seat = jnp.where(core == 0, high, 2.0 - high)
        return chosen(as_column(seat * size + low), 3 * size)

    own_pick, pair_pick = pick_of(*orders[1]), pick_of(*orders[2])
    total = jnp.zeros((rank, part), F32)
    for comp in range(comps):
        span = slice(comp * size, (comp + 1) * size)
        line = (
            first_ref[span],
            own_ref[span, pl.ds(start, part)],
            pair_ref[span, pl.ds(start, part)],
            last_ref[span],
        )
        got = [
            sum(dot(pick[:, i * size : (i + 1) * size], line[i + at]) for i in range(3)).astype(BF16)
            for at, pick in enumerate((own_pick, pair_pick))
        ]
        at = rows + PAD + comp * half
        pair_bases = jnp.concatenate(
            [pair_ref[at : at + half, :size], pair_ref[at : at + half, size : 2 * size]], axis=0
        )
        total += dot(bases_ref[core, comp], got[0]) + dot(pair_bases, got[1])
    total = total.astype(BF16)
    for i in range(many_ref.shape[0]):
        many_ref[i] = total

    low, high = orders[0]
    mine = high == jnp.where(core == 0, 2.0, 0.0)
    place = count_before(mine.astype(F32))
    shape = (quarter, size)
    seats = jnp.broadcast_to(jnp.where(mine, place, -1.0), shape)
    into = (seats == iota(shape, 0).astype(F32)).astype(F32).astype(BF16)
    pack = dot(into, chosen(as_column(low), size)).astype(BF16)
    for comp in range(comps):
        thin_ref[comp * quarter : (comp + 1) * quarter] = dot(
            pack, own_ref[comp * size : (comp + 1) * size]
        ).astype(BF16)
    thin_ref[comps * quarter :] = stacked([low, high], thin_ref.shape[1])


def far_kernel(planes, sc, target, keeps, scale, basis_ref, coupling_ref, weights_ref, high_ref, low_ref):
    blocks, rank, _ = coupling_ref.shape
    width = high_ref.shape[1]
    lane = iota((rank, width), 1)
    for b in range(blocks):
        slot = jnp.where(target[b] < 2, 0, lax.rem(target[b] - 2 - sc[2] + planes, planes))
        first = slot * rank
        tile = coupling_ref[b].astype(F32) * scale[b]
        tile = jnp.concatenate([tile] * (width // rank), axis=1)
        tile = jnp.where((lane >= first) & (lane < first + keeps[b]), tile, 0.0)
        high = tile.astype(BF16)
        high_ref[b * rank : (b + 1) * rank] = high
        low_ref[b * rank : (b + 1) * rank] = (tile - high.astype(F32)).astype(BF16)
    dims = (((0,), (0,)), ((), ()))
    total = lax.dot_general(basis_ref[...], high_ref[...], dims, preferred_element_type=F32)
    total += lax.dot_general(basis_ref[...], low_ref[...], dims, preferred_element_type=F32)
    weights_ref[...] = total


def near_kernel(
    clusters, sc, near_col, orders_ref, tiles, own, thin, near_z, pair_far, pair, far_z, pair_near,
    split, tile_ref, thin_tail, window, blocks, result, sems, tile_sems, tail_sem, out_sems,
):
    count, rows, _ = tiles.shape
    columns = own.shape[1]
    size = rows // 3
    quarter = size // 4
    groups, _, part = split.shape
    core = sc[0]
    seats = (thin, near_z, pair_far, own, pair, far_z, pair_near)
    offs = []
    for j in range(count):
        off = near_col[j] - sc[3] + 2
        off = jnp.where(off < 0, off + clusters, off)
        off = jnp.where(off >= clusters, off - clusters, off) - 2
        offs.append(jnp.where(core == 0, off, -off))
    tail_copy = pltpu.make_async_copy(thin.at[pl.ds(3 * quarter, PAD)], thin_tail, tail_sem.at[0])
    tail_copy.start()
    for j in range(count):
        for o in range(-2, 3):

            @pl.when(offs[j] == o)
            def _(j=j, o=o):
                for w in range(3):
                    source = seats[o + 2 + w]
                    if o + w == -2:
                        for comp in range(3):
                            pltpu.make_async_copy(
                                source.at[pl.ds(comp * quarter, quarter)],
                                window.at[j, w, pl.ds(comp * size, quarter)],
                                sems.at[j, w, comp],
                            ).start()
                            window[j, w, comp * size + quarter : (comp + 1) * size] = jnp.zeros(
                                (size - quarter, columns), BF16
                            )
                    else:
                        pltpu.make_async_copy(
                            source.at[pl.ds(0, rows)], window.at[j, w], sems.at[j, w, 0]
                        ).start()

        pltpu.make_async_copy(tiles.at[j], tile_ref.at[j], tile_sems.at[j]).start()
    tail_copy.wait()
    tail = thin_tail[...].astype(F32)
    for j in range(count):
        edge = offs[j] == -2
        low, high = tail[0:1, :size], tail[1:2, :size]
        for i in range(4):
            low = jnp.where(offs[j] == i - 1, orders_ref[2 * i : 2 * i + 1], low)
            high = jnp.where(offs[j] == i - 1, orders_ref[2 * i + 1 : 2 * i + 2], high)
        seat = jnp.where(core == 0, high, 2.0 - high)
        first = seat == 0.0
        place = count_before(first.astype(F32))
        low = jnp.where(jnp.logical_and(first, edge), place, low)
        pick = chosen(as_column(seat * size + low), 3 * size)
        for w in range(1, 3):
            pltpu.make_async_copy(own, window.at[j, w], sems.at[j, w, 0]).wait()

        @pl.when(edge)
        def _(j=j):
            for comp in range(3):
                pltpu.make_async_copy(
                    thin.at[pl.ds(comp * quarter, quarter)],
                    window.at[j, 0, pl.ds(comp * size, quarter)],
                    sems.at[j, 0, comp],
                ).wait()

        @pl.when(jnp.logical_not(edge))
        def _(j=j):
            pltpu.make_async_copy(own, window.at[j, 0], sems.at[j, 0, 0]).wait()

        for comp in range(3):
            span = slice(comp * size, (comp + 1) * size)
            got = dot(pick[:, :size], window[j, 0, span])
            for w in range(1, 3):
                got += dot(pick[:, w * size : (w + 1) * size], window[j, w, span])
            blocks[j, span] = got.astype(BF16)
    for j in range(count):
        pltpu.make_async_copy(tiles.at[j], tile_ref.at[j], tile_sems.at[j]).wait()
    outs = []
    for r in range(3):
        span = slice(r * size, (r + 1) * size)
        total = dot(tile_ref[0, span], blocks[0])
        for j in range(1, count):
            total += dot(tile_ref[j, span], blocks[j])
        for i in range(groups):
            result[i, span] = total[:, i * part : (i + 1) * part].astype(BF16)
        outs.append(
            pltpu.make_async_copy(
                result.at[:, pl.ds(r * size, size)], split.at[:, pl.ds(r * size, size)], out_sems.at[r]
            )
        )
        outs[-1].start()
    for copy in outs:
        copy.wait()


def add_kernel(a_ref, b_ref, out_ref):
    out_ref[...] = a_ref[...] + b_ref[...]


def reduce_kernel(many_ref, sums_ref):
    total = many_ref[0].astype(F32)
    for i in range(1, many_ref.shape[0]):
        total += many_ref[i].astype(F32)
    for i in range(sums_ref.shape[0]):
        sums_ref[i] = total


def last_kernel(sc, arrived_ref, sums_ref, *refs):
    *weights_refs, out_ref, table_ref = refs
    groups = arrived_ref.shape[0]
    count, rank, _ = sums_ref.shape
    planes = count // 2
    plane = sc[2]
    half = planes // 2
    other = jnp.where(plane < half, half, 0)
    coarse = sums_ref[2 * other]
    for i in range(1, half):
        coarse += sums_ref[2 * (other + i)]
    table_ref[:rank] = coarse
    for i in range(1, planes):
        at = lax.rem(plane + i, planes)
        table_ref[i * rank : (i + 1) * rank] = sums_ref[2 * at + 1]
    weights = weights_refs[0][...]
    for ref in weights_refs[1:]:
        weights += ref[...]
    total = jnp.dot(
        weights, table_ref[...], precision=lax.Precision.HIGHEST, preferred_element_type=F32
    )
    for i in range(groups):
        total += arrived_ref[i].astype(F32)
    out_ref[...] = total


def tie_kernel(*refs):
    del refs


def tied(value, *after):
    return pl.pallas_call(
        tie_kernel,
        out_shape=shape_of(value.shape, value.dtype),
        in_specs=[ANY] * (1 + len(after)),
        out_specs=ANY,
        input_output_aliases={0: 0},
        compiler_params=params(1),
        name="tie",
    )(value, *after)


def in_hbm(*values):
    return [pltpu.with_memory_space_constraint(v, pltpu.MemorySpace.HBM) for v in values]


def shape_of(dims, dtype):
    return jax.ShapeDtypeStruct(dims, dtype)


def on_device(
    forces, order, bases, near_tiles, near_col, far_basis, far_coupling, far_scale, far_rank, far_target
):
    clusters = lax.axis_size(CLU)
    planes = lax.axis_size("clu_0")
    steps = lax.axis_size("clu_1")
    groups = lax.axis_size("grp")
    size = order.shape[0]
    comps, _, columns = forces.shape
    rows = comps * size
    part = columns // groups
    _, rank = bases.shape[:2]
    count = near_tiles.shape[1]
    far_count = far_target.shape[1]
    width = planes * rank
    sc = jnp.stack(
        [lax.axis_index("clu_2"), lax.axis_index("grp"), lax.axis_index("clu_0"), lax.axis_index(CLU)]
    ).astype(jnp.int32)

    def swapped(v):
        return lax.ppermute(v, "clu_2", [(0, 1), (1, 0)])

    def sent(v, by):
        pairs = [(i, (i + by if i % 2 else i - by) % clusters) for i in range(clusters)]
        return lax.ppermute(v, CLU, pairs)

    def exchanged(v, axis):
        return lax.all_to_all(v, axis, split_axis=0, concat_axis=0, tiled=True)

    chain = forces.reshape(rows, columns)
    near_z = sent(chain, -2)
    far_z = sent(chain, 2)
    by_comp = bases.transpose(0, 2, 1, 3)
    block, halo = pl.pallas_call(
        functools.partial(dress_kernel, clusters),
        out_shape=(
            shape_of((rows + PAD + comps * rank // 2, columns), BF16),
            shape_of((rows + PAD, part), BF16),
        ),
        in_specs=[SMEM, VMEM, HBM, HBM],
        out_specs=(VMEM, VMEM),
        scratch_shapes=[pltpu.VMEM((comps, rank, size), BF16), pltpu.SemaphoreType.DMA((3,))],
        compiler_params=params(8),
        name="dress",
    )(sc, order.reshape(1, size), *in_hbm(chain, by_comp))
    first = sent(halo, 1)
    last = sent(halo, 2)
    pair = swapped(block)
    weights = pl.pallas_call(
        functools.partial(far_kernel, planes),
        out_shape=shape_of((rows, width), F32),
        in_specs=[SMEM, SMEM, SMEM, SMEM, VMEM, VMEM],
        out_specs=VMEM,
        scratch_shapes=[pltpu.VMEM((far_count * rank, width), BF16)] * 2,
        compiler_params=params(8),
        name="far_weights",
    )(
        sc, far_target[0], far_rank[0], far_scale[0],
        far_basis.reshape(far_count * rank, rows), far_coupling[0],
    )
    other = lax.ppermute(weights, "grp", [(i, i ^ 1) for i in range(groups)])
    both = pl.pallas_call(
        add_kernel,
        out_shape=shape_of((rows, width), F32),
        in_specs=[VMEM, VMEM],
        out_specs=VMEM,
        compiler_params=params(4),
        name="add",
    )(weights, other)
    rest = lax.ppermute(both, "grp", [(i, groups - 1 - i) for i in range(groups)])

    many, thin, orders = pl.pallas_call(
        pieces_kernel,
        out_shape=(
            shape_of((steps, rank, part), BF16),
            shape_of((rows // 4 + PAD, columns), BF16),
            shape_of((8, size), F32),
        ),
        in_specs=[SMEM] + [VMEM] * 6 + [ANY],
        out_specs=(VMEM, VMEM, VMEM),
        compiler_params=params(12),
        name="pieces",
    )(sc, block[rows : rows + PAD], first, last, chain, pair, by_comp, weights)
    many = exchanged(many, "clu_1")
    thin = sent(thin, 3)

    near_z = tied(near_z, many, thin)
    far_z = tied(far_z, many, both)
    pair_near = swapped(near_z)
    pair_far = swapped(far_z)
    sums = pl.pallas_call(
        reduce_kernel,
        out_shape=shape_of((2 * planes, rank, part), F32),
        in_specs=[VMEM],
        out_specs=VMEM,
        compiler_params=params(4),
        name="reduce",
    )(many)
    sums = exchanged(sums, ("clu_0", "clu_2"))
    split = pl.pallas_call(
        functools.partial(near_kernel, clusters),
        out_shape=shape_of((groups, rows, part), BF16),
        in_specs=[SMEM, SMEM, VMEM, HBM, HBM] + [ANY] * 6,
        out_specs=HBM,
        scratch_shapes=[
            pltpu.VMEM((count, rows, rows), BF16),
            pltpu.VMEM((PAD, columns), BF16),
            pltpu.VMEM((count, 3, rows, columns), BF16),
            pltpu.VMEM((count, rows, columns), BF16),
            pltpu.VMEM((groups, rows, part), BF16),
            pltpu.SemaphoreType.DMA((count, 3, 3)),
            pltpu.SemaphoreType.DMA((count,)),
            pltpu.SemaphoreType.DMA((1,)),
            pltpu.SemaphoreType.DMA((3,)),
        ],
        compiler_params=params(20),
        name="near",
    )(
        sc, near_col[0], orders,
        *in_hbm(near_tiles[0], chain), thin, near_z, pair_far, pair, far_z, pair_near,
    )
    arrived = exchanged(tied(split, rest), "grp")
    velocity = pl.pallas_call(
        last_kernel,
        out_shape=shape_of((rows, part), F32),
        in_specs=[SMEM, VMEM, VMEM] + [VMEM] * 2,
        out_specs=VMEM,
        scratch_shapes=[pltpu.VMEM((width, part), F32)],
        compiler_params=params(8),
        name="last",
    )(sc, arrived, sums, both, rest)
    return velocity.reshape(comps, size, part)


def solution(mesh):
    clusters = mesh.shape["clu"]
    torus = Mesh(
        mesh.devices.reshape(mesh.shape["grp"], 4, clusters // 8, 2),
        ("grp", "clu_0", "clu_1", "clu_2"),
    )
    in_specs = (
        P(None, CLU, None),
        P(CLU),
        P(None, None, None, CLU),
        P(CLU, "grp", None, None),
        P(CLU, "grp"),
        P(CLU, "grp", None, None),
        P(CLU, "grp", None, None),
        P(CLU, "grp"),
        P(CLU, "grp"),
        P(CLU, "grp"),
    )
    return jax.shard_map(
        on_device, mesh=torus, in_specs=in_specs, out_specs=P(None, CLU, "grp"), check_vma=False
    )
```

time: 113 us -> 105 us (0.929)
  the two profiles are of different devices: /device:TPU:34 before, /device:TPU:1 now
where the time goes in v2:
time: 105 us; the launch traced here: 104 us
  starting transfers between devices  54.5 us (52%)
  blocking collectives  15 us (14%)
  Pallas kernels  14.1 us (13%)
  waiting for transfers between devices  12.8 us (12%)
  local copies, waits for them, and re-layouts  7.45 us (7%)
    ppermute x5, starting transfers between devices, sent(): return lax.ppermute(v, CLU, pairs)  18.5 us
    ppermute x3, starting transfers between devices, swapped(): return lax.ppermute(v, 'clu_2', [(0, 1), (1, 0)])  15.1 us
    all_to_all x1, blocking collectives, exchanged(): return lax.all_to_all(v, axis, split_axis=0, concat_axis=0, tiled=True)  15 us
    all_to_all x2, starting transfers between devices, exchanged(): return lax.all_to_all(v, axis, split_axis=0, concat_axis=0, tiled=True)  13.6 us
    ppermute x5, waiting for transfers between devices, sent(): return lax.ppermute(v, CLU, pairs)  8.22 us
    unnamed x30, local copies, waits for them, and re-layouts  7.45 us
    pallas_call x1, Pallas kernels, on_device(): pl.pallas_call(functools.partial(near_kernel, clusters), out_shape=shape_...  5.91 us
    ppermute x1, waiting for transfers between devices, on_device(): other = lax.ppermute(weights, 'grp', [(i, i ^ 1) for i in range(groups)])  4.32 us
  transfers between devices with their start and end apart: 12, of which 4 were waited for; matrix products, arithmetic and copies ran while one was open for 0% of the time, Pallas kernels for 10%

profile of v2, /device:TPU:1, one launch (start us, length us, event | category | flops | bytes accessed | tf_op | source)
XLA Modules:
  0.0 104.2 jit_solution(10373109011306324502)
XLA Ops:
  0.0 0.0 copy-start
  0.0 0.0 copy-start.2
  0.0 0.1 pad_add_fusion.sc
  0.1 0.0 copy-start.4
  0.1 0.0 copy-start.9
  0.1 0.7 copy-done.9
  0.8 1.8 %dress.1 = (bf16[832,512]{1,0:T(8,128)(2,1)S(1)}, bf16[784,128]{1,0:T(8,128)(2,1)S(1)}) custom-call(s32[4]{0:T(128)S(1)} %pad_add_fusion.sc, s32[1,256]{1,0:T(1,128)S(1)} %bitcast.24, bf16[768,512]{1,0:T(8,128)(2,1)} %bitcast.15, bf16[2,3,32,256]{3,2,1,0:T(8,128)(2,1)} %bitcast.21), custom_call_target="tpu_custom_call" | custom-call | tf_op jit(solution)/shard_map/dress/pallas_call | solution.py:380
  2.7 8.8 %collective-permute-start.2 = (bf16[832,512]{1,0:T(8,128)(2,1)S(1)}, bf16[832,512]{1,0:T(8,128)(2,1)S(1)}, u32[]{:S(2)}, u32[]{:S(2)}) collective-permute-start(bf16[832,512]{1,0:T(8,128)(2,1)S(1)} %get-tuple-element.10), channel_id=1, source_target_pairs={{0,1},{1,0},{2,3},{3,2},{4,5},{5,4},{6,7},{7,6},{8,9},{9,8},{10,11... | collective-permute-start | bytes 2555912 | tf_op jit(solution)/shard_map/ppermute | solution.py:367
  11.5 1.9 %collective-permute-start.5 = (bf16[768,512]{1,0:T(8,128)(2,1)}, bf16[768,512]{1,0:T(8,128)(2,1)}, u32[]{:S(2)}, u32[]{:S(2)}) collective-permute-start(bf16[768,512]{1,0:T(8,128)(2,1)} %bitcast.16), channel_id=1, source_target_pairs={{0,126},{1,3},{2,0},{3,5},{4,2},{5,7},{6,4},{7,9},{8,6},{9,11},{10... | collective-permute-start | bytes 2359304 | tf_op jit(solution)/shard_map/ppermute | solution.py:371
  13.4 7.9 %collective-permute-start.4 = (bf16[768,512]{1,0:T(8,128)(2,1)}, bf16[768,512]{1,0:T(8,128)(2,1)S(1)}, u32[]{:S(2)}, u32[]{:S(2)}) collective-permute-start(bf16[768,512]{1,0:T(8,128)(2,1)} %bitcast.17), channel_id=1, source_target_pairs={{0,2},{1,127},{2,4},{3,1},{4,6},{5,3},{6,8},{7,5},{8,10},{9,7},{10... | collective-permute-start | bytes 2359304 | tf_op jit(solution)/shard_map/ppermute | solution.py:371
  21.4 1.9 %collective-permute-start = (bf16[784,128]{1,0:T(8,128)(2,1)S(1)}, bf16[784,128]{1,0:T(8,128)(2,1)S(1)}, u32[]{:S(2)}, u32[]{:S(2)}) collective-permute-start(bf16[784,128]{1,0:T(8,128)(2,1)S(1)} %get-tuple-element.11), channel_id=1, source_target_pairs={{0,127},{1,2},{2,1},{3,4},{4,3},{5,6},{6,5},{7,8},{8,7},{9,10},{10... | collective-permute-start | bytes 602120 | tf_op jit(solution)/shard_map/ppermute | solution.py:371
  23.3 1.9 %collective-permute-start.1 = (bf16[784,128]{1,0:T(8,128)(2,1)S(1)}, bf16[784,128]{1,0:T(8,128)(2,1)S(1)}, u32[]{:S(2)}, u32[]{:S(2)}) collective-permute-start(bf16[784,128]{1,0:T(8,128)(2,1)S(1)} %get-tuple-element.11), channel_id=1, source_target_pairs={{0,126},{1,3},{2,0},{3,5},{4,2},{5,7},{6,4},{7,9},{8,6},{9,11},{10... | collective-permute-start | bytes 602120 | tf_op jit(solution)/shard_map/ppermute | solution.py:371
  25.2 0.0 copy-start.1
  25.2 1.1 %copy-done.1 = bf16[1,16,32,768]{3,2,1,0:T(8,128)(2,1)S(1)} copy-done((bf16[1,16,32,768]{3,2,1,0:T(8,128)(2,1)S(1)}, bf16[1,16,32,768]{3,2,1,0:T(8,128)(2,1)}, u32[]{:S(2)}) %copy-start.1) | copy-done | bytes 786456
  26.4 0.0 copy-start.3
  26.4 0.9 copy-done.3
  27.3 0.0 copy-start.10
  27.3 0.7 copy-done.10
  27.9 0.0 copy-start.11
  27.9 0.7 copy-done.11
  28.6 0.0 copy-start.12
  28.6 0.7 copy-done.12
  29.2 1.4 %far_weights.1.after.a_ref = f32[768,128]{1,0:T(8,128)S(1)} custom-call(s32[4]{0:T(128)S(1)} %pad_add_fusion.sc, s32[16]{0:T(128)S(1)} %bitcast.25, s32[16]{0:T(128)S(1)} %bitcast.26, f32[16]{0:T(128)S(1)} %bitcast.27, bf16[512,768]{1,0:T(8,128)(2,1)S(1)} %bitcast.20, bf16[16,32,32]{2,1,0:T(8,128)(2,1)S(1)} %bitcast.23), custom_call_target="tpu_custom_call" | custom-call | tf_op jit(solution)/shard_map/far_weights/pallas_call | solution.py:395
  30.6 5.2 %collective-permute-done.first_ref = bf16[784,128]{1,0:T(8,128)(2,1)S(1)} collective-permute-done((bf16[784,128]{1,0:T(8,128)(2,1)S(1)}, bf16[784,128]{1,0:T(8,128)(2,1)S(1)}, u32[]{:S(2)}, u32[]{:S(2)}) %collective-permute-start) | collective-permute-done | bytes 200736 | tf_op jit(solution)/shard_map/ppermute | solution.py:371
  35.8 3.1 %collective-permute-done.1.last_ref = bf16[784,128]{1,0:T(8,128)(2,1)S(1)} collective-permute-done((bf16[784,128]{1,0:T(8,128)(2,1)S(1)}, bf16[784,128]{1,0:T(8,128)(2,1)S(1)}, u32[]{:S(2)}, u32[]{:S(2)}) %collective-permute-start.1) | collective-permute-done | bytes 200736 | tf_op jit(solution)/shard_map/ppermute | solution.py:371
  38.8 0.0 collective-permute-done.2.pair_ref.pair
  38.8 0.0 copy-done
  38.8 0.0 copy-done.2
  38.8 2.5 %pieces.1 = (bf16[16,32,128]{2,1,0:T(8,128)(2,1)}, bf16[208,512]{1,0:T(8,128)(2,1)S(1)}, f32[8,256]{1,0:T(8,128)S(1)}) custom-call(s32[4]{0:T(128)S(1)} %pad_add_fusion.sc, bf16[16,512]{1,0:T(8,128)(2,1)S(1)} %slice.3.order_ref, bf16[784,128]{1,0:T(8,128)(2,1)S(1)} %collective-permute-done.first_ref, bf16[784,128]{1,0:T(8,128)(2,1)S(1)} %collective-permute-done.1.last_ref, ...), custom_call_target="tpu_custom_call" | custom-call | tf_op jit(solution)/shard_map/pieces/pallas_call | solution.py:418
  41.3 0.0 copy-done.4
  41.3 0.0 copy-start.14
  41.3 0.7 copy-done.14
  42.0 0.0 copy-start.7
  42.0 9.1 %all-to-all-start = ((bf16[16,32,128]{2,1,0:T(8,128)(2,1)}), bf16[16,32,128]{2,1,0:T(8,128)(2,1)S(1)}, u32[]{:S(2)}, u32[]{:S(2)}) async-start(bf16[16,32,128]{2,1,0:T(8,128)(2,1)} %get-tuple-element.14), calls=%async_computation | async-start | bytes 262144 | tf_op jit(solution)/shard_map/all_to_all | solution.py:374
  51.1 3.2 %collective-permute-start.6 = (f32[768,128]{1,0:T(8,128)S(1)}, f32[768,128]{1,0:T(8,128)S(1)}, u32[]{:S(2)}, u32[]{:S(2)}) collective-permute-start(f32[768,128]{1,0:T(8,128)S(1)} %far_weights.1.after.a_ref), channel_id=1, source_target_pairs={{0,128},{128,0},{256,384},{384,256},{1,129},{129,1},{257,385},{385... | collective-permute-start | bytes 1179656 | tf_op jit(solution)/shard_map/ppermute | solution.py:407
  54.3 4.8 %collective-permute-start.3 = (bf16[208,512]{1,0:T(8,128)(2,1)}, bf16[208,512]{1,0:T(8,128)(2,1)S(1)}, u32[]{:S(2)}, u32[]{:S(2)}) collective-permute-start(bf16[208,512]{1,0:T(8,128)(2,1)} %copy-done.14), channel_id=1, source_target_pairs={{0,125},{1,4},{2,127},{3,6},{4,1},{5,8},{6,3},{7,10},{8,5},{9,12},... | collective-permute-start | bytes 638984 | tf_op jit(solution)/shard_map/ppermute | solution.py:371
  59.1 4.3 %collective-permute-done.6.b_ref = f32[768,128]{1,0:T(8,128)S(1)} collective-permute-done((f32[768,128]{1,0:T(8,128)S(1)}, f32[768,128]{1,0:T(8,128)S(1)}, u32[]{:S(2)}, u32[]{:S(2)}) %collective-permute-start.6) | collective-permute-done | bytes 393248 | tf_op jit(solution)/shard_map/ppermute | solution.py:407
  63.5 0.0 collective-permute-done.5.refs_0_
  63.5 0.3 all-to-all-done.refs_1_.many_ref
  63.8 3.2 %collective-permute-start.7 = (bf16[768,512]{1,0:T(8,128)(2,1)}, bf16[768,512]{1,0:T(8,128)(2,1)}, u32[]{:S(2)}, u32[]{:S(2)}) collective-permute-start(bf16[768,512]{1,0:T(8,128)(2,1)} %tie.4.far_z), channel_id=1, source_target_pairs={{0,1},{1,0},{2,3},{3,2},{4,5},{5,4},{6,7},{7,6},{8,9},{9,8},{10,11... | collective-permute-start | bytes 2359304 | tf_op jit(solution)/shard_map/ppermute | solution.py:367
  67.0 0.0 collective-permute-done.4.refs_0_
  67.0 0.0 collective-permute-done.3.refs_2_.thin
  67.0 0.0 copy-done.7
  67.0 3.1 %collective-permute-start.8 = (bf16[768,512]{1,0:T(8,128)(2,1)S(1)}, bf16[768,512]{1,0:T(8,128)(2,1)}, u32[]{:S(2)}, u32[]{:S(2)}) collective-permute-start(bf16[768,512]{1,0:T(8,128)(2,1)S(1)} %tie.3.near_z), channel_id=1, source_target_pairs={{0,1},{1,0},{2,3},{3,2},{4,5},{5,4},{6,7},{7,6},{8,9},{9,8},{10,11... | collective-permute-start | bytes 2359304 | tf_op jit(solution)/shard_map/ppermute | solution.py:367
  70.1 4.1 %collective-permute-start.9 = (f32[768,128]{1,0:T(8,128)S(1)}, f32[768,128]{1,0:T(8,128)S(1)}, u32[]{:S(2)}, u32[]{:S(2)}) collective-permute-start(f32[768,128]{1,0:T(8,128)S(1)} %add.15.refs_2_.refs_0_), channel_id=1, source_target_pairs={{0,384},{128,256},{256,128},{384,0},{1,385},{129,257},{257,129},{3... | collective-permute-start | bytes 1179656 | tf_op jit(solution)/shard_map/ppermute | solution.py:416
  74.2 0.7 reduce.1
  74.9 4.5 %all-to-all-start.2 = ((f32[8,32,128]{2,1,0:T(8,128)}), f32[8,32,128]{2,1,0:T(8,128)S(1)}, u32[]{:S(2)}, u32[]{:S(2)}) async-start(f32[8,32,128]{2,1,0:T(8,128)} %reduce.1), calls=%async_computation.2 | async-start | bytes 262144 | tf_op jit(solution)/shard_map/all_to_all | solution.py:374
  79.4 0.0 collective-permute-done.7.pair_far
  79.4 0.0 collective-permute-done.8.pair_near
  79.4 0.0 copy-start.5
  79.4 0.7 copy-done.5
  80.1 0.0 copy-start.8
  80.1 0.7 copy-done.8
  80.8 0.0 copy-start.13
  80.8 0.7 copy-done.13
  81.4 5.9 %near.1.refs_0_ = bf16[4,768,128]{2,1,0:T(8,128)(2,1)S(1)} custom-call(s32[4]{0:T(128)S(1)} %copy-done.5, s32[2]{0:T(128)S(1)} %bitcast.28, f32[8,256]{1,0:T(8,128)S(1)} %copy-done.8, bf16[2,768,768]{2,1,0:T(8,128)(2,1)} %bitcast.29, bf16[768,512]{1,0:T(8,128)(2,1)} %bitcast.18, bf16[208,512]{1,0:T(8,128)(2,1)S(1)} %collective-permute-done.3.refs_2_.thin, ...), custom_call_target="tpu_custom_call" | custom-call | tf_op jit(solution)/shard_map/near/pallas_call | solution.py:446
  87.3 0.0 copy-start.6
  87.3 0.0 collective-permute-done.9.refs_1_
  87.4 0.0 all-to-all-done.2.sums_ref
  87.4 15.0 %all_to_all.15.arrived_ref = bf16[4,768,128]{2,1,0:T(8,128)(2,1)S(1)} all-to-all(bf16[4,768,128]{2,1,0:T(8,128)(2,1)S(1)} %tie.5), channel_id=1, replica_groups=mesh['grp'=4,'clu_0'=4,'clu_1'=16,'clu_2'=2] {'grp'}, dimensions={0} | all-to-all | bytes 1572864 | tf_op jit(solution)/shard_map/all_to_all | solution.py:374
  102.4 0.0 copy-done.6
  102.4 1.8 %last.1 = f32[768,128]{1,0:T(8,128)} custom-call(s32[4]{0:T(128)S(1)} %copy-done.6, bf16[4,768,128]{2,1,0:T(8,128)(2,1)S(1)} %all_to_all.15.arrived_ref, f32[8,32,128]{2,1,0:T(8,128)S(1)} %all-to-all-done.2.sums_ref, f32[768,128]{1,0:T(8,128)S(1)} %add.15.refs_2_.refs_0_, f32[768,128]{1,0:T(8,128)S(1)} %collective-permute-done.9.refs_1_), custom_call_target="tpu_custom_call" | custom-call | tf_op jit(solution)/shard_map/last/pallas_call | solution.py:469
  (5 shorter events, 0.0 us)
Async XLA Ops:
  0.0 38.8 %copy-start = (bf16[3,256,512]{2,1,0:T(8,128)(2,1)S(1)}, bf16[3,256,512]{2,1,0:T(8,128)(2,1)}, u32[]{:S(2)}) copy-start(bf16[3,256,512]{2,1,0:T(8,128)(2,1)} %param.10) | copy-start | bytes 2359300
  0.0 38.8 %copy-start.2 = (bf16[2,32,3,256]{3,1,2,0:T(8,128)(2,1)S(1)}, bf16[2,32,3,256]{3,1,2,0:T(8,128)(2,1)}, u32[]{:S(2)}) copy-start(bf16[2,32,3,256]{3,1,2,0:T(8,128)(2,1)} %param.12) | copy-start | bytes 294916
  0.1 41.2 %copy-start.4 = (s32[4]{0:T(128)}, s32[4]{0:T(128)S(1)}, u32[]{:S(2)}) copy-start(s32[4]{0:T(128)S(1)} %pad_add_fusion.sc) | copy-start | bytes 52
  0.1 0.7 copy-start.9
  2.7 36.1 %collective-permute-start.2 = (bf16[832,512]{1,0:T(8,128)(2,1)S(1)}, bf16[832,512]{1,0:T(8,128)(2,1)S(1)}, u32[]{:S(2)}, u32[]{:S(2)}) collective-permute-start(bf16[832,512]{1,0:T(8,128)(2,1)S(1)} %get-tuple-element.10), channel_id=1, source_target_pairs={{0,1},{1,0},{2,3},{3,2},{4,5},{5,4},{6,7},{7,6},{8,9},{9,8},{10,11... | collective-permute-start | bytes 2555912 | tf_op jit(solution)/shard_map/ppermute | solution.py:367
  11.5 52.0 %collective-permute-start.5 = (bf16[768,512]{1,0:T(8,128)(2,1)}, bf16[768,512]{1,0:T(8,128)(2,1)}, u32[]{:S(2)}, u32[]{:S(2)}) collective-permute-start(bf16[768,512]{1,0:T(8,128)(2,1)} %bitcast.16), channel_id=1, source_target_pairs={{0,126},{1,3},{2,0},{3,5},{4,2},{5,7},{6,4},{7,9},{8,6},{9,11},{10... | collective-permute-start | bytes 2359304 | tf_op jit(solution)/shard_map/ppermute | solution.py:371
  13.4 53.6 %collective-permute-start.4 = (bf16[768,512]{1,0:T(8,128)(2,1)}, bf16[768,512]{1,0:T(8,128)(2,1)S(1)}, u32[]{:S(2)}, u32[]{:S(2)}) collective-permute-start(bf16[768,512]{1,0:T(8,128)(2,1)} %bitcast.17), channel_id=1, source_target_pairs={{0,2},{1,127},{2,4},{3,1},{4,6},{5,3},{6,8},{7,5},{8,10},{9,7},{10... | collective-permute-start | bytes 2359304 | tf_op jit(solution)/shard_map/ppermute | solution.py:371
  21.4 14.4 %collective-permute-start = (bf16[784,128]{1,0:T(8,128)(2,1)S(1)}, bf16[784,128]{1,0:T(8,128)(2,1)S(1)}, u32[]{:S(2)}, u32[]{:S(2)}) collective-permute-start(bf16[784,128]{1,0:T(8,128)(2,1)S(1)} %get-tuple-element.11), channel_id=1, source_target_pairs={{0,127},{1,2},{2,1},{3,4},{4,3},{5,6},{6,5},{7,8},{8,7},{9,10},{10... | collective-permute-start | bytes 602120 | tf_op jit(solution)/shard_map/ppermute | solution.py:371
  23.3 15.5 %collective-permute-start.1 = (bf16[784,128]{1,0:T(8,128)(2,1)S(1)}, bf16[784,128]{1,0:T(8,128)(2,1)S(1)}, u32[]{:S(2)}, u32[]{:S(2)}) collective-permute-start(bf16[784,128]{1,0:T(8,128)(2,1)S(1)} %get-tuple-element.11), channel_id=1, source_target_pairs={{0,126},{1,3},{2,0},{3,5},{4,2},{5,7},{6,4},{7,9},{8,6},{9,11},{10... | collective-permute-start | bytes 602120 | tf_op jit(solution)/shard_map/ppermute | solution.py:371
  25.2 1.1 %copy-start.1 = (bf16[1,16,32,768]{3,2,1,0:T(8,128)(2,1)S(1)}, bf16[1,16,32,768]{3,2,1,0:T(8,128)(2,1)}, u32[]{:S(2)}) copy-start(bf16[1,16,32,768]{3,2,1,0:T(8,128)(2,1)} %param.15) | copy-start | bytes 2359300
  26.4 0.9 copy-start.3
  27.3 0.7 copy-start.10
  27.9 0.7 copy-start.11
  28.6 0.7 copy-start.12
  41.3 0.7 copy-start.14
  42.0 25.1 %copy-start.7 = (f32[8,256]{1,0:T(8,128)}, f32[8,256]{1,0:T(8,128)S(1)}, u32[]{:S(2)}) copy-start(f32[8,256]{1,0:T(8,128)S(1)} %get-tuple-element.12.orders_ref) | copy-start | bytes 24580
  42.0 21.8 %all-to-all-start = ((bf16[16,32,128]{2,1,0:T(8,128)(2,1)}), bf16[16,32,128]{2,1,0:T(8,128)(2,1)S(1)}, u32[]{:S(2)}, u32[]{:S(2)}) async-start(bf16[16,32,128]{2,1,0:T(8,128)(2,1)} %get-tuple-element.14), calls=%async_computation | async-start | bytes 262144 | tf_op jit(solution)/shard_map/all_to_all | solution.py:374
  51.1 12.4 %collective-permute-start.6 = (f32[768,128]{1,0:T(8,128)S(1)}, f32[768,128]{1,0:T(8,128)S(1)}, u32[]{:S(2)}, u32[]{:S(2)}) collective-permute-start(f32[768,128]{1,0:T(8,128)S(1)} %far_weights.1.after.a_ref), channel_id=1, source_target_pairs={{0,128},{128,0},{256,384},{384,256},{1,129},{129,1},{257,385},{385... | collective-permute-start | bytes 1179656 | tf_op jit(solution)/shard_map/ppermute | solution.py:407
  54.3 12.7 %collective-permute-start.3 = (bf16[208,512]{1,0:T(8,128)(2,1)}, bf16[208,512]{1,0:T(8,128)(2,1)S(1)}, u32[]{:S(2)}, u32[]{:S(2)}) collective-permute-start(bf16[208,512]{1,0:T(8,128)(2,1)} %copy-done.14), channel_id=1, source_target_pairs={{0,125},{1,4},{2,127},{3,6},{4,1},{5,8},{6,3},{7,10},{8,5},{9,12},... | collective-permute-start | bytes 638984 | tf_op jit(solution)/shard_map/ppermute | solution.py:371
  63.8 15.6 %collective-permute-start.7 = (bf16[768,512]{1,0:T(8,128)(2,1)}, bf16[768,512]{1,0:T(8,128)(2,1)}, u32[]{:S(2)}, u32[]{:S(2)}) collective-permute-start(bf16[768,512]{1,0:T(8,128)(2,1)} %tie.4.far_z), channel_id=1, source_target_pairs={{0,1},{1,0},{2,3},{3,2},{4,5},{5,4},{6,7},{7,6},{8,9},{9,8},{10,11... | collective-permute-start | bytes 2359304 | tf_op jit(solution)/shard_map/ppermute | solution.py:367
  67.0 12.3 %collective-permute-start.8 = (bf16[768,512]{1,0:T(8,128)(2,1)S(1)}, bf16[768,512]{1,0:T(8,128)(2,1)}, u32[]{:S(2)}, u32[]{:S(2)}) collective-permute-start(bf16[768,512]{1,0:T(8,128)(2,1)S(1)} %tie.3.near_z), channel_id=1, source_target_pairs={{0,1},{1,0},{2,3},{3,2},{4,5},{5,4},{6,7},{7,6},{8,9},{9,8},{10,11... | collective-permute-start | bytes 2359304 | tf_op jit(solution)/shard_map/ppermute | solution.py:367
  70.1 17.2 %collective-permute-start.9 = (f32[768,128]{1,0:T(8,128)S(1)}, f32[768,128]{1,0:T(8,128)S(1)}, u32[]{:S(2)}, u32[]{:S(2)}) collective-permute-start(f32[768,128]{1,0:T(8,128)S(1)} %add.15.refs_2_.refs_0_), channel_id=1, source_target_pairs={{0,384},{128,256},{256,128},{384,0},{1,385},{129,257},{257,129},{3... | collective-permute-start | bytes 1179656 | tf_op jit(solution)/shard_map/ppermute | solution.py:416
  74.9 12.5 %all-to-all-start.2 = ((f32[8,32,128]{2,1,0:T(8,128)}), f32[8,32,128]{2,1,0:T(8,128)S(1)}, u32[]{:S(2)}, u32[]{:S(2)}) async-start(f32[8,32,128]{2,1,0:T(8,128)} %reduce.1), calls=%async_computation.2 | async-start | bytes 262144 | tf_op jit(solution)/shard_map/all_to_all | solution.py:374
  79.4 0.7 copy-start.5
  80.1 0.7 copy-start.8
  80.8 0.7 copy-start.13
  87.3 15.0 %copy-start.6 = (s32[4]{0:T(128)S(1)}, s32[4]{0:T(128)}, u32[]{:S(2)}) copy-start(s32[4]{0:T(128)} %copy-done.4) | copy-start | bytes 52

commit v3 on v1

v3 whole, which is shorter than its diff:
```python
import functools

import jax
import jax.numpy as jnp
from jax import lax
from jax.experimental import pallas as pl
from jax.experimental.pallas import tpu as pltpu
from jax.sharding import Mesh
from jax.sharding import PartitionSpec as P

CLU = ("clu_0", "clu_1", "clu_2")
PAD = 16
F32 = jnp.float32
BF16 = jnp.bfloat16
VMEM = pl.BlockSpec(memory_space=pltpu.VMEM)
SMEM = pl.BlockSpec(memory_space=pltpu.SMEM)
ANY = pl.BlockSpec(memory_space=pl.ANY)
HBM = pl.BlockSpec(memory_space=pltpu.MemorySpace.HBM)


def params(mib):
    return pltpu.CompilerParams(vmem_limit_bytes=mib * 2**20)


def iota(shape, dim):
    return lax.broadcasted_iota(jnp.int32, shape, dim)


def dot(a, b):
    return jnp.dot(a, b, preferred_element_type=F32)


def as_column(row):
    size = row.shape[1]
    square = (size, size)
    spread = jnp.where(iota(square, 0) == iota(square, 1), jnp.broadcast_to(row, square), 0.0)
    return jnp.sum(spread, axis=1, keepdims=True)


def count_before(mask):
    size = mask.shape[1]
    square = (size, size)
    upto = (iota(square, 0) <= iota(square, 1)).astype(F32).astype(BF16)
    rows = jnp.broadcast_to(mask, (16, size)).astype(BF16)
    return dot(rows, upto)[:1] - 1.0


def chosen(column, width):
    shape = (column.shape[0], width)
    return (jnp.broadcast_to(column, shape) == iota(shape, 1).astype(F32)).astype(F32).astype(BF16)


def rows_of(v, width):
    return [v[:, i : i + width] for i in range(0, v.shape[1], width)]


def stacked(lines, width):
    at = iota((PAD, width), 0)
    out = jnp.zeros((PAD, width), F32)
    for i, v in enumerate(lines):
        if v.shape[1] < width:
            v = jnp.concatenate([v, jnp.zeros((1, width - v.shape[1]), F32)], axis=1)
        out = jnp.where(at == i, v, out)
    return out.astype(BF16)


def halo_kernel(clusters, sc, order, forces, halo_ref, lines_ref, order_ref, sems):
    rows, columns = forces.shape
    size = order.shape[1]
    part = halo_ref.shape[1]
    start = pl.multiple_of(sc[1] * part, part)
    copies = [
        pltpu.make_async_copy(order, order_ref, sems.at[0]),
        pltpu.make_async_copy(forces.at[:, pl.ds(start, part)], halo_ref.at[pl.ds(0, rows)], sems.at[1]),
    ]
    for copy in copies:
        copy.start()
    copies[0].wait()
    rel = order_ref[...] - (sc[3] - 1) * size
    rel = jnp.where(rel < 0, rel + clusters * size, rel)
    rel = jnp.where(rel >= clusters * size, rel - clusters * size, rel)
    high = (rel >= size).astype(jnp.int32) + (rel >= 2 * size).astype(jnp.int32)
    low = (rel - high * size).astype(F32)
    high = high.astype(F32)
    lines_ref[...] = stacked([low, high], columns)
    halo_ref[rows:] = stacked(rows_of(low, part) + rows_of(high, part), part)
    copies[1].wait()


def block_kernel(lines_ref, forces, block, sems):
    rows = forces.shape[0]
    copies = [
        pltpu.make_async_copy(forces, block.at[pl.ds(0, rows)], sems.at[0]),
        pltpu.make_async_copy(lines_ref, block.at[pl.ds(rows, PAD)], sems.at[1]),
    ]
    for copy in copies:
        copy.start()
    for copy in copies:
        copy.wait()


def pieces_kernel(sc, halo_ref, own_ref, pair_ref, bases_ref, keep_ref, send_ref, thin, thin_ref, sem):
    levels, comps, rank, size = bases_ref.shape
    rows = comps * size
    part = halo_ref.shape[1]
    quarter = size // 4
    core = sc[0]
    start = pl.multiple_of(sc[1] * part, part)
    tail = own_ref[rows:].astype(F32)
    low, high = tail[0:1, :size], tail[1:2, :size]
    seat = jnp.where(core == 0, high, 2.0 - high)
    pick = chosen(as_column(seat * size + low), 3 * size)
    sums = [jnp.zeros((rank, part), F32) for _ in range(levels)]
    for comp in range(comps):
        span = slice(comp * size, (comp + 1) * size)
        got = dot(pick[:, :size], halo_ref[span])
        got += dot(pick[:, size : 2 * size], own_ref[span, pl.ds(start, part)])
        got += dot(pick[:, 2 * size :], pair_ref[span, pl.ds(start, part)])
        got = got.astype(BF16)
        for level in range(levels):
            sums[level] += dot(bases_ref[level, comp], got)
    keep_ref[...] = jnp.where(core == 0, sums[0], sums[1])
    send_ref[...] = jnp.where(core == 0, sums[1], sums[0])
    tail = halo_ref[rows:].astype(F32)
    per = size // part
    low = jnp.concatenate([tail[i : i + 1] for i in range(per)], axis=1)
    high = jnp.concatenate([tail[per + i : per + i + 1] for i in range(per)], axis=1)
    mine = high == jnp.where(core == 0, 2.0, 0.0)
    place = count_before(mine.astype(F32))
    shape = (quarter, size)
    seats = jnp.broadcast_to(jnp.where(mine, place, -1.0), shape)
    into = (seats == iota(shape, 0).astype(F32)).astype(F32).astype(BF16)
    pack = dot(into, chosen(as_column(low), size)).astype(BF16)
    for comp in range(comps):
        thin_ref[comp] = dot(pack, own_ref[comp * size : (comp + 1) * size]).astype(BF16)
    copy = pltpu.make_async_copy(thin_ref, thin, sem.at[0])
    copy.start()
    copy.wait()


def near_kernel(
    clusters, planes, sc, near_col, target, keeps, scale, coupling, tiles,
    own, thin, near_z, pair_far, pair, far_z, pair_near,
    total_ref, high_ref, low_ref,
    col_ref, target_ref, keep_ref, scale_ref, coupling_ref, tile_ref, window, blocks,
    sems, tile_sems, small_sems,
):
    count, rows, _ = tiles.shape
    columns = own.shape[1]
    size = rows // 3
    quarter = size // 4
    core = sc[0]
    pairs = (
        (near_col, col_ref), (target, target_ref), (keeps, keep_ref), (scale, scale_ref),
        (coupling, coupling_ref),
    )
    smalls = [pltpu.make_async_copy(a, b, small_sems.at[i]) for i, (a, b) in enumerate(pairs)]
    for copy in smalls:
        copy.start()
    seats = (thin, near_z, pair_far, own, pair, far_z, pair_near)
    for j in range(count):
        pltpu.make_async_copy(tiles.at[j], tile_ref.at[j], tile_sems.at[j]).start()
    smalls[0].wait()
    offs = []
    for j in range(count):
        off = col_ref[0, j] - sc[3] + 2
        off = jnp.where(off < 0, off + clusters, off)
        off = jnp.where(off >= clusters, off - clusters, off) - 2
        offs.append(jnp.where(core == 0, off, -off))
    for j in range(count):
        for o in range(-2, 3):

            @pl.when(offs[j] == o)
            def _(j=j, o=o):
                for w in range(3):
                    source = seats[o + 2 + w]
                    if o + w == -2:
                        for comp in range(3):
                            pltpu.make_async_copy(
                                source.at[comp],
                                window.at[j, w, pl.ds(comp * size, quarter)],
                                sems.at[j, w, comp],
                            ).start()
                            window[j, w, comp * size + quarter : (comp + 1) * size] = jnp.zeros(
                                (size - quarter, columns), BF16
                            )
                    else:
                        pltpu.make_async_copy(source, window.at[j, w], sems.at[j, w, 0]).start()

    for copy in smalls[1:]:
        copy.wait()
    far_count, rank, _ = coupling_ref.shape
    width = high_ref.shape[1]
    lane = iota((rank, width), 1)
    for b in range(far_count):
        goal = target_ref[0, b]
        start = jnp.where(goal < 2, 0, lax.rem(goal - 2 - sc[2] + planes, planes)) * rank
        tile = coupling_ref[b].astype(F32) * scale_ref[0, b]
        tile = jnp.concatenate([tile] * (width // rank), axis=1)
        tile = jnp.where((lane >= start) & (lane < start + keep_ref[0, b]), tile, 0.0)
        high = tile.astype(BF16)
        high_ref[b * rank : (b + 1) * rank] = high
        low_ref[b * rank : (b + 1) * rank] = (tile - high.astype(F32)).astype(BF16)

    for j in range(count):
        edge = offs[j] == -2
        for w in range(1, 3):
            pltpu.make_async_copy(own, window.at[j, w], sems.at[j, w, 0]).wait()

        @pl.when(edge)
        def _(j=j):
            for comp in range(3):
                pltpu.make_async_copy(
                    thin.at[comp], window.at[j, 0, pl.ds(comp * size, quarter)], sems.at[j, 0, comp]
                ).wait()

        @pl.when(jnp.logical_not(edge))
        def _(j=j):
            pltpu.make_async_copy(own, window.at[j, 0], sems.at[j, 0, 0]).wait()

        tail = window[j, 1, rows:].astype(F32)
        low, high = tail[0:1, :size], tail[1:2, :size]
        seat = jnp.where(core == 0, high, 2.0 - high)
        first = seat == 0.0
        place = count_before(first.astype(F32))
        low = jnp.where(jnp.logical_and(first, edge), place, low)
        pick = chosen(as_column(seat * size + low), 3 * size)
        for comp in range(3):
            span = slice(comp * size, (comp + 1) * size)
            got = dot(pick[:, :size], window[j, 0, span])
            for w in range(1, 3):
                got += dot(pick[:, w * size : (w + 1) * size], window[j, w, span])
            blocks[j, span] = got.astype(BF16)
    for j in range(count):
        pltpu.make_async_copy(tiles.at[j], tile_ref.at[j], tile_sems.at[j]).wait()
    for r in range(3):
        span = slice(r * size, (r + 1) * size)
        total = dot(tile_ref[0, span], blocks[0])
        for j in range(1, count):
            total += dot(tile_ref[j, span], blocks[j])
        total_ref[span] = total


def reduce_kernel(many_ref, sums, sums_ref, sem):
    total = many_ref[0]
    for i in range(1, many_ref.shape[0]):
        total += many_ref[i]
    for i in range(sums_ref.shape[0]):
        sums_ref[i] = total
    copy = pltpu.make_async_copy(sums_ref, sums, sem.at[0])
    copy.start()
    copy.wait()


def mix_kernel(
    planes, sc, near, sums, basis, high_ref, low_ref, split,
    near_ref, sums_ref, basis_ref, table_ref, coupled_ref, result, in_sems, sems,
):
    pairs = ((sums, sums_ref), (basis, basis_ref), (near, near_ref))
    copies = [pltpu.make_async_copy(a, b, in_sems.at[i]) for i, (a, b) in enumerate(pairs)]
    for copy in copies:
        copy.start()
    copies[0].wait()
    groups, rows, part = split.shape
    rank = sums_ref.shape[1]
    plane = sc[2]
    half = planes // 2
    other = jnp.where(plane < half, half, 0)
    for y in range(groups):
        lanes = slice(y * part, (y + 1) * part)
        base = y * 2 * planes
        coarse = sums_ref[base + 2 * other]
        for i in range(1, half):
            coarse += sums_ref[base + 2 * (other + i)]
        table_ref[:rank, lanes] = coarse
        for i in range(1, planes):
            at = lax.rem(plane + i, planes)
            table_ref[i * rank : (i + 1) * rank, lanes] = sums_ref[base + 2 * at + 1]
    table = table_ref[...]
    high = table.astype(BF16)
    low = (table - high.astype(F32)).astype(BF16)
    step = high_ref.shape[0] // 2
    for i in range(2):
        span = slice(i * step, (i + 1) * step)
        coupled = dot(high_ref[span], high) + dot(high_ref[span], low) + dot(low_ref[span], high)
        coupled_ref[span] = coupled.astype(BF16)
    copies[1].wait()
    copies[2].wait()
    outs = []
    size = rows // 3
    for r in range(3):
        span = slice(r * size, (r + 1) * size)
        total = near_ref[span] + lax.dot_general(
            basis_ref[:, span], coupled_ref[...], (((0,), (0,)), ((), ())), preferred_element_type=F32
        )
        for i in range(groups):
            result[i, span] = total[:, i * part : (i + 1) * part].astype(BF16)
        here = pl.ds(r * size, size)
        outs.append(pltpu.make_async_copy(result.at[:, here], split.at[:, here], sems.at[r]))
        outs[-1].start()
    for copy in outs:
        copy.wait()


def last_kernel(arrived_ref, out_ref):
    total = arrived_ref[0].astype(F32)
    for i in range(1, arrived_ref.shape[0]):
        total += arrived_ref[i].astype(F32)
    out_ref[...] = total


def tie_kernel(*refs):
    del refs


def tied(value, *after):
    return pl.pallas_call(
        tie_kernel,
        out_shape=shape_of(value.shape, value.dtype),
        in_specs=[ANY] * (1 + len(after)),
        out_specs=ANY,
        input_output_aliases={0: 0},
        compiler_params=params(1),
        name="tie",
    )(value, *after)


def in_hbm(*values):
    return [pltpu.with_memory_space_constraint(v, pltpu.MemorySpace.HBM) for v in values]


def shape_of(dims, dtype):
    return jax.ShapeDtypeStruct(dims, dtype)


def on_device(
    forces, order, bases, near_tiles, near_col, far_basis, far_coupling, far_scale, far_rank, far_target
):
    clusters = lax.axis_size(CLU)
    planes = lax.axis_size("clu_0")
    steps = lax.axis_size("clu_1")
    groups = lax.axis_size("grp")
    size = order.shape[0]
    comps, _, columns = forces.shape
    rows = comps * size
    part = columns // groups
    _, rank = bases.shape[:2]
    count = near_tiles.shape[1]
    far_count = far_target.shape[1]
    width = planes * rank
    sc = jnp.stack(
        [lax.axis_index("clu_2"), lax.axis_index("grp"), lax.axis_index("clu_0"), lax.axis_index(CLU)]
    ).astype(jnp.int32)

    def swapped(v):
        return lax.ppermute(v, "clu_2", [(0, 1), (1, 0)])

    def sent(v, by):
        pairs = [(i, (i + by if i % 2 else i - by) % clusters) for i in range(clusters)]
        return lax.ppermute(v, CLU, pairs)

    def exchanged(v, axis):
        return lax.all_to_all(v, axis, split_axis=0, concat_axis=0, tiled=True)

    chain = forces.reshape(rows, columns)
    halo, lines = pl.pallas_call(
        functools.partial(halo_kernel, clusters),
        out_shape=(shape_of((rows + PAD, part), BF16), shape_of((PAD, columns), BF16)),
        in_specs=[SMEM, HBM, HBM],
        out_specs=(VMEM, VMEM),
        scratch_shapes=[pltpu.VMEM((1, size), jnp.int32), pltpu.SemaphoreType.DMA((2,))],
        compiler_params=params(4),
        name="halo",
    )(sc, *in_hbm(order.reshape(1, size), chain))
    halo = sent(halo, 1)
    block = pl.pallas_call(
        block_kernel,
        out_shape=shape_of((rows + PAD, columns), BF16),
        in_specs=[VMEM, HBM],
        out_specs=HBM,
        scratch_shapes=[pltpu.SemaphoreType.DMA((2,))],
        compiler_params=params(4),
        name="block",
    )(lines, *in_hbm(chain))
    pair = swapped(block)
    near_z = sent(block, -2)
    far_z = sent(block, 2)

    keep, send, thin = pl.pallas_call(
        pieces_kernel,
        out_shape=(
            shape_of((rank, part), F32),
            shape_of((rank, part), F32),
            shape_of((comps, size // 4, columns), BF16),
        ),
        in_specs=[SMEM, VMEM, VMEM, VMEM, VMEM],
        out_specs=(VMEM, VMEM, HBM),
        scratch_shapes=[
            pltpu.VMEM((comps, size // 4, columns), BF16),
            pltpu.SemaphoreType.DMA((1,)),
        ],
        compiler_params=params(12),
        name="pieces",
    )(sc, halo, block, pair, bases.transpose(0, 2, 1, 3))
    level_sum = keep + swapped(send)
    many = exchanged(jnp.broadcast_to(level_sum, (steps, rank, part)), "clu_1")
    thin = sent(thin, 3)
    many = tied(many, near_z, far_z, *in_hbm(thin))
    pair_near = swapped(near_z)
    pair_far = swapped(far_z)
    fan = groups * 2 * planes
    sums = pl.pallas_call(
        reduce_kernel,
        out_shape=shape_of((fan, rank, part), F32),
        in_specs=[VMEM],
        out_specs=HBM,
        scratch_shapes=[pltpu.VMEM((fan, rank, part), F32), pltpu.SemaphoreType.DMA((1,))],
        compiler_params=params(58),
        name="reduce",
    )(many)
    sums = exchanged(sums, ("grp", "clu_0", "clu_2"))
    near, high, low = pl.pallas_call(
        functools.partial(near_kernel, clusters, planes),
        out_shape=(shape_of((rows, columns), F32),) + (shape_of((far_count * rank, width), BF16),) * 2,
        in_specs=[SMEM] + [HBM] * 6 + [ANY] * 7,
        out_specs=(VMEM, VMEM, VMEM),
        scratch_shapes=[
            pltpu.SMEM((1, count), jnp.int32),
            pltpu.SMEM((1, far_count), jnp.int32),
            pltpu.SMEM((1, far_count), jnp.int32),
            pltpu.SMEM((1, far_count), F32),
            pltpu.VMEM((far_count, rank, rank), BF16),
            pltpu.VMEM((count, rows, rows), BF16),
            pltpu.VMEM((count, 3, rows + PAD, columns), BF16),
            pltpu.VMEM((count, rows, columns), BF16),
            pltpu.SemaphoreType.DMA((count, 3, 3)),
            pltpu.SemaphoreType.DMA((count,)),
            pltpu.SemaphoreType.DMA((5,)),
        ],
        compiler_params=params(48),
        name="near",
    )(
        sc, *in_hbm(near_col, far_target, far_rank, far_scale, far_coupling[0], near_tiles[0]),
        block, *in_hbm(thin), near_z, pair_far, pair, far_z, pair_near,
    )
    split = pl.pallas_call(
        functools.partial(mix_kernel, planes),
        out_shape=shape_of((groups, rows, part), BF16),
        in_specs=[SMEM, HBM, HBM, HBM, VMEM, VMEM],
        out_specs=HBM,
        scratch_shapes=[
            pltpu.VMEM((rows, columns), F32),
            pltpu.VMEM((fan, rank, part), F32),
            pltpu.VMEM((far_count * rank, rows), BF16),
            pltpu.VMEM((width, columns), F32),
            pltpu.VMEM((far_count * rank, columns), BF16),
            pltpu.VMEM((groups, rows, part), BF16),
            pltpu.SemaphoreType.DMA((3,)),
            pltpu.SemaphoreType.DMA((3,)),
        ],
        compiler_params=params(16),
        name="mix",
    )(sc, *in_hbm(near, sums, far_basis.reshape(far_count * rank, rows)), high, low)
    arrived = exchanged(split, "grp")
    velocity = pl.pallas_call(
        last_kernel,
        out_shape=shape_of((rows, part), F32),
        in_specs=[VMEM],
        out_specs=VMEM,
        compiler_params=params(4),
        name="last",
    )(arrived)
    return velocity.reshape(comps, size, part)


def solution(mesh):
    clusters = mesh.shape["clu"]
    torus = Mesh(
        mesh.devices.reshape(mesh.shape["grp"], 4, clusters // 8, 2),
        ("grp", "clu_0", "clu_1", "clu_2"),
    )
    in_specs = (
        P(None, CLU, None),
        P(CLU),
        P(None, None, None, CLU),
        P(CLU, "grp", None, None),
        P(CLU, "grp"),
        P(CLU, "grp", None, None),
        P(CLU, "grp", None, None),
        P(CLU, "grp"),
        P(CLU, "grp"),
        P(CLU, "grp"),
    )
    return jax.shard_map(
        on_device, mesh=torus, in_specs=in_specs, out_specs=P(None, CLU, "grp"), check_vma=False
    )
```

time: 113 us -> 104 us (0.920)
  the two profiles are of different devices: /device:TPU:34 before, /device:TPU:32 now
where the time goes in v3:
time: 104 us; the launch traced here: 103 us
  starting transfers between devices  56.8 us (55%)
  Pallas kernels  17.6 us (17%)
  blocking collectives  15.2 us (15%)
  waiting for transfers between devices  11.8 us (11%)
  local copies, waits for them, and re-layouts  1.44 us (1%)
    ppermute x4, starting transfers between devices, sent(): return lax.ppermute(v, CLU, pairs)  36.9 us
    all_to_all x1, blocking collectives, exchanged(): return lax.all_to_all(v, axis, split_axis=0, concat_axis=0, tiled=True)  15.2 us
    all_to_all x2, starting transfers between devices, exchanged(): return lax.all_to_all(v, axis, split_axis=0, concat_axis=0, tiled=True)  11.8 us
    ppermute x4, starting transfers between devices, swapped(): return lax.ppermute(v, 'clu_2', [(0, 1), (1, 0)])  8.17 us
    pallas_call x1, Pallas kernels, on_device(): pl.pallas_call(functools.partial(near_kernel, clusters, planes), out_shap...  6.85 us
    ppermute x4, waiting for transfers between devices, sent(): return lax.ppermute(v, CLU, pairs)  5.77 us
    all_to_all x2, waiting for transfers between devices, exchanged(): return lax.all_to_all(v, axis, split_axis=0, concat_axis=0, tiled=True)  4.86 us
    pallas_call x1, Pallas kernels, on_device(): pl.pallas_call(functools.partial(mix_kernel, planes), out_shape=shape_of(...  3.44 us
  transfers between devices with their start and end apart: 10, of which 3 were waited for; matrix products, arithmetic and copies ran while one was open for 1% of the time, Pallas kernels for 10%

profile of v3, /device:TPU:32, one launch (start us, length us, event | category | flops | bytes accessed | tf_op | source)
XLA Modules:
  0.0 103.1 jit_solution(7015004723546653553)
XLA Ops:
  0.0 0.0 copy-start.1
  0.0 0.1 pad_add_fusion.sc
  0.1 1.5 %halo.1 = (bf16[784,128]{1,0:T(8,128)(2,1)S(1)}, bf16[16,512]{1,0:T(8,128)(2,1)S(1)}) custom-call(s32[4]{0:T(128)S(1)} %pad_add_fusion.sc, s32[1,256]{1,0:T(1,128)} %bitcast.17, bf16[768,512]{1,0:T(8,128)(2,1)} %bitcast.12), custom_call_target="tpu_custom_call" | custom-call | tf_op jit(solution)/shard_map/halo/pallas_call | solution.py:366
  1.6 1.2 %block.1.own_ref.own = bf16[784,512]{1,0:T(8,128)(2,1)S(1)} custom-call(bf16[16,512]{1,0:T(8,128)(2,1)S(1)} %get-tuple-element.13.lines_ref, bf16[768,512]{1,0:T(8,128)(2,1)} %bitcast.13), custom_call_target="tpu_custom_call" | custom-call | tf_op jit(solution)/shard_map/block/pallas_call | solution.py:376
  2.8 1.9 %collective-permute-start.1 = (bf16[784,512]{1,0:T(8,128)(2,1)S(1)}, bf16[784,512]{1,0:T(8,128)(2,1)S(1)}, u32[]{:S(2)}, u32[]{:S(2)}) collective-permute-start(bf16[784,512]{1,0:T(8,128)(2,1)S(1)} %block.1.own_ref.own), channel_id=1, source_target_pairs={{0,1},{1,0},{2,3},{3,2},{4,5},{5,4},{6,7},{7,6},{8,9},{9,8},{10,11... | collective-permute-start | bytes 2408456 | tf_op jit(solution)/shard_map/ppermute | solution.py:356
  4.7 7.5 %collective-permute-start = (bf16[784,128]{1,0:T(8,128)(2,1)S(1)}, bf16[784,128]{1,0:T(8,128)(2,1)S(1)}, u32[]{:S(2)}, u32[]{:S(2)}) collective-permute-start(bf16[784,128]{1,0:T(8,128)(2,1)S(1)} %get-tuple-element.14), channel_id=1, source_target_pairs={{0,127},{1,2},{2,1},{3,4},{4,3},{5,6},{6,5},{7,8},{8,7},{9,10},{10... | collective-permute-start | bytes 602120 | tf_op jit(solution)/shard_map/ppermute | solution.py:360
  12.2 8.2 %collective-permute-start.4 = (bf16[784,512]{1,0:T(8,128)(2,1)S(1)}, bf16[784,512]{1,0:T(8,128)(2,1)S(1)}, u32[]{:S(2)}, u32[]{:S(2)}) collective-permute-start(bf16[784,512]{1,0:T(8,128)(2,1)S(1)} %block.1.own_ref.own), channel_id=1, source_target_pairs={{0,126},{1,3},{2,0},{3,5},{4,2},{5,7},{6,4},{7,9},{8,6},{9,11},{10... | collective-permute-start | bytes 2408456 | tf_op jit(solution)/shard_map/ppermute | solution.py:360
  20.4 1.9 %collective-permute-start.3 = (bf16[784,512]{1,0:T(8,128)(2,1)S(1)}, bf16[784,512]{1,0:T(8,128)(2,1)S(1)}, u32[]{:S(2)}, u32[]{:S(2)}) collective-permute-start(bf16[784,512]{1,0:T(8,128)(2,1)S(1)} %block.1.own_ref.own), channel_id=1, source_target_pairs={{0,2},{1,127},{2,4},{3,1},{4,6},{5,3},{6,8},{7,5},{8,10},{9,7},{10... | collective-permute-start | bytes 2408456 | tf_op jit(solution)/shard_map/ppermute | solution.py:360
  22.3 0.0 collective-permute-done.halo_ref
  22.4 0.0 collective-permute-done.1.pair_ref.pair
  22.4 0.0 copy-done.1
  22.4 2.0 %pieces.1 = (f32[32,128]{1,0:T(8,128)S(1)}, f32[32,128]{1,0:T(8,128)S(1)}, bf16[3,64,512]{2,1,0:T(8,128)(2,1)S(1)}) custom-call(s32[4]{0:T(128)S(1)} %pad_add_fusion.sc, bf16[784,128]{1,0:T(8,128)(2,1)S(1)} %collective-permute-done.halo_ref, bf16[784,512]{1,0:T(8,128)(2,1)S(1)} %block.1.own_ref.own, ...), custom_call_target="tpu_custom_call" | custom-call | tf_op jit(solution)/shard_map/pieces/pallas_call | solution.py:389
  24.4 0.0 copy-start.2
  24.4 1.9 %collective-permute-start.7 = (f32[32,128]{1,0:T(8,128)S(1)}, f32[32,128]{1,0:T(8,128)S(1)}, u32[]{:S(2)}, u32[]{:S(2)}) collective-permute-start(f32[32,128]{1,0:T(8,128)S(1)} %get-tuple-element.18), channel_id=1, source_target_pairs={{0,1},{1,0},{2,3},{3,2},{4,5},{5,4},{6,7},{7,6},{8,9},{9,8},{10,11... | collective-permute-start | bytes 49160 | tf_op jit(solution)/shard_map/ppermute | solution.py:356
  26.3 1.1 %collective-permute-done.7 = f32[32,128]{1,0:T(8,128)S(1)} collective-permute-done((f32[32,128]{1,0:T(8,128)S(1)}, f32[32,128]{1,0:T(8,128)S(1)}, u32[]{:S(2)}, u32[]{:S(2)}) %collective-permute-start.7) | collective-permute-done | bytes 16416 | tf_op jit(solution)/shard_map/ppermute | solution.py:356
  27.5 0.0 copy-done.2
  27.5 0.7 broadcast_in_dim.3
  28.2 6.8 %all-to-all-start = ((f32[16,32,128]{2,1,0:T(8,128)}), f32[16,32,128]{2,1,0:T(8,128)S(1)}, u32[]{:S(2)}, u32[]{:S(2)}) async-start(f32[16,32,128]{2,1,0:T(8,128)} %broadcast_in_dim.3), calls=%async_computation | async-start | bytes 524288 | tf_op jit(solution)/shard_map/all_to_all | solution.py:363
  35.0 0.0 collective-permute-done.4.far_z.refs_2_
  35.0 1.9 %collective-permute-start.5 = (bf16[784,512]{1,0:T(8,128)(2,1)S(1)}, bf16[784,512]{1,0:T(8,128)(2,1)}, u32[]{:S(2)}, u32[]{:S(2)}) collective-permute-start(bf16[784,512]{1,0:T(8,128)(2,1)S(1)} %collective-permute-done.4.far_z.refs_2_), channel_id=1, source_target_pairs={{0,1},{1,0},{2,3},{3,2},{4,5},{5,4},{6,7},{7,6},{8,9},{9,8},{10,11... | collective-permute-start | bytes 2408456 | tf_op jit(solution)/shard_map/ppermute | solution.py:356
  36.9 0.0 collective-permute-done.3.near_z.refs_1_
  36.9 2.4 %collective-permute-start.6 = (bf16[784,512]{1,0:T(8,128)(2,1)S(1)}, bf16[784,512]{1,0:T(8,128)(2,1)}, u32[]{:S(2)}, u32[]{:S(2)}) collective-permute-start(bf16[784,512]{1,0:T(8,128)(2,1)S(1)} %collective-permute-done.3.near_z.refs_1_), channel_id=1, source_target_pairs={{0,1},{1,0},{2,3},{3,2},{4,5},{5,4},{6,7},{7,6},{8,9},{9,8},{10,11... | collective-permute-start | bytes 2408456 | tf_op jit(solution)/shard_map/ppermute | solution.py:356
  39.4 19.2 %collective-permute-start.2 = (bf16[3,64,512]{2,1,0:T(8,128)(2,1)}, bf16[3,64,512]{2,1,0:T(8,128)(2,1)}, u32[]{:S(2)}, u32[]{:S(2)}) collective-permute-start(bf16[3,64,512]{2,1,0:T(8,128)(2,1)} %copy-done.2), channel_id=1, source_target_pairs={{0,125},{1,4},{2,127},{3,6},{4,1},{5,8},{6,3},{7,10},{8,5},{9,12},... | collective-permute-start | bytes 589832 | tf_op jit(solution)/shard_map/ppermute | solution.py:360
  58.6 5.8 %collective-permute-done.2.thin.refs_3_ = bf16[3,64,512]{2,1,0:T(8,128)(2,1)} collective-permute-done((bf16[3,64,512]{2,1,0:T(8,128)(2,1)}, bf16[3,64,512]{2,1,0:T(8,128)(2,1)}, u32[]{:S(2)}, u32[]{:S(2)}) %collective-permute-start.2) | collective-permute-done | bytes 196640 | tf_op jit(solution)/shard_map/ppermute | solution.py:360
  64.4 0.0 all-to-all-done.refs_0_
  64.4 0.0 copy-start
  64.4 0.7 copy-done
  65.1 1.8 %reduce.1 = f32[32,32,128]{2,1,0:T(8,128)} custom-call(f32[16,32,128]{2,1,0:T(8,128)} %copy-done), custom_call_target="tpu_custom_call" | custom-call | tf_op jit(solution)/shard_map/reduce/pallas_call | solution.py:412
  66.9 5.0 %all-to-all-start.1 = ((f32[32,32,128]{2,1,0:T(8,128)}), f32[32,32,128]{2,1,0:T(8,128)}, u32[]{:S(2)}, u32[]{:S(2)}) async-start(f32[32,32,128]{2,1,0:T(8,128)} %reduce.1), calls=%async_computation.1 | async-start | bytes 1048576 | tf_op jit(solution)/shard_map/all_to_all | solution.py:363
  71.9 0.0 collective-permute-done.5.pair_far
  71.9 0.0 collective-permute-done.6.pair_near
  71.9 6.9 %near.1 = (f32[768,512]{1,0:T(8,128)}, bf16[512,128]{1,0:T(8,128)(2,1)S(1)}, bf16[512,128]{1,0:T(8,128)(2,1)S(1)}) custom-call(s32[4]{0:T(128)S(1)} %pad_add_fusion.sc, s32[1,2]{1,0:T(1,128)} %near_col.1, s32[1,16]{1,0:T(1,128)} %target.1, s32[1,16]{1,0:T(1,128)} %keeps.1, f32[1,16]{1,0:T(1,128)} %scale.1, bf16[16,32,32]{2,1,0:T(8,128)(2,1)} %bitcast.16, ...), custom_call_target="tpu_custom_call" | custom-call | tf_op jit(solution)/shard_map/near/pallas_call | solution.py:422
  78.8 4.9 %all-to-all-done.1.sums = f32[32,32,128]{2,1,0:T(8,128)} async-done(((f32[32,32,128]{2,1,0:T(8,128)}), f32[32,32,128]{2,1,0:T(8,128)}, u32[]{:S(2)}, u32[]{:S(2)}) %all-to-all-start.1) | async-done | bytes 524320 | tf_op jit(solution)/shard_map/all_to_all | solution.py:363
  83.7 3.4 %mix.1 = bf16[4,768,128]{2,1,0:T(8,128)(2,1)S(1)} custom-call(s32[4]{0:T(128)S(1)} %pad_add_fusion.sc, f32[768,512]{1,0:T(8,128)} %get-tuple-element.16.near, f32[32,32,128]{2,1,0:T(8,128)} %all-to-all-done.1.sums, bf16[512,768]{1,0:T(8,128)(2,1)} %bitcast.15, bf16[512,128]{1,0:T(8,128)(2,1)S(1)} %get-tuple-element.19.high_ref, ...), custom_call_target="tpu_custom_call" | custom-call | tf_op jit(solution)/shard_map/mix/pallas_call | solution.py:446
  87.1 15.2 %all_to_all.15.arrived_ref = bf16[4,768,128]{2,1,0:T(8,128)(2,1)S(1)} all-to-all(bf16[4,768,128]{2,1,0:T(8,128)(2,1)S(1)} %mix.1), channel_id=1, replica_groups=mesh['grp'=4,'clu_0'=4,'clu_1'=16,'clu_2'=2] {'grp'}, dimensions={0} | all-to-all | bytes 1572864 | tf_op jit(solution)/shard_map/all_to_all | solution.py:363
  102.3 0.8 last.1
  (2 shorter events, 0.0 us)
Async XLA Ops:
  0.0 22.4 %copy-start.1 = (bf16[2,32,3,256]{3,1,2,0:T(8,128)(2,1)S(1)}, bf16[2,32,3,256]{3,1,2,0:T(8,128)(2,1)}, u32[]{:S(2)}) copy-start(bf16[2,32,3,256]{3,1,2,0:T(8,128)(2,1)} %param.12) | copy-start | bytes 294916
  2.8 19.6 %collective-permute-start.1 = (bf16[784,512]{1,0:T(8,128)(2,1)S(1)}, bf16[784,512]{1,0:T(8,128)(2,1)S(1)}, u32[]{:S(2)}, u32[]{:S(2)}) collective-permute-start(bf16[784,512]{1,0:T(8,128)(2,1)S(1)} %block.1.own_ref.own), channel_id=1, source_target_pairs={{0,1},{1,0},{2,3},{3,2},{4,5},{5,4},{6,7},{7,6},{8,9},{9,8},{10,11... | collective-permute-start | bytes 2408456 | tf_op jit(solution)/shard_map/ppermute | solution.py:356
  4.7 17.7 %collective-permute-start = (bf16[784,128]{1,0:T(8,128)(2,1)S(1)}, bf16[784,128]{1,0:T(8,128)(2,1)S(1)}, u32[]{:S(2)}, u32[]{:S(2)}) collective-permute-start(bf16[784,128]{1,0:T(8,128)(2,1)S(1)} %get-tuple-element.14), channel_id=1, source_target_pairs={{0,127},{1,2},{2,1},{3,4},{4,3},{5,6},{6,5},{7,8},{8,7},{9,10},{10... | collective-permute-start | bytes 602120 | tf_op jit(solution)/shard_map/ppermute | solution.py:360
  12.2 22.8 %collective-permute-start.4 = (bf16[784,512]{1,0:T(8,128)(2,1)S(1)}, bf16[784,512]{1,0:T(8,128)(2,1)S(1)}, u32[]{:S(2)}, u32[]{:S(2)}) collective-permute-start(bf16[784,512]{1,0:T(8,128)(2,1)S(1)} %block.1.own_ref.own), channel_id=1, source_target_pairs={{0,126},{1,3},{2,0},{3,5},{4,2},{5,7},{6,4},{7,9},{8,6},{9,11},{10... | collective-permute-start | bytes 2408456 | tf_op jit(solution)/shard_map/ppermute | solution.py:360
  20.4 16.5 %collective-permute-start.3 = (bf16[784,512]{1,0:T(8,128)(2,1)S(1)}, bf16[784,512]{1,0:T(8,128)(2,1)S(1)}, u32[]{:S(2)}, u32[]{:S(2)}) collective-permute-start(bf16[784,512]{1,0:T(8,128)(2,1)S(1)} %block.1.own_ref.own), channel_id=1, source_target_pairs={{0,2},{1,127},{2,4},{3,1},{4,6},{5,3},{6,8},{7,5},{8,10},{9,7},{10... | collective-permute-start | bytes 2408456 | tf_op jit(solution)/shard_map/ppermute | solution.py:360
  24.4 3.1 %copy-start.2 = (bf16[3,64,512]{2,1,0:T(8,128)(2,1)}, bf16[3,64,512]{2,1,0:T(8,128)(2,1)S(1)}, u32[]{:S(2)}) copy-start(bf16[3,64,512]{2,1,0:T(8,128)(2,1)S(1)} %get-tuple-element.15) | copy-start | bytes 589828
  24.4 3.1 %collective-permute-start.7 = (f32[32,128]{1,0:T(8,128)S(1)}, f32[32,128]{1,0:T(8,128)S(1)}, u32[]{:S(2)}, u32[]{:S(2)}) collective-permute-start(f32[32,128]{1,0:T(8,128)S(1)} %get-tuple-element.18), channel_id=1, source_target_pairs={{0,1},{1,0},{2,3},{3,2},{4,5},{5,4},{6,7},{7,6},{8,9},{9,8},{10,11... | collective-permute-start | bytes 49160 | tf_op jit(solution)/shard_map/ppermute | solution.py:356
  28.2 36.1 %all-to-all-start = ((f32[16,32,128]{2,1,0:T(8,128)}), f32[16,32,128]{2,1,0:T(8,128)S(1)}, u32[]{:S(2)}, u32[]{:S(2)}) async-start(f32[16,32,128]{2,1,0:T(8,128)} %broadcast_in_dim.3), calls=%async_computation | async-start | bytes 524288 | tf_op jit(solution)/shard_map/all_to_all | solution.py:363
  35.0 36.9 %collective-permute-start.5 = (bf16[784,512]{1,0:T(8,128)(2,1)S(1)}, bf16[784,512]{1,0:T(8,128)(2,1)}, u32[]{:S(2)}, u32[]{:S(2)}) collective-permute-start(bf16[784,512]{1,0:T(8,128)(2,1)S(1)} %collective-permute-done.4.far_z.refs_2_), channel_id=1, source_target_pairs={{0,1},{1,0},{2,3},{3,2},{4,5},{5,4},{6,7},{7,6},{8,9},{9,8},{10,11... | collective-permute-start | bytes 2408456 | tf_op jit(solution)/shard_map/ppermute | solution.py:356
  36.9 35.0 %collective-permute-start.6 = (bf16[784,512]{1,0:T(8,128)(2,1)S(1)}, bf16[784,512]{1,0:T(8,128)(2,1)}, u32[]{:S(2)}, u32[]{:S(2)}) collective-permute-start(bf16[784,512]{1,0:T(8,128)(2,1)S(1)} %collective-permute-done.3.near_z.refs_1_), channel_id=1, source_target_pairs={{0,1},{1,0},{2,3},{3,2},{4,5},{5,4},{6,7},{7,6},{8,9},{9,8},{10,11... | collective-permute-start | bytes 2408456 | tf_op jit(solution)/shard_map/ppermute | solution.py:356
  39.4 25.0 %collective-permute-start.2 = (bf16[3,64,512]{2,1,0:T(8,128)(2,1)}, bf16[3,64,512]{2,1,0:T(8,128)(2,1)}, u32[]{:S(2)}, u32[]{:S(2)}) collective-permute-start(bf16[3,64,512]{2,1,0:T(8,128)(2,1)} %copy-done.2), channel_id=1, source_target_pairs={{0,125},{1,4},{2,127},{3,6},{4,1},{5,8},{6,3},{7,10},{8,5},{9,12},... | collective-permute-start | bytes 589832 | tf_op jit(solution)/shard_map/ppermute | solution.py:360
  64.4 0.7 copy-start
  66.9 16.7 %all-to-all-start.1 = ((f32[32,32,128]{2,1,0:T(8,128)}), f32[32,32,128]{2,1,0:T(8,128)}, u32[]{:S(2)}, u32[]{:S(2)}) async-start(f32[32,32,128]{2,1,0:T(8,128)} %reduce.1), calls=%async_computation.1 | async-start | bytes 1048576 | tf_op jit(solution)/shard_map/all_to_all | solution.py:363

commit v4 on v3

--- a/solution.py
+++ b/solution.py
@@ -64,7 +64,7 @@
     return out.astype(BF16)
 
 
-def halo_kernel(clusters, sc, order, forces, halo_ref, lines_ref, order_ref, sems):
+def dress_kernel(clusters, sc, order, forces, halo_ref, block, order_ref, lines_ref, sems):
     rows, columns = forces.shape
     size = order.shape[1]
     part = halo_ref.shape[1]
@@ -72,6 +72,7 @@
     copies = [
         pltpu.make_async_copy(order, order_ref, sems.at[0]),
         pltpu.make_async_copy(forces.at[:, pl.ds(start, part)], halo_ref.at[pl.ds(0, rows)], sems.at[1]),
+        pltpu.make_async_copy(forces, block.at[pl.ds(0, rows)], sems.at[2]),
     ]
     for copy in copies:
         copy.start()
@@ -83,27 +84,18 @@
     low = (rel - high * size).astype(F32)
     high = high.astype(F32)
     lines_ref[...] = stacked([low, high], columns)
+    copy = pltpu.make_async_copy(lines_ref, block.at[pl.ds(rows, PAD)], sems.at[3])
+    copy.start()
     halo_ref[rows:] = stacked(rows_of(low, part) + rows_of(high, part), part)
+    copy.wait()
     copies[1].wait()
-
-
-def block_kernel(lines_ref, forces, block, sems):
-    rows = forces.shape[0]
-    copies = [
-        pltpu.make_async_copy(forces, block.at[pl.ds(0, rows)], sems.at[0]),
-        pltpu.make_async_copy(lines_ref, block.at[pl.ds(rows, PAD)], sems.at[1]),
-    ]
-    for copy in copies:
-        copy.start()
-    for copy in copies:
-        copy.wait()
-
-
-def pieces_kernel(sc, halo_ref, own_ref, pair_ref, bases_ref, keep_ref, send_ref, thin, thin_ref, sem):
+    copies[2].wait()
+
+
+def pieces_kernel(sc, halo_ref, own_ref, pair_ref, bases_ref, keep_ref, send_ref):
     levels, comps, rank, size = bases_ref.shape
     rows = comps * size
     part = halo_ref.shape[1]
-    quarter = size // 4
     core = sc[0]
     start = pl.multiple_of(sc[1] * part, part)
     tail = own_ref[rows:].astype(F32)
@@ -121,6 +113,15 @@
             sums[level] += dot(bases_ref[level, comp], got)
     keep_ref[...] = jnp.where(core == 0, sums[0], sums[1])
     send_ref[...] = jnp.where(core == 0, sums[1], sums[0])
+
+
+def thin_kernel(sc, halo_ref, own_ref, after, thin, thin_ref, sem):
+    del after
+    comps, quarter, _ = thin.shape
+    size = 4 * quarter
+    rows = comps * size
+    part = halo_ref.shape[1]
+    core = sc[0]
     tail = halo_ref[rows:].astype(F32)
     per = size // part
     low = jnp.concatenate([tail[i : i + 1] for i in range(per)], axis=1)
@@ -241,13 +242,16 @@
         total_ref[span] = total
 
 
-def reduce_kernel(many_ref, sums, sums_ref, sem):
+def reduce_kernel(many, sums, many_ref, sums_ref, sem):
+    copy = pltpu.make_async_copy(many, many_ref, sem.at[0])
+    copy.start()
+    copy.wait()
     total = many_ref[0]
     for i in range(1, many_ref.shape[0]):
         total += many_ref[i]
     for i in range(sums_ref.shape[0]):
         sums_ref[i] = total
-    copy = pltpu.make_async_copy(sums_ref, sums, sem.at[0])
+    copy = pltpu.make_async_copy(sums_ref, sums, sem.at[1])
     copy.start()
     copy.wait()
 
@@ -313,7 +317,11 @@
     del refs
 
 
-def tied(value, *after):
+def cost_of(flops):
+    return pl.CostEstimate(flops=flops, bytes_accessed=10**6, transcendentals=0)
+
+
+def tied(value, *after, flops=0):
     return pl.pallas_call(
         tie_kernel,
         out_shape=shape_of(value.shape, value.dtype),
@@ -321,6 +329,7 @@
         out_specs=ANY,
         input_output_aliases={0: 0},
         compiler_params=params(1),
+        cost_estimate=cost_of(flops),
         name="tie",
     )(value, *after)
 
@@ -363,58 +372,63 @@
         return lax.all_to_all(v, axis, split_axis=0, concat_axis=0, tiled=True)
 
     chain = forces.reshape(rows, columns)
-    halo, lines = pl.pallas_call(
-        functools.partial(halo_kernel, clusters),
-        out_shape=(shape_of((rows + PAD, part), BF16), shape_of((PAD, columns), BF16)),
+    halo, block = pl.pallas_call(
+        functools.partial(dress_kernel, clusters),
+        out_shape=(shape_of((rows + PAD, part), BF16), shape_of((rows + PAD, columns), BF16)),
         in_specs=[SMEM, HBM, HBM],
-        out_specs=(VMEM, VMEM),
-        scratch_shapes=[pltpu.VMEM((1, size), jnp.int32), pltpu.SemaphoreType.DMA((2,))],
+        out_specs=(VMEM, HBM),
+        scratch_shapes=[
+            pltpu.VMEM((1, size), jnp.int32),
+            pltpu.VMEM((PAD, columns), BF16),
+            pltpu.SemaphoreType.DMA((4,)),
+        ],
         compiler_params=params(4),
-        name="halo",
+        name="dress",
     )(sc, *in_hbm(order.reshape(1, size), chain))
     halo = sent(halo, 1)
-    block = pl.pallas_call(
-        block_kernel,
-        out_shape=shape_of((rows + PAD, columns), BF16),
-        in_specs=[VMEM, HBM],
-        out_specs=HBM,
-        scratch_shapes=[pltpu.SemaphoreType.DMA((2,))],
-        compiler_params=params(4),
-        name="block",
-    )(lines, *in_hbm(chain))
+    block = tied(block, flops=12 * 10**9)
     pair = swapped(block)
     near_z = sent(block, -2)
     far_z = sent(block, 2)
 
-    keep, send, thin = pl.pallas_call(
+    keep, send = pl.pallas_call(
         pieces_kernel,
-        out_shape=(
-            shape_of((rank, part), F32),
-            shape_of((rank, part), F32),
-            shape_of((comps, size // 4, columns), BF16),
-        ),
+        out_shape=(shape_of((rank, part), F32),) * 2,
         in_specs=[SMEM, VMEM, VMEM, VMEM, VMEM],
-        out_specs=(VMEM, VMEM, HBM),
+        out_specs=(VMEM, VMEM),
+        compiler_params=params(12),
+        cost_estimate=cost_of(10 * 10**9),
+        name="pieces",
+    )(sc, halo, block, pair, bases.transpose(0, 2, 1, 3))
+    level_sum = keep + swapped(send)
+    many = exchanged(jnp.broadcast_to(level_sum, (steps, rank, part)), "clu_1")
+    thin = pl.pallas_call(
+        thin_kernel,
+        out_shape=shape_of((comps, size // 4, columns), BF16),
+        in_specs=[SMEM, VMEM, VMEM, ANY],
+        out_specs=HBM,
         scratch_shapes=[
             pltpu.VMEM((comps, size // 4, columns), BF16),
             pltpu.SemaphoreType.DMA((1,)),
         ],
         compiler_params=params(12),
-        name="pieces",
-    )(sc, halo, block, pair, bases.transpose(0, 2, 1, 3))
-    level_sum = keep + swapped(send)
-    many = exchanged(jnp.broadcast_to(level_sum, (steps, rank, part)), "clu_1")
+        name="thin",
+    )(sc, halo, block, level_sum)
     thin = sent(thin, 3)
-    many = tied(many, near_z, far_z, *in_hbm(thin))
+    many = tied(*in_hbm(many), near_z, far_z)
     pair_near = swapped(near_z)
     pair_far = swapped(far_z)
     fan = groups * 2 * planes
     sums = pl.pallas_call(
         reduce_kernel,
         out_shape=shape_of((fan, rank, part), F32),
-        in_specs=[VMEM],
+        in_specs=[ANY],
         out_specs=HBM,
-        scratch_shapes=[pltpu.VMEM((fan, rank, part), F32), pltpu.SemaphoreType.DMA((1,))],
+        scratch_shapes=[
+            pltpu.VMEM((steps, rank, part), F32),
+            pltpu.VMEM((fan, rank, part), F32),
+            pltpu.SemaphoreType.DMA((2,)),
+        ],
         compiler_params=params(58),
         name="reduce",
     )(many)
@@ -438,6 +452,7 @@
             pltpu.SemaphoreType.DMA((5,)),
         ],
         compiler_params=params(48),
+        cost_estimate=cost_of(12 * 10**9),
         name="near",
     )(
         sc, *in_hbm(near_col, far_target, far_rank, far_scale, far_coupling[0], near_tiles[0]),

time: 104 us -> 99.5 us (0.957)
  waiting for transfers between devices: 11.8 us -> 3.82 us
  local copies, waits for them, and re-layouts: 1.44 us -> 4.05 us
    ppermute x4, waiting for transfers between devices: 5.77 us -> 0.12 us  [sent(): return lax.ppermute(v, CLU, pairs)]
    unnamed x6 -> x12, local copies, waits for them, and re-layouts: 0.71 us -> 3.32 us
    all_to_all x2, waiting for transfers between devices: 4.86 us -> 2.55 us  [exchanged(): return lax.all_to_all(v, axis, split_axis=0, concat_axis=0, tiled=True)]
  transfers between devices with their start and end apart: 10 -> 10, of which waited for: 3 -> 3; matrix products, arithmetic and copies ran while one was open for 1% -> 1% of each run, Pallas kernels for 10% -> 12%
where the time goes in v4:
time: 99.5 us; the launch traced here: 98.7 us
  starting transfers between devices  57.3 us (58%)
  Pallas kernels  18 us (18%)
  blocking collectives  15.2 us (15%)
  local copies, waits for them, and re-layouts  4.05 us (4%)
  waiting for transfers between devices  3.82 us (4%)
    ppermute x4, starting transfers between devices, sent(): return lax.ppermute(v, CLU, pairs)  37.4 us
    all_to_all x1, blocking collectives, exchanged(): return lax.all_to_all(v, axis, split_axis=0, concat_axis=0, tiled=True)  15.2 us
    all_to_all x2, starting transfers between devices, exchanged(): return lax.all_to_all(v, axis, split_axis=0, concat_axis=0, tiled=True)  11.6 us
    ppermute x4, starting transfers between devices, swapped(): return lax.ppermute(v, 'clu_2', [(0, 1), (1, 0)])  8.29 us
    pallas_call x1, Pallas kernels, on_device(): pl.pallas_call(functools.partial(near_kernel, clusters, planes), out_shap...  7.38 us
    pallas_call x1, Pallas kernels, on_device(): pl.pallas_call(functools.partial(mix_kernel, planes), out_shape=shape_of(...  3.44 us
    unnamed x12, local copies, waits for them, and re-layouts  3.32 us
    all_to_all x2, waiting for transfers between devices, exchanged(): return lax.all_to_all(v, axis, split_axis=0, concat_axis=0, tiled=True)  2.55 us
  transfers between devices with their start and end apart: 10, of which 3 were waited for; matrix products, arithmetic and copies ran while one was open for 1% of the time, Pallas kernels for 12%

profile of v4, /device:TPU:32, one launch (start us, length us, event | category | flops | bytes accessed | tf_op | source)
XLA Modules:
  0.0 98.7 jit_solution(8194365324020730780)
XLA Ops:
  0.0 0.1 pad_add_fusion.sc
  0.1 1.8 %dress.1 = (bf16[784,128]{1,0:T(8,128)(2,1)S(1)}, bf16[784,512]{1,0:T(8,128)(2,1)S(1)}) custom-call(s32[4]{0:T(128)S(1)} %pad_add_fusion.sc, s32[1,256]{1,0:T(1,128)} %bitcast.14, bf16[768,512]{1,0:T(8,128)(2,1)} %bitcast.12), custom_call_target="tpu_custom_call" | custom-call | tf_op jit(solution)/shard_map/dress/pallas_call | solution.py:375
  1.9 0.0 copy-start.2
  1.9 2.1 %collective-permute-start.1 = (bf16[784,512]{1,0:T(8,128)(2,1)S(1)}, bf16[784,512]{1,0:T(8,128)(2,1)S(1)}, u32[]{:S(2)}, u32[]{:S(2)}) collective-permute-start(bf16[784,512]{1,0:T(8,128)(2,1)S(1)} %tie.2.own_ref.own), channel_id=1, source_target_pairs={{0,1},{1,0},{2,3},{3,2},{4,5},{5,4},{6,7},{7,6},{8,9},{9,8},{10,11... | collective-permute-start | bytes 2408456 | tf_op jit(solution)/shard_map/ppermute | solution.py:365
  4.0 7.5 %collective-permute-start = (bf16[784,128]{1,0:T(8,128)(2,1)S(1)}, bf16[784,128]{1,0:T(8,128)(2,1)S(1)}, u32[]{:S(2)}, u32[]{:S(2)}) collective-permute-start(bf16[784,128]{1,0:T(8,128)(2,1)S(1)} %get-tuple-element.13), channel_id=1, source_target_pairs={{0,127},{1,2},{2,1},{3,4},{4,3},{5,6},{6,5},{7,8},{8,7},{9,10},{10... | collective-permute-start | bytes 602120 | tf_op jit(solution)/shard_map/ppermute | solution.py:369
  11.5 8.2 %collective-permute-start.5 = (bf16[784,512]{1,0:T(8,128)(2,1)S(1)}, bf16[784,512]{1,0:T(8,128)(2,1)S(1)}, u32[]{:S(2)}, u32[]{:S(2)}) collective-permute-start(bf16[784,512]{1,0:T(8,128)(2,1)S(1)} %tie.2.own_ref.own), channel_id=1, source_target_pairs={{0,126},{1,3},{2,0},{3,5},{4,2},{5,7},{6,4},{7,9},{8,6},{9,11},{10... | collective-permute-start | bytes 2408456 | tf_op jit(solution)/shard_map/ppermute | solution.py:369
  19.7 1.9 %collective-permute-start.4 = (bf16[784,512]{1,0:T(8,128)(2,1)S(1)}, bf16[784,512]{1,0:T(8,128)(2,1)S(1)}, u32[]{:S(2)}, u32[]{:S(2)}) collective-permute-start(bf16[784,512]{1,0:T(8,128)(2,1)S(1)} %tie.2.own_ref.own), channel_id=1, source_target_pairs={{0,2},{1,127},{2,4},{3,1},{4,6},{5,3},{6,8},{7,5},{8,10},{9,7},{10... | collective-permute-start | bytes 2408456 | tf_op jit(solution)/shard_map/ppermute | solution.py:369
  21.7 0.0 collective-permute-done.halo_ref
  21.7 0.0 collective-permute-done.1.pair_ref.pair
  21.7 0.0 copy-start
  21.7 0.0 copy-done.2
  21.7 1.4 %pieces.1 = (f32[32,128]{1,0:T(8,128)S(1)}, f32[32,128]{1,0:T(8,128)S(1)}) custom-call(s32[4]{0:T(128)S(1)} %pad_add_fusion.sc, bf16[784,128]{1,0:T(8,128)(2,1)S(1)} %collective-permute-done.halo_ref, bf16[784,512]{1,0:T(8,128)(2,1)S(1)} %tie.2.own_ref.own, bf16[784,512]{1,0:T(8,128)(2,1)S(1)} %collective-permute-done.1.pair_ref.pair, ...), custom_call_target="tpu_custom_call" | custom-call | flops 10000000000 | bytes 1000000 | tf_op jit(solution)/shard_map/pieces/pallas_call | solution.py:394
  23.1 0.0 copy-done
  23.1 1.9 %collective-permute-start.2 = (f32[32,128]{1,0:T(8,128)S(1)}, f32[32,128]{1,0:T(8,128)S(1)}, u32[]{:S(2)}, u32[]{:S(2)}) collective-permute-start(f32[32,128]{1,0:T(8,128)S(1)} %get-tuple-element.15), channel_id=1, source_target_pairs={{0,1},{1,0},{2,3},{3,2},{4,5},{5,4},{6,7},{7,6},{8,9},{9,8},{10,11... | collective-permute-start | bytes 49160 | tf_op jit(solution)/shard_map/ppermute | solution.py:365
  25.1 1.1 %collective-permute-done.2 = f32[32,128]{1,0:T(8,128)S(1)} collective-permute-done((f32[32,128]{1,0:T(8,128)S(1)}, f32[32,128]{1,0:T(8,128)S(1)}, u32[]{:S(2)}, u32[]{:S(2)}) %collective-permute-start.2) | collective-permute-done | bytes 16416 | tf_op jit(solution)/shard_map/ppermute | solution.py:365
  26.2 0.7 broadcast_in_dim.3
  27.0 6.8 %all-to-all-start = ((f32[16,32,128]{2,1,0:T(8,128)}), f32[16,32,128]{2,1,0:T(8,128)S(1)}, u32[]{:S(2)}, u32[]{:S(2)}) async-start(f32[16,32,128]{2,1,0:T(8,128)} %broadcast_in_dim.3), calls=%async_computation | async-start | bytes 524288 | tf_op jit(solution)/shard_map/all_to_all | solution.py:372
  33.7 0.1 collective-permute-done.5.far_z.refs_2_
  33.8 1.9 %collective-permute-start.6 = (bf16[784,512]{1,0:T(8,128)(2,1)S(1)}, bf16[784,512]{1,0:T(8,128)(2,1)}, u32[]{:S(2)}, u32[]{:S(2)}) collective-permute-start(bf16[784,512]{1,0:T(8,128)(2,1)S(1)} %collective-permute-done.5.far_z.refs_2_), channel_id=1, source_target_pairs={{0,1},{1,0},{2,3},{3,2},{4,5},{5,4},{6,7},{7,6},{8,9},{9,8},{10,11... | collective-permute-start | bytes 2408456 | tf_op jit(solution)/shard_map/ppermute | solution.py:365
  35.7 0.0 collective-permute-done.4.near_z.refs_1_
  35.8 2.4 %collective-permute-start.7 = (bf16[784,512]{1,0:T(8,128)(2,1)S(1)}, bf16[784,512]{1,0:T(8,128)(2,1)}, u32[]{:S(2)}, u32[]{:S(2)}) collective-permute-start(bf16[784,512]{1,0:T(8,128)(2,1)S(1)} %collective-permute-done.4.near_z.refs_1_), channel_id=1, source_target_pairs={{0,1},{1,0},{2,3},{3,2},{4,5},{5,4},{6,7},{7,6},{8,9},{9,8},{10,11... | collective-permute-start | bytes 2408456 | tf_op jit(solution)/shard_map/ppermute | solution.py:365
  38.2 1.3 %thin.1 = bf16[3,64,512]{2,1,0:T(8,128)(2,1)S(1)} custom-call(s32[4]{0:T(128)S(1)} %pad_add_fusion.sc, bf16[784,128]{1,0:T(8,128)(2,1)S(1)} %collective-permute-done.halo_ref, bf16[784,512]{1,0:T(8,128)(2,1)S(1)} %tie.2.own_ref.own, f32[32,128]{1,0:T(8,128)S(1)} %add.11.after), custom_call_target="tpu_custom_call" | custom-call | tf_op jit(solution)/shard_map/thin/pallas_call | solution.py:405
  39.5 19.8 %collective-permute-start.3 = (bf16[3,64,512]{2,1,0:T(8,128)(2,1)S(1)}, bf16[3,64,512]{2,1,0:T(8,128)(2,1)S(1)}, u32[]{:S(2)}, u32[]{:S(2)}) collective-permute-start(bf16[3,64,512]{2,1,0:T(8,128)(2,1)S(1)} %thin.1), channel_id=1, source_target_pairs={{0,125},{1,4},{2,127},{3,6},{4,1},{5,8},{6,3},{7,10},{8,5},{9,12},... | collective-permute-start | bytes 589832 | tf_op jit(solution)/shard_map/ppermute | solution.py:369
  59.2 0.0 all-to-all-done.refs_0_
  59.3 0.0 copy-start.3
  59.3 0.7 copy-done.3
  60.0 1.8 %reduce.1 = f32[32,32,128]{2,1,0:T(8,128)} custom-call(f32[16,32,128]{2,1,0:T(8,128)} %tie.3.many), custom_call_target="tpu_custom_call" | custom-call | tf_op jit(solution)/shard_map/reduce/pallas_call | solution.py:422
  61.8 4.9 %all-to-all-start.1 = ((f32[32,32,128]{2,1,0:T(8,128)}), f32[32,32,128]{2,1,0:T(8,128)S(1)}, u32[]{:S(2)}, u32[]{:S(2)}) async-start(f32[32,32,128]{2,1,0:T(8,128)} %reduce.1), calls=%async_computation.1 | async-start | bytes 1048576 | tf_op jit(solution)/shard_map/all_to_all | solution.py:372
  66.7 0.0 collective-permute-done.3.thin
  66.7 0.0 copy-start.5
  66.7 0.0 collective-permute-done.6.pair_far
  66.7 0.0 collective-permute-done.7.pair_near
  66.7 0.6 copy-done.5
  67.4 0.0 copy-start.1
  67.4 1.1 %copy-done.1 = bf16[784,512]{1,0:T(8,128)(2,1)S(1)} copy-done((bf16[784,512]{1,0:T(8,128)(2,1)S(1)}, bf16[784,512]{1,0:T(8,128)(2,1)}, u32[]{:S(2)}) %copy-start.1) | copy-done | bytes 802840
  68.5 7.4 %near.1 = (f32[768,512]{1,0:T(8,128)}, bf16[512,128]{1,0:T(8,128)(2,1)S(1)}, bf16[512,128]{1,0:T(8,128)(2,1)S(1)}) custom-call(s32[4]{0:T(128)S(1)} %pad_add_fusion.sc, s32[1,2]{1,0:T(1,128)} %near_col.1, s32[1,16]{1,0:T(1,128)} %target.1, s32[1,16]{1,0:T(1,128)} %keeps.1, f32[1,16]{1,0:T(1,128)} %scale.1, bf16[16,32,32]{2,1,0:T(8,128)(2,1)} %bitcast.16, ...), custom_call_target="tpu_custom_call" | custom-call | flops 12000000000 | bytes 1000000 | tf_op jit(solution)/shard_map/near/pallas_call | solution.py:436
  75.9 2.5 %all-to-all-done.1.sums = f32[32,32,128]{2,1,0:T(8,128)S(1)} async-done(((f32[32,32,128]{2,1,0:T(8,128)}), f32[32,32,128]{2,1,0:T(8,128)S(1)}, u32[]{:S(2)}, u32[]{:S(2)}) %all-to-all-start.1) | async-done | bytes 524320 | tf_op jit(solution)/shard_map/all_to_all | solution.py:372
  78.4 0.0 copy-start.4
  78.4 0.8 copy-done.4
  79.3 3.4 %mix.1 = bf16[4,768,128]{2,1,0:T(8,128)(2,1)S(1)} custom-call(s32[4]{0:T(128)S(1)} %pad_add_fusion.sc, f32[768,512]{1,0:T(8,128)} %get-tuple-element.16.near, f32[32,32,128]{2,1,0:T(8,128)} %copy-done.4, bf16[512,768]{1,0:T(8,128)(2,1)} %bitcast.13, bf16[512,128]{1,0:T(8,128)(2,1)S(1)} %get-tuple-element.17.high_ref, ...), custom_call_target="tpu_custom_call" | custom-call | tf_op jit(solution)/shard_map/mix/pallas_call | solution.py:461
  82.7 15.2 %all_to_all.15.arrived_ref = bf16[4,768,128]{2,1,0:T(8,128)(2,1)S(1)} all-to-all(bf16[4,768,128]{2,1,0:T(8,128)(2,1)S(1)} %mix.1), channel_id=1, replica_groups=mesh['grp'=4,'clu_0'=4,'clu_1'=16,'clu_2'=2] {'grp'}, dimensions={0} | all-to-all | bytes 1572864 | tf_op jit(solution)/shard_map/all_to_all | solution.py:372
  97.9 0.8 last.1
  (3 shorter events, 0.0 us)
Async XLA Ops:
  1.9 19.8 %copy-start.2 = (bf16[2,32,3,256]{3,1,2,0:T(8,128)(2,1)S(1)}, bf16[2,32,3,256]{3,1,2,0:T(8,128)(2,1)}, u32[]{:S(2)}) copy-start(bf16[2,32,3,256]{3,1,2,0:T(8,128)(2,1)} %param.12) | copy-start | bytes 294916
  1.9 19.7 %collective-permute-start.1 = (bf16[784,512]{1,0:T(8,128)(2,1)S(1)}, bf16[784,512]{1,0:T(8,128)(2,1)S(1)}, u32[]{:S(2)}, u32[]{:S(2)}) collective-permute-start(bf16[784,512]{1,0:T(8,128)(2,1)S(1)} %tie.2.own_ref.own), channel_id=1, source_target_pairs={{0,1},{1,0},{2,3},{3,2},{4,5},{5,4},{6,7},{7,6},{8,9},{9,8},{10,11... | collective-permute-start | bytes 2408456 | tf_op jit(solution)/shard_map/ppermute | solution.py:365
  4.0 17.7 %collective-permute-start = (bf16[784,128]{1,0:T(8,128)(2,1)S(1)}, bf16[784,128]{1,0:T(8,128)(2,1)S(1)}, u32[]{:S(2)}, u32[]{:S(2)}) collective-permute-start(bf16[784,128]{1,0:T(8,128)(2,1)S(1)} %get-tuple-element.13), channel_id=1, source_target_pairs={{0,127},{1,2},{2,1},{3,4},{4,3},{5,6},{6,5},{7,8},{8,7},{9,10},{10... | collective-permute-start | bytes 602120 | tf_op jit(solution)/shard_map/ppermute | solution.py:369
  11.5 22.3 %collective-permute-start.5 = (bf16[784,512]{1,0:T(8,128)(2,1)S(1)}, bf16[784,512]{1,0:T(8,128)(2,1)S(1)}, u32[]{:S(2)}, u32[]{:S(2)}) collective-permute-start(bf16[784,512]{1,0:T(8,128)(2,1)S(1)} %tie.2.own_ref.own), channel_id=1, source_target_pairs={{0,126},{1,3},{2,0},{3,5},{4,2},{5,7},{6,4},{7,9},{8,6},{9,11},{10... | collective-permute-start | bytes 2408456 | tf_op jit(solution)/shard_map/ppermute | solution.py:369
  19.7 16.0 %collective-permute-start.4 = (bf16[784,512]{1,0:T(8,128)(2,1)S(1)}, bf16[784,512]{1,0:T(8,128)(2,1)S(1)}, u32[]{:S(2)}, u32[]{:S(2)}) collective-permute-start(bf16[784,512]{1,0:T(8,128)(2,1)S(1)} %tie.2.own_ref.own), channel_id=1, source_target_pairs={{0,2},{1,127},{2,4},{3,1},{4,6},{5,3},{6,8},{7,5},{8,10},{9,7},{10... | collective-permute-start | bytes 2408456 | tf_op jit(solution)/shard_map/ppermute | solution.py:369
  21.7 1.4 %copy-start = (bf16[784,512]{1,0:T(8,128)(2,1)}, bf16[784,512]{1,0:T(8,128)(2,1)S(1)}, u32[]{:S(2)}) copy-start(bf16[784,512]{1,0:T(8,128)(2,1)S(1)} %collective-permute-done.1.pair_ref.pair) | copy-start | bytes 2408452
  23.1 3.1 %collective-permute-start.2 = (f32[32,128]{1,0:T(8,128)S(1)}, f32[32,128]{1,0:T(8,128)S(1)}, u32[]{:S(2)}, u32[]{:S(2)}) collective-permute-start(f32[32,128]{1,0:T(8,128)S(1)} %get-tuple-element.15), channel_id=1, source_target_pairs={{0,1},{1,0},{2,3},{3,2},{4,5},{5,4},{6,7},{7,6},{8,9},{9,8},{10,11... | collective-permute-start | bytes 49160 | tf_op jit(solution)/shard_map/ppermute | solution.py:365
  27.0 32.3 %all-to-all-start = ((f32[16,32,128]{2,1,0:T(8,128)}), f32[16,32,128]{2,1,0:T(8,128)S(1)}, u32[]{:S(2)}, u32[]{:S(2)}) async-start(f32[16,32,128]{2,1,0:T(8,128)} %broadcast_in_dim.3), calls=%async_computation | async-start | bytes 524288 | tf_op jit(solution)/shard_map/all_to_all | solution.py:372
  33.8 32.9 %collective-permute-start.6 = (bf16[784,512]{1,0:T(8,128)(2,1)S(1)}, bf16[784,512]{1,0:T(8,128)(2,1)}, u32[]{:S(2)}, u32[]{:S(2)}) collective-permute-start(bf16[784,512]{1,0:T(8,128)(2,1)S(1)} %collective-permute-done.5.far_z.refs_2_), channel_id=1, source_target_pairs={{0,1},{1,0},{2,3},{3,2},{4,5},{5,4},{6,7},{7,6},{8,9},{9,8},{10,11... | collective-permute-start | bytes 2408456 | tf_op jit(solution)/shard_map/ppermute | solution.py:365
  35.8 31.0 %collective-permute-start.7 = (bf16[784,512]{1,0:T(8,128)(2,1)S(1)}, bf16[784,512]{1,0:T(8,128)(2,1)}, u32[]{:S(2)}, u32[]{:S(2)}) collective-permute-start(bf16[784,512]{1,0:T(8,128)(2,1)S(1)} %collective-permute-done.4.near_z.refs_1_), channel_id=1, source_target_pairs={{0,1},{1,0},{2,3},{3,2},{4,5},{5,4},{6,7},{7,6},{8,9},{9,8},{10,11... | collective-permute-start | bytes 2408456 | tf_op jit(solution)/shard_map/ppermute | solution.py:365
  39.5 27.2 %collective-permute-start.3 = (bf16[3,64,512]{2,1,0:T(8,128)(2,1)S(1)}, bf16[3,64,512]{2,1,0:T(8,128)(2,1)S(1)}, u32[]{:S(2)}, u32[]{:S(2)}) collective-permute-start(bf16[3,64,512]{2,1,0:T(8,128)(2,1)S(1)} %thin.1), channel_id=1, source_target_pairs={{0,125},{1,4},{2,127},{3,6},{4,1},{5,8},{6,3},{7,10},{8,5},{9,12},... | collective-permute-start | bytes 589832 | tf_op jit(solution)/shard_map/ppermute | solution.py:369
  59.3 0.7 copy-start.3
  61.8 16.6 %all-to-all-start.1 = ((f32[32,32,128]{2,1,0:T(8,128)}), f32[32,32,128]{2,1,0:T(8,128)S(1)}, u32[]{:S(2)}, u32[]{:S(2)}) async-start(f32[32,32,128]{2,1,0:T(8,128)} %reduce.1), calls=%async_computation.1 | async-start | bytes 1048576 | tf_op jit(solution)/shard_map/all_to_all | solution.py:372
  66.7 0.7 copy-start.5
  67.4 1.1 %copy-start.1 = (bf16[784,512]{1,0:T(8,128)(2,1)S(1)}, bf16[784,512]{1,0:T(8,128)(2,1)}, u32[]{:S(2)}) copy-start(bf16[784,512]{1,0:T(8,128)(2,1)} %copy-done) | copy-start | bytes 2408452
  78.4 0.8 copy-start.4

commit v5 on v4

--- a/solution.py
+++ b/solution.py
@@ -140,31 +140,18 @@
 
 
 def near_kernel(
-    clusters, planes, sc, near_col, target, keeps, scale, coupling, tiles,
-    own, thin, near_z, pair_far, pair, far_z, pair_near,
-    total_ref, high_ref, low_ref,
-    col_ref, target_ref, keep_ref, scale_ref, coupling_ref, tile_ref, window, blocks,
-    sems, tile_sems, small_sems,
+    clusters, sc, near_col, tiles, own, thin, near_z, pair_far, pair, far_z, pair_near,
+    total, tile_ref, tails, window, blocks, total_ref, sems, tail_sems, tile_sems, out_sems,
 ):
     count, rows, _ = tiles.shape
     columns = own.shape[1]
     size = rows // 3
     quarter = size // 4
     core = sc[0]
-    pairs = (
-        (near_col, col_ref), (target, target_ref), (keeps, keep_ref), (scale, scale_ref),
-        (coupling, coupling_ref),
-    )
-    smalls = [pltpu.make_async_copy(a, b, small_sems.at[i]) for i, (a, b) in enumerate(pairs)]
-    for copy in smalls:
-        copy.start()
     seats = (thin, near_z, pair_far, own, pair, far_z, pair_near)
-    for j in range(count):
-        pltpu.make_async_copy(tiles.at[j], tile_ref.at[j], tile_sems.at[j]).start()
-    smalls[0].wait()
     offs = []
     for j in range(count):
-        off = col_ref[0, j] - sc[3] + 2
+        off = near_col[j] - sc[3] + 2
         off = jnp.where(off < 0, off + clusters, off)
         off = jnp.where(off >= clusters, off - clusters, off) - 2
         offs.append(jnp.where(core == 0, off, -off))
@@ -173,53 +160,34 @@
 
             @pl.when(offs[j] == o)
             def _(j=j, o=o):
-                for w in range(3):
-                    source = seats[o + 2 + w]
-                    if o + w == -2:
-                        for comp in range(3):
+                pltpu.make_async_copy(seats[o + 3].at[pl.ds(rows, PAD)], tails.at[j], tail_sems.at[j]).start()
+                for comp in range(3):
+                    for w in range(3):
+                        source = seats[o + 2 + w]
+                        if o + w == -2:
                             pltpu.make_async_copy(
                                 source.at[comp],
-                                window.at[j, w, pl.ds(comp * size, quarter)],
-                                sems.at[j, w, comp],
+                                window.at[j, comp, pl.ds(w * size, quarter)],
+                                sems.at[j, comp, w],
                             ).start()
-                            window[j, w, comp * size + quarter : (comp + 1) * size] = jnp.zeros(
+                            window[j, comp, w * size + quarter : (w + 1) * size] = jnp.zeros(
                                 (size - quarter, columns), BF16
                             )
-                    else:
-                        pltpu.make_async_copy(source, window.at[j, w], sems.at[j, w, 0]).start()
-
-    for copy in smalls[1:]:
-        copy.wait()
-    far_count, rank, _ = coupling_ref.shape
-    width = high_ref.shape[1]
-    lane = iota((rank, width), 1)
-    for b in range(far_count):
-        goal = target_ref[0, b]
-        start = jnp.where(goal < 2, 0, lax.rem(goal - 2 - sc[2] + planes, planes)) * rank
-        tile = coupling_ref[b].astype(F32) * scale_ref[0, b]
-        tile = jnp.concatenate([tile] * (width // rank), axis=1)
-        tile = jnp.where((lane >= start) & (lane < start + keep_ref[0, b]), tile, 0.0)
-        high = tile.astype(BF16)
-        high_ref[b * rank : (b + 1) * rank] = high
-        low_ref[b * rank : (b + 1) * rank] = (tile - high.astype(F32)).astype(BF16)
-
+                        else:
+                            pltpu.make_async_copy(
+                                source.at[pl.ds(comp * size, size)],
+                                window.at[j, comp, pl.ds(w * size, size)],
+                                sems.at[j, comp, w],
+                            ).start()
+
+    for j in range(count):
+        pltpu.make_async_copy(
+            tiles.at[j], tile_ref.at[:, pl.ds(j * rows, rows)], tile_sems.at[j]
+        ).start()
     for j in range(count):
         edge = offs[j] == -2
-        for w in range(1, 3):
-            pltpu.make_async_copy(own, window.at[j, w], sems.at[j, w, 0]).wait()
-
-        @pl.when(edge)
-        def _(j=j):
-            for comp in range(3):
-                pltpu.make_async_copy(
-                    thin.at[comp], window.at[j, 0, pl.ds(comp * size, quarter)], sems.at[j, 0, comp]
-                ).wait()
-
-        @pl.when(jnp.logical_not(edge))
-        def _(j=j):
-            pltpu.make_async_copy(own, window.at[j, 0], sems.at[j, 0, 0]).wait()
-
-        tail = window[j, 1, rows:].astype(F32)
+        pltpu.make_async_copy(own.at[pl.ds(rows, PAD)], tails.at[j], tail_sems.at[j]).wait()
+        tail = tails[j].astype(F32)
         low, high = tail[0:1, :size], tail[1:2, :size]
         seat = jnp.where(core == 0, high, 2.0 - high)
         first = seat == 0.0
@@ -227,40 +195,82 @@
         low = jnp.where(jnp.logical_and(first, edge), place, low)
         pick = chosen(as_column(seat * size + low), 3 * size)
         for comp in range(3):
-            span = slice(comp * size, (comp + 1) * size)
-            got = dot(pick[:, :size], window[j, 0, span])
+
+            @pl.when(edge)
+            def _(j=j, comp=comp):
+                pltpu.make_async_copy(
+                    thin.at[comp], window.at[j, comp, pl.ds(0, quarter)], sems.at[j, comp, 0]
+                ).wait()
+
+            @pl.when(jnp.logical_not(edge))
+            def _(j=j, comp=comp):
+                pltpu.make_async_copy(
+                    own.at[pl.ds(0, size)], window.at[j, comp, pl.ds(0, size)], sems.at[j, comp, 0]
+                ).wait()
+
             for w in range(1, 3):
-                got += dot(pick[:, w * size : (w + 1) * size], window[j, w, span])
-            blocks[j, span] = got.astype(BF16)
+                pltpu.make_async_copy(
+                    own.at[pl.ds(0, size)], window.at[j, comp, pl.ds(w * size, size)], sems.at[j, comp, w]
+                ).wait()
+            at = j * rows + comp * size
+            blocks[at : at + size] = dot(pick, window[j, comp]).astype(BF16)
     for j in range(count):
-        pltpu.make_async_copy(tiles.at[j], tile_ref.at[j], tile_sems.at[j]).wait()
+        pltpu.make_async_copy(
+            tiles.at[j], tile_ref.at[:, pl.ds(j * rows, rows)], tile_sems.at[j]
+        ).wait()
+    outs = []
     for r in range(3):
         span = slice(r * size, (r + 1) * size)
-        total = dot(tile_ref[0, span], blocks[0])
-        for j in range(1, count):
-            total += dot(tile_ref[j, span], blocks[j])
-        total_ref[span] = total
-
-
-def reduce_kernel(many, sums, many_ref, sums_ref, sem):
-    copy = pltpu.make_async_copy(many, many_ref, sem.at[0])
+        total_ref[span] = dot(tile_ref[span], blocks[...])
+        here = pl.ds(r * size, size)
+        outs.append(pltpu.make_async_copy(total_ref.at[here], total.at[here], out_sems.at[r]))
+        outs[-1].start()
+    for copy in outs:
+        copy.wait()
+
+
+def couple_kernel(
+    planes, sc, target, keeps, scale, coupling, after, mixed, coupling_ref, mixed_ref, sems
+):
+    del after
+    copy = pltpu.make_async_copy(coupling, coupling_ref, sems.at[0])
     copy.start()
     copy.wait()
+    blocks, rank, _ = coupling_ref.shape
+    width = mixed_ref.shape[1] // 3
+    lane = iota((rank, width), 1)
+    for b in range(blocks):
+        goal = target[b]
+        first = jnp.where(goal < 2, 0, lax.rem(goal - 2 - sc[2] + planes, planes)) * rank
+        tile = coupling_ref[b].astype(F32) * scale[b]
+        tile = jnp.concatenate([tile] * (width // rank), axis=1)
+        tile = jnp.where((lane >= first) & (lane < first + keeps[b]), tile, 0.0)
+        high = tile.astype(BF16)
+        at = slice(b * rank, (b + 1) * rank)
+        mixed_ref[at, :width] = high
+        mixed_ref[at, width : 2 * width] = high
+        mixed_ref[at, 2 * width :] = (tile - high.astype(F32)).astype(BF16)
+    copy = pltpu.make_async_copy(mixed_ref, mixed, sems.at[1])
+    copy.start()
+    copy.wait()
+
+
+def reduce_kernel(many_ref, sums, sums_ref, sem):
     total = many_ref[0]
     for i in range(1, many_ref.shape[0]):
         total += many_ref[i]
     for i in range(sums_ref.shape[0]):
         sums_ref[i] = total
-    copy = pltpu.make_async_copy(sums_ref, sums, sem.at[1])
+    copy = pltpu.make_async_copy(sums_ref, sums, sem.at[0])
     copy.start()
     copy.wait()
 
 
 def mix_kernel(
-    planes, sc, near, sums, basis, high_ref, low_ref, split,
-    near_ref, sums_ref, basis_ref, table_ref, coupled_ref, result, in_sems, sems,
+    planes, sc, near, sums, basis, mixed, split,
+    near_ref, sums_ref, basis_ref, mixed_ref, table_ref, stack_ref, coupled_ref, result, in_sems, sems,
 ):
-    pairs = ((sums, sums_ref), (basis, basis_ref), (near, near_ref))
+    pairs = ((sums, sums_ref), (basis, basis_ref), (near, near_ref), (mixed, mixed_ref))
     copies = [pltpu.make_async_copy(a, b, in_sems.at[i]) for i, (a, b) in enumerate(pairs)]
     for copy in copies:
         copy.start()
@@ -281,13 +291,16 @@
             at = lax.rem(plane + i, planes)
             table_ref[i * rank : (i + 1) * rank, lanes] = sums_ref[base + 2 * at + 1]
     table = table_ref[...]
+    width = table.shape[0]
     high = table.astype(BF16)
-    low = (table - high.astype(F32)).astype(BF16)
-    step = high_ref.shape[0] // 2
+    stack_ref[:width] = high
+    stack_ref[width : 2 * width] = (table - high.astype(F32)).astype(BF16)
+    stack_ref[2 * width :] = high
+    copies[3].wait()
+    step = mixed_ref.shape[0] // 2
     for i in range(2):
         span = slice(i * step, (i + 1) * step)
-        coupled = dot(high_ref[span], high) + dot(high_ref[span], low) + dot(low_ref[span], high)
-        coupled_ref[span] = coupled.astype(BF16)
+        coupled_ref[span] = dot(mixed_ref[span], stack_ref[...]).astype(BF16)
     copies[1].wait()
     copies[2].wait()
     outs = []
@@ -415,67 +428,76 @@
         name="thin",
     )(sc, halo, block, level_sum)
     thin = sent(thin, 3)
-    many = tied(*in_hbm(many), near_z, far_z)
+    many = tied(many, near_z, far_z)
     pair_near = swapped(near_z)
     pair_far = swapped(far_z)
     fan = groups * 2 * planes
     sums = pl.pallas_call(
         reduce_kernel,
         out_shape=shape_of((fan, rank, part), F32),
-        in_specs=[ANY],
+        in_specs=[VMEM],
         out_specs=HBM,
-        scratch_shapes=[
-            pltpu.VMEM((steps, rank, part), F32),
-            pltpu.VMEM((fan, rank, part), F32),
-            pltpu.SemaphoreType.DMA((2,)),
-        ],
-        compiler_params=params(58),
+        scratch_shapes=[pltpu.VMEM((fan, rank, part), F32), pltpu.SemaphoreType.DMA((1,))],
+        compiler_params=params(4),
         name="reduce",
     )(many)
     sums = exchanged(sums, ("grp", "clu_0", "clu_2"))
-    near, high, low = pl.pallas_call(
-        functools.partial(near_kernel, clusters, planes),
-        out_shape=(shape_of((rows, columns), F32),) + (shape_of((far_count * rank, width), BF16),) * 2,
-        in_specs=[SMEM] + [HBM] * 6 + [ANY] * 7,
-        out_specs=(VMEM, VMEM, VMEM),
+    near = pl.pallas_call(
+        functools.partial(near_kernel, clusters),
+        out_shape=shape_of((rows, columns), F32),
+        in_specs=[SMEM, SMEM, HBM] + [ANY] * 7,
+        out_specs=HBM,
         scratch_shapes=[
-            pltpu.SMEM((1, count), jnp.int32),
-            pltpu.SMEM((1, far_count), jnp.int32),
-            pltpu.SMEM((1, far_count), jnp.int32),
-            pltpu.SMEM((1, far_count), F32),
-            pltpu.VMEM((far_count, rank, rank), BF16),
-            pltpu.VMEM((count, rows, rows), BF16),
-            pltpu.VMEM((count, 3, rows + PAD, columns), BF16),
-            pltpu.VMEM((count, rows, columns), BF16),
+            pltpu.VMEM((rows, count * rows), BF16),
+            pltpu.VMEM((count, PAD, columns), BF16),
+            pltpu.VMEM((count, comps, rows, columns), BF16),
+            pltpu.VMEM((count * rows, columns), BF16),
+            pltpu.VMEM((rows, columns), F32),
             pltpu.SemaphoreType.DMA((count, 3, 3)),
             pltpu.SemaphoreType.DMA((count,)),
-            pltpu.SemaphoreType.DMA((5,)),
+            pltpu.SemaphoreType.DMA((count,)),
+            pltpu.SemaphoreType.DMA((3,)),
         ],
         compiler_params=params(48),
         cost_estimate=cost_of(12 * 10**9),
         name="near",
     )(
-        sc, *in_hbm(near_col, far_target, far_rank, far_scale, far_coupling[0], near_tiles[0]),
-        block, *in_hbm(thin), near_z, pair_far, pair, far_z, pair_near,
+        sc, *in_hbm(near_col[0], near_tiles[0]),
+        *in_hbm(block), *in_hbm(thin), *in_hbm(near_z), pair_far, *in_hbm(pair), far_z, pair_near,
     )
+    mixed = pl.pallas_call(
+        functools.partial(couple_kernel, planes),
+        out_shape=shape_of((far_count * rank, 3 * width), BF16),
+        in_specs=[SMEM, SMEM, SMEM, SMEM, HBM, ANY],
+        out_specs=HBM,
+        scratch_shapes=[
+            pltpu.VMEM((far_count, rank, rank), BF16),
+            pltpu.VMEM((far_count * rank, 3 * width), BF16),
+            pltpu.SemaphoreType.DMA((2,)),
+        ],
+        compiler_params=params(4),
+        name="couple",
+    )(sc, *in_hbm(far_target[0], far_rank[0], far_scale[0], far_coupling[0]), level_sum)
     split = pl.pallas_call(
         functools.partial(mix_kernel, planes),
         out_shape=shape_of((groups, rows, part), BF16),
-        in_specs=[SMEM, HBM, HBM, HBM, VMEM, VMEM],
+        in_specs=[SMEM, ANY, ANY, HBM, ANY],
         out_specs=HBM,
         scratch_shapes=[
             pltpu.VMEM((rows, columns), F32),
             pltpu.VMEM((fan, rank, part), F32),
             pltpu.VMEM((far_count * rank, rows), BF16),
+            pltpu.VMEM((far_count * rank, 3 * width), BF16),
             pltpu.VMEM((width, columns), F32),
+            pltpu.VMEM((3 * width, columns), BF16),
             pltpu.VMEM((far_count * rank, columns), BF16),
             pltpu.VMEM((groups, rows, part), BF16),
-            pltpu.SemaphoreType.DMA((3,)),
+            pltpu.SemaphoreType.DMA((4,)),
             pltpu.SemaphoreType.DMA((3,)),
         ],
         compiler_params=params(16),
         name="mix",
-    )(sc, *in_hbm(near, sums, far_basis.reshape(far_count * rank, rows)), high, low)
+    )(sc, near, sums, *in_hbm(far_basis.reshape(far_count * rank, rows)), mixed)
     arrived = exchanged(split, "grp")
     velocity = pl.pallas_call(
         last_kernel,

time: 99.5 us -> 98.4 us (0.989)
  local copies, waits for them, and re-layouts: 4.05 us -> 1.4 us
    unnamed x12 -> x10, local copies, waits for them, and re-layouts: 3.32 us -> 0.67 us
    pallas_call x1 -> x2, Pallas kernels: 7.38 us -> 9.63 us  [the longest x1 7.55 us: on_device(): pl.pallas_call(functools.partial(near_kernel, clusters), out_shape=shape_...]
  transfers between devices with their start and end apart: 10 -> 10, of which waited for: 3 -> 3; matrix products, arithmetic and copies ran while one was open for 1% -> 1% of each run, Pallas kernels for 12% -> 14%
where the time goes in v5:
time: 98.4 us; the launch traced here: 97.8 us
  starting transfers between devices  57.3 us (58%)
  Pallas kernels  18.7 us (19%)
  blocking collectives  15.2 us (15%)
  waiting for transfers between devices  4.79 us (5%)
  local copies, waits for them, and re-layouts  1.4 us (1%)
    ppermute x4, starting transfers between devices, sent(): return lax.ppermute(v, CLU, pairs)  37.4 us
    all_to_all x1, blocking collectives, exchanged(): return lax.all_to_all(v, axis, split_axis=0, concat_axis=0, tiled=True)  15.2 us
    all_to_all x2, starting transfers between devices, exchanged(): return lax.all_to_all(v, axis, split_axis=0, concat_axis=0, tiled=True)  11.6 us
    ppermute x4, starting transfers between devices, swapped(): return lax.ppermute(v, 'clu_2', [(0, 1), (1, 0)])  8.29 us
    pallas_call x1, Pallas kernels, on_device(): pl.pallas_call(functools.partial(near_kernel, clusters), out_shape=shape_...  7.55 us
    all_to_all x2, waiting for transfers between devices, exchanged(): return lax.all_to_all(v, axis, split_axis=0, concat_axis=0, tiled=True)  3.51 us
    pallas_call x1, Pallas kernels, on_device(): pl.pallas_call(functools.partial(mix_kernel, planes), out_shape=shape_of(...  2.8 us
    pallas_call x1, Pallas kernels, on_device(): pl.pallas_call(functools.partial(couple_kernel, planes), out_shape=shape_...  2.08 us
  transfers between devices with their start and end apart: 10, of which 3 were waited for; matrix products, arithmetic and copies ran while one was open for 1% of the time, Pallas kernels for 14%

profile of v5, /device:TPU:32, one launch (start us, length us, event | category | flops | bytes accessed | tf_op | source)
XLA Modules:
  0.0 97.8 jit_solution(16478797759651727447)
XLA Ops:
  0.0 0.1 pad_add_fusion.sc
  0.1 1.8 %dress.1 = (bf16[784,128]{1,0:T(8,128)(2,1)S(1)}, bf16[784,512]{1,0:T(8,128)(2,1)S(1)}) custom-call(s32[4]{0:T(128)S(1)} %pad_add_fusion.sc, s32[1,256]{1,0:T(1,128)} %bitcast.19, bf16[768,512]{1,0:T(8,128)(2,1)} %bitcast.17), custom_call_target="tpu_custom_call" | custom-call | tf_op jit(solution)/shard_map/dress/pallas_call | solution.py:388
  1.9 0.0 copy-start.3
  1.9 0.0 copy-start.1
  2.0 2.1 %collective-permute-start.1 = (bf16[784,512]{1,0:T(8,128)(2,1)S(1)}, bf16[784,512]{1,0:T(8,128)(2,1)S(1)}, u32[]{:S(2)}, u32[]{:S(2)}) collective-permute-start(bf16[784,512]{1,0:T(8,128)(2,1)S(1)} %tie.2.own_ref.own), channel_id=1, source_target_pairs={{0,1},{1,0},{2,3},{3,2},{4,5},{5,4},{6,7},{7,6},{8,9},{9,8},{10,11... | collective-permute-start | bytes 2408456 | tf_op jit(solution)/shard_map/ppermute | solution.py:378
  4.0 7.5 %collective-permute-start = (bf16[784,128]{1,0:T(8,128)(2,1)S(1)}, bf16[784,128]{1,0:T(8,128)(2,1)S(1)}, u32[]{:S(2)}, u32[]{:S(2)}) collective-permute-start(bf16[784,128]{1,0:T(8,128)(2,1)S(1)} %get-tuple-element.10), channel_id=1, source_target_pairs={{0,127},{1,2},{2,1},{3,4},{4,3},{5,6},{6,5},{7,8},{8,7},{9,10},{10... | collective-permute-start | bytes 602120 | tf_op jit(solution)/shard_map/ppermute | solution.py:382
  11.5 8.2 %collective-permute-start.5 = (bf16[784,512]{1,0:T(8,128)(2,1)S(1)}, bf16[784,512]{1,0:T(8,128)(2,1)S(1)}, u32[]{:S(2)}, u32[]{:S(2)}) collective-permute-start(bf16[784,512]{1,0:T(8,128)(2,1)S(1)} %tie.2.own_ref.own), channel_id=1, source_target_pairs={{0,126},{1,3},{2,0},{3,5},{4,2},{5,7},{6,4},{7,9},{8,6},{9,11},{10... | collective-permute-start | bytes 2408456 | tf_op jit(solution)/shard_map/ppermute | solution.py:382
  19.7 1.9 %collective-permute-start.4 = (bf16[784,512]{1,0:T(8,128)(2,1)S(1)}, bf16[784,512]{1,0:T(8,128)(2,1)S(1)}, u32[]{:S(2)}, u32[]{:S(2)}) collective-permute-start(bf16[784,512]{1,0:T(8,128)(2,1)S(1)} %tie.2.own_ref.own), channel_id=1, source_target_pairs={{0,2},{1,127},{2,4},{3,1},{4,6},{5,3},{6,8},{7,5},{8,10},{9,7},{10... | collective-permute-start | bytes 2408456 | tf_op jit(solution)/shard_map/ppermute | solution.py:382
  21.7 0.0 collective-permute-done.halo_ref
  21.7 0.0 collective-permute-done.1.pair_ref.pair
  21.7 0.0 copy-start.2
  21.7 0.0 copy-done.3
  21.7 1.4 %pieces.1 = (f32[32,128]{1,0:T(8,128)S(1)}, f32[32,128]{1,0:T(8,128)S(1)}) custom-call(s32[4]{0:T(128)S(1)} %pad_add_fusion.sc, bf16[784,128]{1,0:T(8,128)(2,1)S(1)} %collective-permute-done.halo_ref, bf16[784,512]{1,0:T(8,128)(2,1)S(1)} %tie.2.own_ref.own, bf16[784,512]{1,0:T(8,128)(2,1)S(1)} %collective-permute-done.1.pair_ref.pair, ...), custom_call_target="tpu_custom_call" | custom-call | flops 10000000000 | bytes 1000000 | tf_op jit(solution)/shard_map/pieces/pallas_call | solution.py:407
  23.1 0.0 copy-done.2
  23.1 1.9 %collective-permute-start.2 = (f32[32,128]{1,0:T(8,128)S(1)}, f32[32,128]{1,0:T(8,128)S(1)}, u32[]{:S(2)}, u32[]{:S(2)}) collective-permute-start(f32[32,128]{1,0:T(8,128)S(1)} %get-tuple-element.12), channel_id=1, source_target_pairs={{0,1},{1,0},{2,3},{3,2},{4,5},{5,4},{6,7},{7,6},{8,9},{9,8},{10,11... | collective-permute-start | bytes 49160 | tf_op jit(solution)/shard_map/ppermute | solution.py:378
  25.1 1.1 %collective-permute-done.2 = f32[32,128]{1,0:T(8,128)S(1)} collective-permute-done((f32[32,128]{1,0:T(8,128)S(1)}, f32[32,128]{1,0:T(8,128)S(1)}, u32[]{:S(2)}, u32[]{:S(2)}) %collective-permute-start.2) | collective-permute-done | bytes 16416 | tf_op jit(solution)/shard_map/ppermute | solution.py:378
  26.2 0.7 broadcast_in_dim.3
  27.0 6.8 %all-to-all-start = ((f32[16,32,128]{2,1,0:T(8,128)}), f32[16,32,128]{2,1,0:T(8,128)S(1)}, u32[]{:S(2)}, u32[]{:S(2)}) async-start(f32[16,32,128]{2,1,0:T(8,128)} %broadcast_in_dim.3), calls=%async_computation | async-start | bytes 524288 | tf_op jit(solution)/shard_map/all_to_all | solution.py:385
  33.7 0.1 collective-permute-done.5.far_z.refs_2_
  33.8 1.9 %collective-permute-start.6 = (bf16[784,512]{1,0:T(8,128)(2,1)S(1)}, bf16[784,512]{1,0:T(8,128)(2,1)}, u32[]{:S(2)}, u32[]{:S(2)}) collective-permute-start(bf16[784,512]{1,0:T(8,128)(2,1)S(1)} %collective-permute-done.5.far_z.refs_2_), channel_id=1, source_target_pairs={{0,1},{1,0},{2,3},{3,2},{4,5},{5,4},{6,7},{7,6},{8,9},{9,8},{10,11... | collective-permute-start | bytes 2408456 | tf_op jit(solution)/shard_map/ppermute | solution.py:378
  35.8 0.0 collective-permute-done.4.near_z.refs_1_
  35.8 0.0 copy-start
  35.8 2.4 %collective-permute-start.7 = (bf16[784,512]{1,0:T(8,128)(2,1)S(1)}, bf16[784,512]{1,0:T(8,128)(2,1)}, u32[]{:S(2)}, u32[]{:S(2)}) collective-permute-start(bf16[784,512]{1,0:T(8,128)(2,1)S(1)} %collective-permute-done.4.near_z.refs_1_), channel_id=1, source_target_pairs={{0,1},{1,0},{2,3},{3,2},{4,5},{5,4},{6,7},{7,6},{8,9},{9,8},{10,11... | collective-permute-start | bytes 2408456 | tf_op jit(solution)/shard_map/ppermute | solution.py:378
  38.2 0.0 copy-done.1
  38.2 1.3 %thin.1 = bf16[3,64,512]{2,1,0:T(8,128)(2,1)S(1)} custom-call(s32[4]{0:T(128)S(1)} %pad_add_fusion.sc, bf16[784,128]{1,0:T(8,128)(2,1)S(1)} %collective-permute-done.halo_ref, bf16[784,512]{1,0:T(8,128)(2,1)S(1)} %tie.2.own_ref.own, f32[32,128]{1,0:T(8,128)S(1)} %add.11.after), custom_call_target="tpu_custom_call" | custom-call | tf_op jit(solution)/shard_map/thin/pallas_call | solution.py:418
  39.5 19.8 %collective-permute-start.3 = (bf16[3,64,512]{2,1,0:T(8,128)(2,1)S(1)}, bf16[3,64,512]{2,1,0:T(8,128)(2,1)S(1)}, u32[]{:S(2)}, u32[]{:S(2)}) collective-permute-start(bf16[3,64,512]{2,1,0:T(8,128)(2,1)S(1)} %thin.1), channel_id=1, source_target_pairs={{0,125},{1,4},{2,127},{3,6},{4,1},{5,8},{6,3},{7,10},{8,5},{9,12},... | collective-permute-start | bytes 589832 | tf_op jit(solution)/shard_map/ppermute | solution.py:382
  59.3 2.1 %couple.1.mixed = bf16[512,384]{1,0:T(8,128)(2,1)S(1)} custom-call(s32[4]{0:T(128)S(1)} %pad_add_fusion.sc, s32[16]{0:T(128)} %bitcast.20, s32[16]{0:T(128)} %bitcast.21, f32[16]{0:T(128)} %bitcast.22, bf16[16,32,32]{2,1,0:T(8,128)(2,1)} %bitcast.18, f32[32,128]{1,0:T(8,128)S(1)} %add.11.after), custom_call_target="tpu_custom_call" | custom-call | tf_op jit(solution)/shard_map/couple/pallas_call | solution.py:468
  61.4 0.0 all-to-all-done.refs_0_
  61.4 0.9 reduce.1
  62.3 0.0 copy-done
  62.3 4.9 %all-to-all-start.1 = ((f32[32,32,128]{2,1,0:T(8,128)}), f32[32,32,128]{2,1,0:T(8,128)S(1)}, u32[]{:S(2)}, u32[]{:S(2)}) async-start(f32[32,32,128]{2,1,0:T(8,128)} %reduce.1), calls=%async_computation.1 | async-start | bytes 1048576 | tf_op jit(solution)/shard_map/all_to_all | solution.py:385
  67.1 0.0 collective-permute-done.3.thin
  67.2 0.0 copy-start.4
  67.2 0.0 collective-permute-done.6.pair_far
  67.2 0.0 collective-permute-done.7.pair_near
  67.2 0.6 copy-done.4
  67.8 7.6 %near.1 = f32[768,512]{1,0:T(8,128)S(1)} custom-call(s32[4]{0:T(128)S(1)} %pad_add_fusion.sc, s32[2]{0:T(128)} %bitcast.24, bf16[2,768,768]{2,1,0:T(8,128)(2,1)} %bitcast.23, bf16[784,512]{1,0:T(8,128)(2,1)} %copy-done.1, bf16[3,64,512]{2,1,0:T(8,128)(2,1)} %copy-done.4, bf16[784,512]{1,0:T(8,128)(2,1)} %copy-done, ...), custom_call_target="tpu_custom_call" | custom-call | flops 12000000000 | bytes 1000000 | tf_op jit(solution)/shard_map/near/pallas_call | solution.py:445
  75.4 3.5 %all-to-all-done.1.sums = f32[32,32,128]{2,1,0:T(8,128)S(1)} async-done(((f32[32,32,128]{2,1,0:T(8,128)}), f32[32,32,128]{2,1,0:T(8,128)S(1)}, u32[]{:S(2)}, u32[]{:S(2)}) %all-to-all-start.1) | async-done | bytes 524320 | tf_op jit(solution)/shard_map/all_to_all | solution.py:385
  78.9 2.8 %mix.1 = bf16[4,768,128]{2,1,0:T(8,128)(2,1)S(1)} custom-call(s32[4]{0:T(128)S(1)} %pad_add_fusion.sc, f32[768,512]{1,0:T(8,128)S(1)} %near.1, f32[32,32,128]{2,1,0:T(8,128)S(1)} %all-to-all-done.1.sums, bf16[512,768]{1,0:T(8,128)(2,1)} %bitcast.16, bf16[512,384]{1,0:T(8,128)(2,1)S(1)} %couple.1.mixed), custom_call_target="tpu_custom_call" | custom-call | tf_op jit(solution)/shard_map/mix/pallas_call | solution.py:481
  81.7 15.2 %all_to_all.15.arrived_ref = bf16[4,768,128]{2,1,0:T(8,128)(2,1)S(1)} all-to-all(bf16[4,768,128]{2,1,0:T(8,128)(2,1)S(1)} %mix.1), channel_id=1, replica_groups=mesh['grp'=4,'clu_0'=4,'clu_1'=16,'clu_2'=2] {'grp'}, dimensions={0} | all-to-all | bytes 1572864 | tf_op jit(solution)/shard_map/all_to_all | solution.py:385
  96.9 0.8 last.1
  (3 shorter events, 0.0 us)
Async XLA Ops:
  1.9 19.8 %copy-start.3 = (bf16[2,32,3,256]{3,1,2,0:T(8,128)(2,1)S(1)}, bf16[2,32,3,256]{3,1,2,0:T(8,128)(2,1)}, u32[]{:S(2)}) copy-start(bf16[2,32,3,256]{3,1,2,0:T(8,128)(2,1)} %param.12) | copy-start | bytes 294916
  1.9 36.2 %copy-start.1 = (bf16[784,512]{1,0:T(8,128)(2,1)}, bf16[784,512]{1,0:T(8,128)(2,1)S(1)}, u32[]{:S(2)}) copy-start(bf16[784,512]{1,0:T(8,128)(2,1)S(1)} %tie.2.own_ref.own) | copy-start | bytes 2408452
  2.0 19.7 %collective-permute-start.1 = (bf16[784,512]{1,0:T(8,128)(2,1)S(1)}, bf16[784,512]{1,0:T(8,128)(2,1)S(1)}, u32[]{:S(2)}, u32[]{:S(2)}) collective-permute-start(bf16[784,512]{1,0:T(8,128)(2,1)S(1)} %tie.2.own_ref.own), channel_id=1, source_target_pairs={{0,1},{1,0},{2,3},{3,2},{4,5},{5,4},{6,7},{7,6},{8,9},{9,8},{10,11... | collective-permute-start | bytes 2408456 | tf_op jit(solution)/shard_map/ppermute | solution.py:378
  4.0 17.7 %collective-permute-start = (bf16[784,128]{1,0:T(8,128)(2,1)S(1)}, bf16[784,128]{1,0:T(8,128)(2,1)S(1)}, u32[]{:S(2)}, u32[]{:S(2)}) collective-permute-start(bf16[784,128]{1,0:T(8,128)(2,1)S(1)} %get-tuple-element.10), channel_id=1, source_target_pairs={{0,127},{1,2},{2,1},{3,4},{4,3},{5,6},{6,5},{7,8},{8,7},{9,10},{10... | collective-permute-start | bytes 602120 | tf_op jit(solution)/shard_map/ppermute | solution.py:382
  11.5 22.3 %collective-permute-start.5 = (bf16[784,512]{1,0:T(8,128)(2,1)S(1)}, bf16[784,512]{1,0:T(8,128)(2,1)S(1)}, u32[]{:S(2)}, u32[]{:S(2)}) collective-permute-start(bf16[784,512]{1,0:T(8,128)(2,1)S(1)} %tie.2.own_ref.own), channel_id=1, source_target_pairs={{0,126},{1,3},{2,0},{3,5},{4,2},{5,7},{6,4},{7,9},{8,6},{9,11},{10... | collective-permute-start | bytes 2408456 | tf_op jit(solution)/shard_map/ppermute | solution.py:382
  19.7 16.0 %collective-permute-start.4 = (bf16[784,512]{1,0:T(8,128)(2,1)S(1)}, bf16[784,512]{1,0:T(8,128)(2,1)S(1)}, u32[]{:S(2)}, u32[]{:S(2)}) collective-permute-start(bf16[784,512]{1,0:T(8,128)(2,1)S(1)} %tie.2.own_ref.own), channel_id=1, source_target_pairs={{0,2},{1,127},{2,4},{3,1},{4,6},{5,3},{6,8},{7,5},{8,10},{9,7},{10... | collective-permute-start | bytes 2408456 | tf_op jit(solution)/shard_map/ppermute | solution.py:382
  21.7 1.4 %copy-start.2 = (bf16[784,512]{1,0:T(8,128)(2,1)}, bf16[784,512]{1,0:T(8,128)(2,1)S(1)}, u32[]{:S(2)}) copy-start(bf16[784,512]{1,0:T(8,128)(2,1)S(1)} %collective-permute-done.1.pair_ref.pair) | copy-start | bytes 2408452
  23.1 3.1 %collective-permute-start.2 = (f32[32,128]{1,0:T(8,128)S(1)}, f32[32,128]{1,0:T(8,128)S(1)}, u32[]{:S(2)}, u32[]{:S(2)}) collective-permute-start(f32[32,128]{1,0:T(8,128)S(1)} %get-tuple-element.12), channel_id=1, source_target_pairs={{0,1},{1,0},{2,3},{3,2},{4,5},{5,4},{6,7},{7,6},{8,9},{9,8},{10,11... | collective-permute-start | bytes 49160 | tf_op jit(solution)/shard_map/ppermute | solution.py:378
  27.0 34.4 %all-to-all-start = ((f32[16,32,128]{2,1,0:T(8,128)}), f32[16,32,128]{2,1,0:T(8,128)S(1)}, u32[]{:S(2)}, u32[]{:S(2)}) async-start(f32[16,32,128]{2,1,0:T(8,128)} %broadcast_in_dim.3), calls=%async_computation | async-start | bytes 524288 | tf_op jit(solution)/shard_map/all_to_all | solution.py:385
  33.8 33.3 %collective-permute-start.6 = (bf16[784,512]{1,0:T(8,128)(2,1)S(1)}, bf16[784,512]{1,0:T(8,128)(2,1)}, u32[]{:S(2)}, u32[]{:S(2)}) collective-permute-start(bf16[784,512]{1,0:T(8,128)(2,1)S(1)} %collective-permute-done.5.far_z.refs_2_), channel_id=1, source_target_pairs={{0,1},{1,0},{2,3},{3,2},{4,5},{5,4},{6,7},{7,6},{8,9},{9,8},{10,11... | collective-permute-start | bytes 2408456 | tf_op jit(solution)/shard_map/ppermute | solution.py:378
  35.8 26.5 %copy-start = (bf16[784,512]{1,0:T(8,128)(2,1)}, bf16[784,512]{1,0:T(8,128)(2,1)S(1)}, u32[]{:S(2)}) copy-start(bf16[784,512]{1,0:T(8,128)(2,1)S(1)} %collective-permute-done.4.near_z.refs_1_) | copy-start | bytes 2408452
  35.8 31.4 %collective-permute-start.7 = (bf16[784,512]{1,0:T(8,128)(2,1)S(1)}, bf16[784,512]{1,0:T(8,128)(2,1)}, u32[]{:S(2)}, u32[]{:S(2)}) collective-permute-start(bf16[784,512]{1,0:T(8,128)(2,1)S(1)} %collective-permute-done.4.near_z.refs_1_), channel_id=1, source_target_pairs={{0,1},{1,0},{2,3},{3,2},{4,5},{5,4},{6,7},{7,6},{8,9},{9,8},{10,11... | collective-permute-start | bytes 2408456 | tf_op jit(solution)/shard_map/ppermute | solution.py:378
  39.5 27.7 %collective-permute-start.3 = (bf16[3,64,512]{2,1,0:T(8,128)(2,1)S(1)}, bf16[3,64,512]{2,1,0:T(8,128)(2,1)S(1)}, u32[]{:S(2)}, u32[]{:S(2)}) collective-permute-start(bf16[3,64,512]{2,1,0:T(8,128)(2,1)S(1)} %thin.1), channel_id=1, source_target_pairs={{0,125},{1,4},{2,127},{3,6},{4,1},{5,8},{6,3},{7,10},{8,5},{9,12},... | collective-permute-start | bytes 589832 | tf_op jit(solution)/shard_map/ppermute | solution.py:382
  62.3 16.6 %all-to-all-start.1 = ((f32[32,32,128]{2,1,0:T(8,128)}), f32[32,32,128]{2,1,0:T(8,128)S(1)}, u32[]{:S(2)}, u32[]{:S(2)}) async-start(f32[32,32,128]{2,1,0:T(8,128)} %reduce.1), calls=%async_computation.1 | async-start | bytes 1048576 | tf_op jit(solution)/shard_map/all_to_all | solution.py:385
  67.2 0.7 copy-start.4

commit v6 on v5

--- a/solution.py
+++ b/solution.py
@@ -139,22 +139,26 @@
     copy.wait()
 
 
+def offsets_of(clusters, sc, near_col, count):
+    offs = []
+    for j in range(count):
+        off = near_col[j] - sc[3] + 2
+        off = jnp.where(off < 0, off + clusters, off)
+        off = jnp.where(off >= clusters, off - clusters, off) - 2
+        offs.append(jnp.where(sc[0] == 0, off, -off))
+    return offs
+
+
 def near_kernel(
-    clusters, sc, near_col, tiles, own, thin, near_z, pair_far, pair, far_z, pair_near,
+    clusters, sc, near_col, tiles, own, near_z, pair_far, pair, far_z, pair_near,
     total, tile_ref, tails, window, blocks, total_ref, sems, tail_sems, tile_sems, out_sems,
 ):
     count, rows, _ = tiles.shape
     columns = own.shape[1]
     size = rows // 3
-    quarter = size // 4
     core = sc[0]
-    seats = (thin, near_z, pair_far, own, pair, far_z, pair_near)
-    offs = []
-    for j in range(count):
-        off = near_col[j] - sc[3] + 2
-        off = jnp.where(off < 0, off + clusters, off)
-        off = jnp.where(off >= clusters, off - clusters, off) - 2
-        offs.append(jnp.where(core == 0, off, -off))
+    seats = (None, near_z, pair_far, own, pair, far_z, pair_near)
+    offs = offsets_of(clusters, sc, near_col, count)
     for j in range(count):
         for o in range(-2, 3):
 
@@ -164,15 +168,8 @@
                 for comp in range(3):
                     for w in range(3):
                         source = seats[o + 2 + w]
-                        if o + w == -2:
-                            pltpu.make_async_copy(
-                                source.at[comp],
-                                window.at[j, comp, pl.ds(w * size, quarter)],
-                                sems.at[j, comp, w],
-                            ).start()
-                            window[j, comp, w * size + quarter : (w + 1) * size] = jnp.zeros(
-                                (size - quarter, columns), BF16
-                            )
+                        if source is None:
+                            window[j, comp, :size] = jnp.zeros((size, columns), BF16)
                         else:
                             pltpu.make_async_copy(
                                 source.at[pl.ds(comp * size, size)],
@@ -190,17 +187,8 @@
         tail = tails[j].astype(F32)
         low, high = tail[0:1, :size], tail[1:2, :size]
         seat = jnp.where(core == 0, high, 2.0 - high)
-        first = seat == 0.0
-        place = count_before(first.astype(F32))
-        low = jnp.where(jnp.logical_and(first, edge), place, low)
         pick = chosen(as_column(seat * size + low), 3 * size)
         for comp in range(3):
-
-            @pl.when(edge)
-            def _(j=j, comp=comp):
-                pltpu.make_async_copy(
-                    thin.at[comp], window.at[j, comp, pl.ds(0, quarter)], sems.at[j, comp, 0]
-                ).wait()
 
             @pl.when(jnp.logical_not(edge))
             def _(j=j, comp=comp):
@@ -267,13 +255,40 @@
 
 
 def mix_kernel(
-    planes, sc, near, sums, basis, mixed, split,
-    near_ref, sums_ref, basis_ref, mixed_ref, table_ref, stack_ref, coupled_ref, result, in_sems, sems,
+    clusters, planes, sc, near_col, near, sums, basis, mixed, tiles, thin, near_z, split,
+    near_ref, sums_ref, basis_ref, mixed_ref, table_ref, stack_ref, coupled_ref, result,
+    tile_ref, thin_ref, tail_ref, edge_ref, in_sems, sems, tile_sems, edge_sems,
 ):
+    count, rows, _ = tiles.shape
+    offs = offsets_of(clusters, sc, near_col, count)
+    edges = [off == -2 for off in offs]
+    some = functools.reduce(jnp.logical_or, edges)
+
+    def edge_copies():
+        return (
+            pltpu.make_async_copy(thin, thin_ref, edge_sems.at[0]),
+            pltpu.make_async_copy(near_z.at[pl.ds(rows, PAD)], tail_ref, edge_sems.at[1]),
+        )
+
+    def tile_copy(j):
+        return pltpu.make_async_copy(tiles.at[j], tile_ref.at[j], tile_sems.at[j])
+
     pairs = ((sums, sums_ref), (basis, basis_ref), (near, near_ref), (mixed, mixed_ref))
     copies = [pltpu.make_async_copy(a, b, in_sems.at[i]) for i, (a, b) in enumerate(pairs)]
     for copy in copies:
         copy.start()
+
+    @pl.when(some)
+    def _():
+        for copy in edge_copies():
+            copy.start()
+
+    for j in range(count):
+
+        @pl.when(edges[j])
+        def _(j=j):
+            tile_copy(j).start()
+
     copies[0].wait()
     groups, rows, part = split.shape
     rank = sums_ref.shape[1]
@@ -303,8 +318,29 @@
         coupled_ref[span] = dot(mixed_ref[span], stack_ref[...]).astype(BF16)
     copies[1].wait()
     copies[2].wait()
+    size = rows // 3
+
+    @pl.when(some)
+    def _():
+        for copy in edge_copies():
+            copy.wait()
+        tail = tail_ref[...].astype(F32)
+        first = tail[1:2, :size] == jnp.where(sc[0] == 0, 0.0, 2.0)
+        place = jnp.where(first, count_before(first.astype(F32)), -1.0)
+        pick = chosen(as_column(place), size // 4)
+        for comp in range(3):
+            edge_ref[comp * size : (comp + 1) * size] = dot(pick, thin_ref[comp]).astype(BF16)
+
+    for j in range(count):
+
+        @pl.when(edges[j])
+        def _(j=j):
+            tile_copy(j).wait()
+            for r in range(3):
+                span = slice(r * size, (r + 1) * size)
+                near_ref[span] += dot(tile_ref[j, span], edge_ref[...])
+
     outs = []
-    size = rows // 3
     for r in range(3):
         span = slice(r * size, (r + 1) * size)
         total = near_ref[span] + lax.dot_general(
@@ -427,8 +463,21 @@
         compiler_params=params(12),
         name="thin",
     )(sc, halo, block, level_sum)
+    mixed = pl.pallas_call(
+        functools.partial(couple_kernel, planes),
+        out_shape=shape_of((far_count * rank, 3 * width), BF16),
+        in_specs=[SMEM, SMEM, SMEM, SMEM, HBM, ANY],
+        out_specs=HBM,
+        scratch_shapes=[
+            pltpu.VMEM((far_count, rank, rank), BF16),
+            pltpu.VMEM((far_count * rank, 3 * width), BF16),
+            pltpu.SemaphoreType.DMA((2,)),
+        ],
+        compiler_params=params(4),
+        name="couple",
+    )(sc, *in_hbm(far_target[0], far_rank[0], far_scale[0], far_coupling[0]), level_sum)
+    many = tied(many, near_z, far_z, thin, mixed)
     thin = sent(thin, 3)
-    many = tied(many, near_z, far_z)
     pair_near = swapped(near_z)
     pair_far = swapped(far_z)
     fan = groups * 2 * planes
@@ -445,7 +494,7 @@
     near = pl.pallas_call(
         functools.partial(near_kernel, clusters),
         out_shape=shape_of((rows, columns), F32),
-        in_specs=[SMEM, SMEM, HBM] + [ANY] * 7,
+        in_specs=[SMEM, SMEM, HBM] + [ANY] * 6,
         out_specs=HBM,
         scratch_shapes=[
             pltpu.VMEM((rows, count * rows), BF16),
@@ -459,29 +508,16 @@
             pltpu.SemaphoreType.DMA((3,)),
         ],
         compiler_params=params(48),
-        cost_estimate=cost_of(12 * 10**9),
+        cost_estimate=cost_of(4 * 10**9),
         name="near",
     )(
         sc, *in_hbm(near_col[0], near_tiles[0]),
-        *in_hbm(block), *in_hbm(thin), *in_hbm(near_z), pair_far, *in_hbm(pair), far_z, pair_near,
+        *in_hbm(block, near_z), pair_far, *in_hbm(pair, far_z), pair_near,
     )
-    mixed = pl.pallas_call(
-        functools.partial(couple_kernel, planes),
-        out_shape=shape_of((far_count * rank, 3 * width), BF16),
-        in_specs=[SMEM, SMEM, SMEM, SMEM, HBM, ANY],
-        out_specs=HBM,
-        scratch_shapes=[
-            pltpu.VMEM((far_count, rank, rank), BF16),
-            pltpu.VMEM((far_count * rank, 3 * width), BF16),
-            pltpu.SemaphoreType.DMA((2,)),
-        ],
-        compiler_params=params(4),
-        name="couple",
-    )(sc, *in_hbm(far_target[0], far_rank[0], far_scale[0], far_coupling[0]), level_sum)
     split = pl.pallas_call(
-        functools.partial(mix_kernel, planes),
+        functools.partial(mix_kernel, clusters, planes),
         out_shape=shape_of((groups, rows, part), BF16),
-        in_specs=[SMEM, ANY, ANY, HBM, ANY],
+        in_specs=[SMEM, SMEM, ANY, ANY, HBM, ANY, HBM, HBM, HBM],
         out_specs=HBM,
         scratch_shapes=[
             pltpu.VMEM((rows, columns), F32),
@@ -492,12 +528,21 @@
             pltpu.VMEM((3 * width, columns), BF16),
             pltpu.VMEM((far_count * rank, columns), BF16),
             pltpu.VMEM((groups, rows, part), BF16),
+            pltpu.VMEM((count, rows, rows), BF16),
+            pltpu.VMEM((comps, size // 4, columns), BF16),
+            pltpu.VMEM((PAD, columns), BF16),
+            pltpu.VMEM((rows, columns), BF16),
             pltpu.SemaphoreType.DMA((4,)),
             pltpu.SemaphoreType.DMA((3,)),
+            pltpu.SemaphoreType.DMA((count,)),
+            pltpu.SemaphoreType.DMA((2,)),
         ],
-        compiler_params=params(16),
+        compiler_params=params(24),
         name="mix",
-    )(sc, near, sums, *in_hbm(far_basis.reshape(far_count * rank, rows)), mixed)
+    )(
+        sc, *in_hbm(near_col[0]), near, sums, *in_hbm(far_basis.reshape(far_count * rank, rows)), mixed,
+        *in_hbm(near_tiles[0], thin, near_z),
+    )
     arrived = exchanged(split, "grp")
     velocity = pl.pallas_call(
         last_kernel,

time: 98.4 us -> 99.3 us (level)
  the two profiles are of different devices: /device:TPU:32 before, /device:TPU:2 now
where the time goes in v6:
time: 99.3 us; the launch traced here: 98.6 us
  starting transfers between devices  48 us (48%)
  Pallas kernels  17.9 us (18%)
  blocking collectives  17.4 us (18%)
  waiting for transfers between devices  14.2 us (14%)
    ppermute x4, starting transfers between devices, sent(): return lax.ppermute(v, CLU, pairs)  21.4 us
    all_to_all x2, starting transfers between devices, exchanged(): return lax.all_to_all(v, axis, split_axis=0, concat_axis=0, tiled=True)  18.3 us
    all_to_all x1, blocking collectives, exchanged(): return lax.all_to_all(v, axis, split_axis=0, concat_axis=0, tiled=True)  17.4 us
    ppermute x4, waiting for transfers between devices, sent(): return lax.ppermute(v, CLU, pairs)  12.7 us
    ppermute x4, starting transfers between devices, swapped(): return lax.ppermute(v, 'clu_2', [(0, 1), (1, 0)])  8.29 us
    pallas_call x1, Pallas kernels, on_device(): pl.pallas_call(functools.partial(near_kernel, clusters), out_shape=shape_...  6.59 us
    pallas_call x1, Pallas kernels, on_device(): pl.pallas_call(functools.partial(mix_kernel, clusters, planes), out_shape...  2.98 us
    pallas_call x1, Pallas kernels, on_device(): pl.pallas_call(functools.partial(couple_kernel, planes), out_shape=shape_...  2.08 us
  transfers between devices with their start and end apart: 10, of which 4 were waited for; matrix products, arithmetic and copies ran while one was open for 1% of the time, Pallas kernels for 12%

profile of v6, /device:TPU:2, one launch (start us, length us, event | category | flops | bytes accessed | tf_op | source)
XLA Modules:
  0.0 98.6 jit_solution(1393715735636969753)
XLA Ops:
  0.0 0.1 pad_add_fusion.sc
  0.1 1.8 %dress.1 = (bf16[784,128]{1,0:T(8,128)(2,1)S(1)}, bf16[784,512]{1,0:T(8,128)(2,1)S(1)}) custom-call(s32[4]{0:T(128)S(1)} %pad_add_fusion.sc, s32[1,256]{1,0:T(1,128)} %bitcast.21, bf16[768,512]{1,0:T(8,128)(2,1)} %bitcast.18), custom_call_target="tpu_custom_call" | custom-call | tf_op jit(solution)/shard_map/dress/pallas_call | solution.py:424
  1.9 0.0 copy-start.4
  1.9 0.0 copy-start.2
  2.0 2.1 %collective-permute-start.3 = (bf16[784,512]{1,0:T(8,128)(2,1)S(1)}, bf16[784,512]{1,0:T(8,128)(2,1)S(1)}, u32[]{:S(2)}, u32[]{:S(2)}) collective-permute-start(bf16[784,512]{1,0:T(8,128)(2,1)S(1)} %tie.2.own.own_ref), channel_id=1, source_target_pairs={{0,1},{1,0},{2,3},{3,2},{4,5},{5,4},{6,7},{7,6},{8,9},{9,8},{10,11... | collective-permute-start | bytes 2408456 | tf_op jit(solution)/shard_map/ppermute | solution.py:414
  4.0 11.5 %collective-permute-start.5 = (bf16[784,128]{1,0:T(8,128)(2,1)S(1)}, bf16[784,128]{1,0:T(8,128)(2,1)S(1)}, u32[]{:S(2)}, u32[]{:S(2)}) collective-permute-start(bf16[784,128]{1,0:T(8,128)(2,1)S(1)} %get-tuple-element.10), channel_id=1, source_target_pairs={{0,127},{1,2},{2,1},{3,4},{4,3},{5,6},{6,5},{7,8},{8,7},{9,10},{10... | collective-permute-start | bytes 602120 | tf_op jit(solution)/shard_map/ppermute | solution.py:418
  15.5 1.9 %collective-permute-start = (bf16[784,512]{1,0:T(8,128)(2,1)S(1)}, bf16[784,512]{1,0:T(8,128)(2,1)S(1)}, u32[]{:S(2)}, u32[]{:S(2)}) collective-permute-start(bf16[784,512]{1,0:T(8,128)(2,1)S(1)} %tie.2.own.own_ref), channel_id=1, source_target_pairs={{0,2},{1,127},{2,4},{3,1},{4,6},{5,3},{6,8},{7,5},{8,10},{9,7},{10... | collective-permute-start | bytes 2408456 | tf_op jit(solution)/shard_map/ppermute | solution.py:418
  17.4 6.0 %collective-permute-start.1 = (bf16[784,512]{1,0:T(8,128)(2,1)S(1)}, bf16[784,512]{1,0:T(8,128)(2,1)S(1)}, u32[]{:S(2)}, u32[]{:S(2)}) collective-permute-start(bf16[784,512]{1,0:T(8,128)(2,1)S(1)} %tie.2.own.own_ref), channel_id=1, source_target_pairs={{0,126},{1,3},{2,0},{3,5},{4,2},{5,7},{6,4},{7,9},{8,6},{9,11},{10... | collective-permute-start | bytes 2408456 | tf_op jit(solution)/shard_map/ppermute | solution.py:418
  23.5 0.0 collective-permute-done.5.halo_ref
  23.5 0.0 collective-permute-done.3.pair.pair_ref
  23.5 0.0 copy-start.3
  23.5 0.0 copy-done.4
  23.5 1.4 %pieces.1 = (f32[32,128]{1,0:T(8,128)S(1)}, f32[32,128]{1,0:T(8,128)S(1)}) custom-call(s32[4]{0:T(128)S(1)} %pad_add_fusion.sc, bf16[784,128]{1,0:T(8,128)(2,1)S(1)} %collective-permute-done.5.halo_ref, bf16[784,512]{1,0:T(8,128)(2,1)S(1)} %tie.2.own.own_ref, bf16[784,512]{1,0:T(8,128)(2,1)S(1)} %collective-permute-done.3.pair.pair_ref, ...), custom_call_target="tpu_custom_call" | custom-call | flops 10000000000 | bytes 1000000 | tf_op jit(solution)/shard_map/pieces/pallas_call | solution.py:443
  24.9 0.0 copy-done.3
  24.9 1.9 %collective-permute-start.6 = (f32[32,128]{1,0:T(8,128)S(1)}, f32[32,128]{1,0:T(8,128)S(1)}, u32[]{:S(2)}, u32[]{:S(2)}) collective-permute-start(f32[32,128]{1,0:T(8,128)S(1)} %get-tuple-element.12), channel_id=1, source_target_pairs={{0,1},{1,0},{2,3},{3,2},{4,5},{5,4},{6,7},{7,6},{8,9},{9,8},{10,11... | collective-permute-start | bytes 49160 | tf_op jit(solution)/shard_map/ppermute | solution.py:414
  26.9 1.1 %collective-permute-done.6 = f32[32,128]{1,0:T(8,128)S(1)} collective-permute-done((f32[32,128]{1,0:T(8,128)S(1)}, f32[32,128]{1,0:T(8,128)S(1)}, u32[]{:S(2)}, u32[]{:S(2)}) %collective-permute-start.6) | collective-permute-done | bytes 16416 | tf_op jit(solution)/shard_map/ppermute | solution.py:414
  28.0 0.7 broadcast_in_dim.3
  28.8 4.9 %all-to-all-start = ((f32[16,32,128]{2,1,0:T(8,128)}), f32[16,32,128]{2,1,0:T(8,128)S(1)}, u32[]{:S(2)}, u32[]{:S(2)}) async-start(f32[16,32,128]{2,1,0:T(8,128)} %broadcast_in_dim.3), calls=%async_computation | async-start | bytes 524288 | tf_op jit(solution)/shard_map/all_to_all | solution.py:421
  33.7 11.1 %collective-permute-done.1.far_z.refs_2_ = bf16[784,512]{1,0:T(8,128)(2,1)S(1)} collective-permute-done((bf16[784,512]{1,0:T(8,128)(2,1)S(1)}, bf16[784,512]{1,0:T(8,128)(2,1)S(1)}, u32[]{:S(2)}, u32[]{:S(2)}) %collective-permute-start.1) | collective-permute-done | bytes 802848 | tf_op jit(solution)/shard_map/ppermute | solution.py:418
  44.8 0.0 copy-start.1
  44.8 1.9 %collective-permute-start.2 = (bf16[784,512]{1,0:T(8,128)(2,1)S(1)}, bf16[784,512]{1,0:T(8,128)(2,1)}, u32[]{:S(2)}, u32[]{:S(2)}) collective-permute-start(bf16[784,512]{1,0:T(8,128)(2,1)S(1)} %collective-permute-done.1.far_z.refs_2_), channel_id=1, source_target_pairs={{0,1},{1,0},{2,3},{3,2},{4,5},{5,4},{6,7},{7,6},{8,9},{9,8},{10,11... | collective-permute-start | bytes 2408456 | tf_op jit(solution)/shard_map/ppermute | solution.py:414
  46.7 0.0 collective-permute-done.near_z.refs_1_
  46.8 0.0 copy-start
  46.8 2.4 %collective-permute-start.4 = (bf16[784,512]{1,0:T(8,128)(2,1)S(1)}, bf16[784,512]{1,0:T(8,128)(2,1)}, u32[]{:S(2)}, u32[]{:S(2)}) collective-permute-start(bf16[784,512]{1,0:T(8,128)(2,1)S(1)} %collective-permute-done.near_z.refs_1_), channel_id=1, source_target_pairs={{0,1},{1,0},{2,3},{3,2},{4,5},{5,4},{6,7},{7,6},{8,9},{9,8},{10,11... | collective-permute-start | bytes 2408456 | tf_op jit(solution)/shard_map/ppermute | solution.py:414
  49.2 2.1 %couple.1.refs_4_.mixed = bf16[512,384]{1,0:T(8,128)(2,1)S(1)} custom-call(s32[4]{0:T(128)S(1)} %pad_add_fusion.sc, s32[16]{0:T(128)} %bitcast.24, s32[16]{0:T(128)} %bitcast.25, f32[16]{0:T(128)} %bitcast.26, bf16[16,32,32]{2,1,0:T(8,128)(2,1)} %bitcast.20, f32[32,128]{1,0:T(8,128)S(1)} %add.11.after), custom_call_target="tpu_custom_call" | custom-call | tf_op jit(solution)/shard_map/couple/pallas_call | solution.py:466
  51.3 0.0 copy-done.2
  51.3 1.3 %thin.1.refs_3_ = bf16[3,64,512]{2,1,0:T(8,128)(2,1)S(1)} custom-call(s32[4]{0:T(128)S(1)} %pad_add_fusion.sc, bf16[784,128]{1,0:T(8,128)(2,1)S(1)} %collective-permute-done.5.halo_ref, bf16[784,512]{1,0:T(8,128)(2,1)S(1)} %tie.2.own.own_ref, f32[32,128]{1,0:T(8,128)S(1)} %add.11.after), custom_call_target="tpu_custom_call" | custom-call | tf_op jit(solution)/shard_map/thin/pallas_call | solution.py:454
  52.6 0.0 all-to-all-done.refs_0_
  52.6 0.9 reduce.1
  53.5 0.0 copy-done.1
  53.5 0.0 copy-done
  53.5 13.4 %all-to-all-start.1 = ((f32[32,32,128]{2,1,0:T(8,128)}), f32[32,32,128]{2,1,0:T(8,128)S(1)}, u32[]{:S(2)}, u32[]{:S(2)}) async-start(f32[32,32,128]{2,1,0:T(8,128)} %reduce.1), calls=%async_computation.1 | async-start | bytes 1048576 | tf_op jit(solution)/shard_map/all_to_all | solution.py:421
  66.9 1.9 %collective-permute-start.7 = (bf16[3,64,512]{2,1,0:T(8,128)(2,1)S(1)}, bf16[3,64,512]{2,1,0:T(8,128)(2,1)}, u32[]{:S(2)}, u32[]{:S(2)}) collective-permute-start(bf16[3,64,512]{2,1,0:T(8,128)(2,1)S(1)} %thin.1.refs_3_), channel_id=1, source_target_pairs={{0,125},{1,4},{2,127},{3,6},{4,1},{5,8},{6,3},{7,10},{8,5},{9,12},... | collective-permute-start | bytes 589832 | tf_op jit(solution)/shard_map/ppermute | solution.py:418
  68.8 0.0 collective-permute-done.2.pair_far
  68.8 0.0 collective-permute-done.4.pair_near
  68.9 6.6 %near.1 = f32[768,512]{1,0:T(8,128)S(1)} custom-call(s32[4]{0:T(128)S(1)} %pad_add_fusion.sc, s32[2]{0:T(128)} %bitcast.22, bf16[2,768,768]{2,1,0:T(8,128)(2,1)} %bitcast.16, bf16[784,512]{1,0:T(8,128)(2,1)} %copy-done.2, bf16[784,512]{1,0:T(8,128)(2,1)} %copy-done, bf16[784,512]{1,0:T(8,128)(2,1)} %collective-permute-done.2.pair_far, ...), custom_call_target="tpu_custom_call" | custom-call | flops 4000000000 | bytes 1000000 | tf_op jit(solution)/shard_map/near/pallas_call | solution.py:494
  75.5 1.6 %collective-permute-done.7.thin = bf16[3,64,512]{2,1,0:T(8,128)(2,1)} collective-permute-done((bf16[3,64,512]{2,1,0:T(8,128)(2,1)S(1)}, bf16[3,64,512]{2,1,0:T(8,128)(2,1)}, u32[]{:S(2)}, u32[]{:S(2)}) %collective-permute-start.7) | collective-permute-done | bytes 196640 | tf_op jit(solution)/shard_map/ppermute | solution.py:418
  77.0 0.4 all-to-all-done.1.sums
  77.4 3.0 %mix.1 = bf16[4,768,128]{2,1,0:T(8,128)(2,1)S(1)} custom-call(s32[4]{0:T(128)S(1)} %pad_add_fusion.sc, s32[2]{0:T(128)} %bitcast.23, f32[768,512]{1,0:T(8,128)S(1)} %near.1, f32[32,32,128]{2,1,0:T(8,128)S(1)} %all-to-all-done.1.sums, bf16[512,768]{1,0:T(8,128)(2,1)} %bitcast.19, bf16[512,384]{1,0:T(8,128)(2,1)S(1)} %couple.1.refs_4_.mixed, ...), custom_call_target="tpu_custom_call" | custom-call | tf_op jit(solution)/shard_map/mix/pallas_call | solution.py:517
  80.4 17.4 %all_to_all.15.arrived_ref = bf16[4,768,128]{2,1,0:T(8,128)(2,1)S(1)} all-to-all(bf16[4,768,128]{2,1,0:T(8,128)(2,1)S(1)} %mix.1), channel_id=1, replica_groups=mesh['grp'=4,'clu_0'=4,'clu_1'=16,'clu_2'=2] {'grp'}, dimensions={0} | all-to-all | bytes 1572864 | tf_op jit(solution)/shard_map/all_to_all | solution.py:421
  97.8 0.8 last.1
  (3 shorter events, 0.0 us)
Async XLA Ops:
  1.9 21.6 %copy-start.4 = (bf16[2,32,3,256]{3,1,2,0:T(8,128)(2,1)S(1)}, bf16[2,32,3,256]{3,1,2,0:T(8,128)(2,1)}, u32[]{:S(2)}) copy-start(bf16[2,32,3,256]{3,1,2,0:T(8,128)(2,1)} %param.12) | copy-start | bytes 294916
  1.9 49.3 %copy-start.2 = (bf16[784,512]{1,0:T(8,128)(2,1)}, bf16[784,512]{1,0:T(8,128)(2,1)S(1)}, u32[]{:S(2)}) copy-start(bf16[784,512]{1,0:T(8,128)(2,1)S(1)} %tie.2.own.own_ref) | copy-start | bytes 2408452
  2.0 21.5 %collective-permute-start.3 = (bf16[784,512]{1,0:T(8,128)(2,1)S(1)}, bf16[784,512]{1,0:T(8,128)(2,1)S(1)}, u32[]{:S(2)}, u32[]{:S(2)}) collective-permute-start(bf16[784,512]{1,0:T(8,128)(2,1)S(1)} %tie.2.own.own_ref), channel_id=1, source_target_pairs={{0,1},{1,0},{2,3},{3,2},{4,5},{5,4},{6,7},{7,6},{8,9},{9,8},{10,11... | collective-permute-start | bytes 2408456 | tf_op jit(solution)/shard_map/ppermute | solution.py:414
  4.0 19.5 %collective-permute-start.5 = (bf16[784,128]{1,0:T(8,128)(2,1)S(1)}, bf16[784,128]{1,0:T(8,128)(2,1)S(1)}, u32[]{:S(2)}, u32[]{:S(2)}) collective-permute-start(bf16[784,128]{1,0:T(8,128)(2,1)S(1)} %get-tuple-element.10), channel_id=1, source_target_pairs={{0,127},{1,2},{2,1},{3,4},{4,3},{5,6},{6,5},{7,8},{8,7},{9,10},{10... | collective-permute-start | bytes 602120 | tf_op jit(solution)/shard_map/ppermute | solution.py:418
  15.5 31.2 %collective-permute-start = (bf16[784,512]{1,0:T(8,128)(2,1)S(1)}, bf16[784,512]{1,0:T(8,128)(2,1)S(1)}, u32[]{:S(2)}, u32[]{:S(2)}) collective-permute-start(bf16[784,512]{1,0:T(8,128)(2,1)S(1)} %tie.2.own.own_ref), channel_id=1, source_target_pairs={{0,2},{1,127},{2,4},{3,1},{4,6},{5,3},{6,8},{7,5},{8,10},{9,7},{10... | collective-permute-start | bytes 2408456 | tf_op jit(solution)/shard_map/ppermute | solution.py:418
  17.4 27.4 %collective-permute-start.1 = (bf16[784,512]{1,0:T(8,128)(2,1)S(1)}, bf16[784,512]{1,0:T(8,128)(2,1)S(1)}, u32[]{:S(2)}, u32[]{:S(2)}) collective-permute-start(bf16[784,512]{1,0:T(8,128)(2,1)S(1)} %tie.2.own.own_ref), channel_id=1, source_target_pairs={{0,126},{1,3},{2,0},{3,5},{4,2},{5,7},{6,4},{7,9},{8,6},{9,11},{10... | collective-permute-start | bytes 2408456 | tf_op jit(solution)/shard_map/ppermute | solution.py:418
  23.5 1.4 %copy-start.3 = (bf16[784,512]{1,0:T(8,128)(2,1)}, bf16[784,512]{1,0:T(8,128)(2,1)S(1)}, u32[]{:S(2)}) copy-start(bf16[784,512]{1,0:T(8,128)(2,1)S(1)} %collective-permute-done.3.pair.pair_ref) | copy-start | bytes 2408452
  24.9 3.1 %collective-permute-start.6 = (f32[32,128]{1,0:T(8,128)S(1)}, f32[32,128]{1,0:T(8,128)S(1)}, u32[]{:S(2)}, u32[]{:S(2)}) collective-permute-start(f32[32,128]{1,0:T(8,128)S(1)} %get-tuple-element.12), channel_id=1, source_target_pairs={{0,1},{1,0},{2,3},{3,2},{4,5},{5,4},{6,7},{7,6},{8,9},{9,8},{10,11... | collective-permute-start | bytes 49160 | tf_op jit(solution)/shard_map/ppermute | solution.py:414
  28.8 23.8 %all-to-all-start = ((f32[16,32,128]{2,1,0:T(8,128)}), f32[16,32,128]{2,1,0:T(8,128)S(1)}, u32[]{:S(2)}, u32[]{:S(2)}) async-start(f32[16,32,128]{2,1,0:T(8,128)} %broadcast_in_dim.3), calls=%async_computation | async-start | bytes 524288 | tf_op jit(solution)/shard_map/all_to_all | solution.py:421
  44.8 8.7 %copy-start.1 = (bf16[784,512]{1,0:T(8,128)(2,1)}, bf16[784,512]{1,0:T(8,128)(2,1)S(1)}, u32[]{:S(2)}) copy-start(bf16[784,512]{1,0:T(8,128)(2,1)S(1)} %collective-permute-done.1.far_z.refs_2_) | copy-start | bytes 2408452
  44.8 24.0 %collective-permute-start.2 = (bf16[784,512]{1,0:T(8,128)(2,1)S(1)}, bf16[784,512]{1,0:T(8,128)(2,1)}, u32[]{:S(2)}, u32[]{:S(2)}) collective-permute-start(bf16[784,512]{1,0:T(8,128)(2,1)S(1)} %collective-permute-done.1.far_z.refs_2_), channel_id=1, source_target_pairs={{0,1},{1,0},{2,3},{3,2},{4,5},{5,4},{6,7},{7,6},{8,9},{9,8},{10,11... | collective-permute-start | bytes 2408456 | tf_op jit(solution)/shard_map/ppermute | solution.py:414
  46.8 6.8 %copy-start = (bf16[784,512]{1,0:T(8,128)(2,1)}, bf16[784,512]{1,0:T(8,128)(2,1)S(1)}, u32[]{:S(2)}) copy-start(bf16[784,512]{1,0:T(8,128)(2,1)S(1)} %collective-permute-done.near_z.refs_1_) | copy-start | bytes 2408452
  46.8 22.1 %collective-permute-start.4 = (bf16[784,512]{1,0:T(8,128)(2,1)S(1)}, bf16[784,512]{1,0:T(8,128)(2,1)}, u32[]{:S(2)}, u32[]{:S(2)}) collective-permute-start(bf16[784,512]{1,0:T(8,128)(2,1)S(1)} %collective-permute-done.near_z.refs_1_), channel_id=1, source_target_pairs={{0,1},{1,0},{2,3},{3,2},{4,5},{5,4},{6,7},{7,6},{8,9},{9,8},{10,11... | collective-permute-start | bytes 2408456 | tf_op jit(solution)/shard_map/ppermute | solution.py:414
  53.5 23.9 %all-to-all-start.1 = ((f32[32,32,128]{2,1,0:T(8,128)}), f32[32,32,128]{2,1,0:T(8,128)S(1)}, u32[]{:S(2)}, u32[]{:S(2)}) async-start(f32[32,32,128]{2,1,0:T(8,128)} %reduce.1), calls=%async_computation.1 | async-start | bytes 1048576 | tf_op jit(solution)/shard_map/all_to_all | solution.py:421
  66.9 10.1 %collective-permute-start.7 = (bf16[3,64,512]{2,1,0:T(8,128)(2,1)S(1)}, bf16[3,64,512]{2,1,0:T(8,128)(2,1)}, u32[]{:S(2)}, u32[]{:S(2)}) collective-permute-start(bf16[3,64,512]{2,1,0:T(8,128)(2,1)S(1)} %thin.1.refs_3_), channel_id=1, source_target_pairs={{0,125},{1,4},{2,127},{3,6},{4,1},{5,8},{6,3},{7,10},{8,5},{9,12},... | collective-permute-start | bytes 589832 | tf_op jit(solution)/shard_map/ppermute | solution.py:418

commit v7 on v6

--- a/solution.py
+++ b/solution.py
@@ -115,8 +115,15 @@
     send_ref[...] = jnp.where(core == 0, sums[1], sums[0])
 
 
-def thin_kernel(sc, halo_ref, own_ref, after, thin, thin_ref, sem):
+def side_kernel(
+    planes, sc, target, keeps, scale, coupling, own, halo_ref, after, thin, mixed,
+    coupling_ref, own_ref, mixed_ref, thin_ref, sems,
+):
     del after
+    copy = pltpu.make_async_copy(coupling, coupling_ref, sems.at[0])
+    copy.start()
+    own_copy = pltpu.make_async_copy(own.at[pl.ds(0, own_ref.shape[0])], own_ref, sems.at[3])
+    own_copy.start()
     comps, quarter, _ = thin.shape
     size = 4 * quarter
     rows = comps * size
@@ -132,97 +139,11 @@
     seats = jnp.broadcast_to(jnp.where(mine, place, -1.0), shape)
     into = (seats == iota(shape, 0).astype(F32)).astype(F32).astype(BF16)
     pack = dot(into, chosen(as_column(low), size)).astype(BF16)
+    own_copy.wait()
     for comp in range(comps):
         thin_ref[comp] = dot(pack, own_ref[comp * size : (comp + 1) * size]).astype(BF16)
-    copy = pltpu.make_async_copy(thin_ref, thin, sem.at[0])
-    copy.start()
-    copy.wait()
-
-
-def offsets_of(clusters, sc, near_col, count):
-    offs = []
-    for j in range(count):
-        off = near_col[j] - sc[3] + 2
-        off = jnp.where(off < 0, off + clusters, off)
-        off = jnp.where(off >= clusters, off - clusters, off) - 2
-        offs.append(jnp.where(sc[0] == 0, off, -off))
-    return offs
-
-
-def near_kernel(
-    clusters, sc, near_col, tiles, own, near_z, pair_far, pair, far_z, pair_near,
-    total, tile_ref, tails, window, blocks, total_ref, sems, tail_sems, tile_sems, out_sems,
-):
-    count, rows, _ = tiles.shape
-    columns = own.shape[1]
-    size = rows // 3
-    core = sc[0]
-    seats = (None, near_z, pair_far, own, pair, far_z, pair_near)
-    offs = offsets_of(clusters, sc, near_col, count)
-    for j in range(count):
-        for o in range(-2, 3):
-
-            @pl.when(offs[j] == o)
-            def _(j=j, o=o):
-                pltpu.make_async_copy(seats[o + 3].at[pl.ds(rows, PAD)], tails.at[j], tail_sems.at[j]).start()
-                for comp in range(3):
-                    for w in range(3):
-                        source = seats[o + 2 + w]
-                        if source is None:
-                            window[j, comp, :size] = jnp.zeros((size, columns), BF16)
-                        else:
-                            pltpu.make_async_copy(
-                                source.at[pl.ds(comp * size, size)],
-                                window.at[j, comp, pl.ds(w * size, size)],
-                                sems.at[j, comp, w],
-                            ).start()
-
-    for j in range(count):
-        pltpu.make_async_copy(
-            tiles.at[j], tile_ref.at[:, pl.ds(j * rows, rows)], tile_sems.at[j]
-        ).start()
-    for j in range(count):
-        edge = offs[j] == -2
-        pltpu.make_async_copy(own.at[pl.ds(rows, PAD)], tails.at[j], tail_sems.at[j]).wait()
-        tail = tails[j].astype(F32)
-        low, high = tail[0:1, :size], tail[1:2, :size]
-        seat = jnp.where(core == 0, high, 2.0 - high)
-        pick = chosen(as_column(seat * size + low), 3 * size)
-        for comp in range(3):
-
-            @pl.when(jnp.logical_not(edge))
-            def _(j=j, comp=comp):
-                pltpu.make_async_copy(
-                    own.at[pl.ds(0, size)], window.at[j, comp, pl.ds(0, size)], sems.at[j, comp, 0]
-                ).wait()
-
-            for w in range(1, 3):
-                pltpu.make_async_copy(
-                    own.at[pl.ds(0, size)], window.at[j, comp, pl.ds(w * size, size)], sems.at[j, comp, w]
-                ).wait()
-            at = j * rows + comp * size
-            blocks[at : at + size] = dot(pick, window[j, comp]).astype(BF16)
-    for j in range(count):
-        pltpu.make_async_copy(
-            tiles.at[j], tile_ref.at[:, pl.ds(j * rows, rows)], tile_sems.at[j]
-        ).wait()
-    outs = []
-    for r in range(3):
-        span = slice(r * size, (r + 1) * size)
-        total_ref[span] = dot(tile_ref[span], blocks[...])
-        here = pl.ds(r * size, size)
-        outs.append(pltpu.make_async_copy(total_ref.at[here], total.at[here], out_sems.at[r]))
-        outs[-1].start()
-    for copy in outs:
-        copy.wait()
-
-
-def couple_kernel(
-    planes, sc, target, keeps, scale, coupling, after, mixed, coupling_ref, mixed_ref, sems
-):
-    del after
-    copy = pltpu.make_async_copy(coupling, coupling_ref, sems.at[0])
-    copy.start()
+    thin_copy = pltpu.make_async_copy(thin_ref, thin, sems.at[1])
+    thin_copy.start()
     copy.wait()
     blocks, rank, _ = coupling_ref.shape
     width = mixed_ref.shape[1] // 3
@@ -238,9 +159,88 @@
         mixed_ref[at, :width] = high
         mixed_ref[at, width : 2 * width] = high
         mixed_ref[at, 2 * width :] = (tile - high.astype(F32)).astype(BF16)
-    copy = pltpu.make_async_copy(mixed_ref, mixed, sems.at[1])
+    copy = pltpu.make_async_copy(mixed_ref, mixed, sems.at[2])
     copy.start()
     copy.wait()
+    thin_copy.wait()
+
+
+def offsets_of(clusters, sc, near_col, count):
+    offs = []
+    for j in range(count):
+        off = near_col[j] - sc[3] + 2
+        off = jnp.where(off < 0, off + clusters, off)
+        off = jnp.where(off >= clusters, off - clusters, off) - 2
+        offs.append(jnp.where(sc[0] == 0, off, -off))
+    return offs
+
+
+def near_kernel(
+    clusters, sc, near_col, tiles, own, near_z, pair_far, pair, far_z, pair_near,
+    total, tile_ref, tails, window, blocks, total_ref, sems, tail_sems, tile_sems, out_sems,
+):
+    count, rows, _ = tiles.shape
+    columns = own.shape[1]
+    size = rows // 3
+    core = sc[0]
+    seats = (None, near_z, pair_far, own, pair, far_z, pair_near)
+    offs = offsets_of(clusters, sc, near_col, count)
+    for j in range(count):
+        for o in range(-2, 3):
+
+            @pl.when(offs[j] == o)
+            def _(j=j, o=o):
+                pltpu.make_async_copy(seats[o + 3].at[pl.ds(rows, PAD)], tails.at[j], tail_sems.at[j]).start()
+                for comp in range(3):
+                    for w in range(3):
+                        source = seats[o + 2 + w]
+                        if source is None:
+                            window[j, comp, :size] = jnp.zeros((size, columns), BF16)
+                        else:
+                            pltpu.make_async_copy(
+                                source.at[pl.ds(comp * size, size)],
+                                window.at[j, comp, pl.ds(w * size, size)],
+                                sems.at[j, comp, w],
+                            ).start()
+
+    for j in range(count):
+        pltpu.make_async_copy(
+            tiles.at[j], tile_ref.at[:, pl.ds(j * rows, rows)], tile_sems.at[j]
+        ).start()
+    for j in range(count):
+        edge = offs[j] == -2
+        pltpu.make_async_copy(own.at[pl.ds(rows, PAD)], tails.at[j], tail_sems.at[j]).wait()
+        tail = tails[j].astype(F32)
+        low, high = tail[0:1, :size], tail[1:2, :size]
+        seat = jnp.where(core == 0, high, 2.0 - high)
+        pick = chosen(as_column(seat * size + low), 3 * size)
+        for comp in range(3):
+
+            @pl.when(jnp.logical_not(edge))
+            def _(j=j, comp=comp):
+                pltpu.make_async_copy(
+                    own.at[pl.ds(0, size)], window.at[j, comp, pl.ds(0, size)], sems.at[j, comp, 0]
+                ).wait()
+
+            for w in range(1, 3):
+                pltpu.make_async_copy(
+                    own.at[pl.ds(0, size)], window.at[j, comp, pl.ds(w * size, size)], sems.at[j, comp, w]
+                ).wait()
+            at = j * rows + comp * size
+            blocks[at : at + size] = dot(pick, window[j, comp]).astype(BF16)
+    for j in range(count):
+        pltpu.make_async_copy(
+            tiles.at[j], tile_ref.at[:, pl.ds(j * rows, rows)], tile_sems.at[j]
+        ).wait()
+    outs = []
+    for r in range(3):
+        span = slice(r * size, (r + 1) * size)
+        total_ref[span] = dot(tile_ref[span], blocks[...])
+        here = pl.ds(r * size, size)
+        outs.append(pltpu.make_async_copy(total_ref.at[here], total.at[here], out_sems.at[r]))
+        outs[-1].start()
+    for copy in outs:
+        copy.wait()
 
 
 def reduce_kernel(many_ref, sums, sums_ref, sem):
@@ -446,36 +446,31 @@
         in_specs=[SMEM, VMEM, VMEM, VMEM, VMEM],
         out_specs=(VMEM, VMEM),
         compiler_params=params(12),
-        cost_estimate=cost_of(10 * 10**9),
+        cost_estimate=cost_of(5 * 10**9),
         name="pieces",
     )(sc, halo, block, pair, bases.transpose(0, 2, 1, 3))
     level_sum = keep + swapped(send)
     many = exchanged(jnp.broadcast_to(level_sum, (steps, rank, part)), "clu_1")
-    thin = pl.pallas_call(
-        thin_kernel,
-        out_shape=shape_of((comps, size // 4, columns), BF16),
-        in_specs=[SMEM, VMEM, VMEM, ANY],
-        out_specs=HBM,
+    thin, mixed = pl.pallas_call(
+        functools.partial(side_kernel, planes),
+        out_shape=(
+            shape_of((comps, size // 4, columns), BF16),
+            shape_of((far_count * rank, 3 * width), BF16),
+        ),
+        in_specs=[SMEM, SMEM, SMEM, SMEM, HBM, HBM, VMEM, ANY],
+        out_specs=(HBM, HBM),
         scratch_shapes=[
+            pltpu.VMEM((far_count, rank, rank), BF16),
+            pltpu.VMEM((rows, columns), BF16),
+            pltpu.VMEM((far_count * rank, 3 * width), BF16),
             pltpu.VMEM((comps, size // 4, columns), BF16),
-            pltpu.SemaphoreType.DMA((1,)),
+            pltpu.SemaphoreType.DMA((4,)),
         ],
         compiler_params=params(12),
-        name="thin",
-    )(sc, halo, block, level_sum)
-    mixed = pl.pallas_call(
-        functools.partial(couple_kernel, planes),
-        out_shape=shape_of((far_count * rank, 3 * width), BF16),
-        in_specs=[SMEM, SMEM, SMEM, SMEM, HBM, ANY],
-        out_specs=HBM,
-        scratch_shapes=[
-            pltpu.VMEM((far_count, rank, rank), BF16),
-            pltpu.VMEM((far_count * rank, 3 * width), BF16),
-            pltpu.SemaphoreType.DMA((2,)),
-        ],
-        compiler_params=params(4),
-        name="couple",
-    )(sc, *in_hbm(far_target[0], far_rank[0], far_scale[0], far_coupling[0]), level_sum)
+        name="side",
+    )(
+        sc, *in_hbm(far_target[0], far_rank[0], far_scale[0], far_coupling[0], block), halo, level_sum,
+    )
     many = tied(many, near_z, far_z, thin, mixed)
     thin = sent(thin, 3)
     pair_near = swapped(near_z)

time: 99.3 us -> 95.5 us (0.962)
  the two profiles are of different devices: /device:TPU:2 before, /device:TPU:32 now
where the time goes in v7:
time: 95.5 us; the launch traced here: 94.9 us
  starting transfers between devices  48.5 us (51%)
  Pallas kernels  17.5 us (18%)
  blocking collectives  15.1 us (16%)
  waiting for transfers between devices  12.7 us (13%)
    ppermute x4, starting transfers between devices, sent(): return lax.ppermute(v, CLU, pairs)  25.9 us
    all_to_all x1, blocking collectives, exchanged(): return lax.all_to_all(v, axis, split_axis=0, concat_axis=0, tiled=True)  15.1 us
    all_to_all x2, starting transfers between devices, exchanged(): return lax.all_to_all(v, axis, split_axis=0, concat_axis=0, tiled=True)  14.3 us
    all_to_all x2, waiting for transfers between devices, exchanged(): return lax.all_to_all(v, axis, split_axis=0, concat_axis=0, tiled=True)  11.4 us
    ppermute x4, starting transfers between devices, swapped(): return lax.ppermute(v, 'clu_2', [(0, 1), (1, 0)])  8.29 us
    pallas_call x1, Pallas kernels, on_device(): pl.pallas_call(functools.partial(near_kernel, clusters), out_shape=shape_...  6.6 us
    pallas_call x1, Pallas kernels, on_device(): pl.pallas_call(functools.partial(mix_kernel, clusters, planes), out_shape...  2.99 us
    pallas_call x1, Pallas kernels, on_device(): pl.pallas_call(functools.partial(side_kernel, planes), out_shape=(shape_o...  2.9 us
  transfers between devices with their start and end apart: 10, of which 3 were waited for; matrix products, arithmetic and copies ran while one was open for 1% of the time, Pallas kernels for 12%

profile of v7, /device:TPU:32, one launch (start us, length us, event | category | flops | bytes accessed | tf_op | source)
XLA Modules:
  0.0 94.9 jit_solution(15486235105137822575)
XLA Ops:
  0.0 0.1 pad_add_fusion.sc
  0.1 1.8 %dress.1 = (bf16[784,128]{1,0:T(8,128)(2,1)S(1)}, bf16[784,512]{1,0:T(8,128)(2,1)S(1)}) custom-call(s32[4]{0:T(128)S(1)} %pad_add_fusion.sc, s32[1,256]{1,0:T(1,128)} %bitcast.21, bf16[768,512]{1,0:T(8,128)(2,1)} %bitcast.18), custom_call_target="tpu_custom_call" | custom-call | tf_op jit(solution)/shard_map/dress/pallas_call | solution.py:424
  1.9 0.0 copy-start.4
  1.9 0.0 copy-start.2
  2.0 2.1 %collective-permute-start.3 = (bf16[784,512]{1,0:T(8,128)(2,1)S(1)}, bf16[784,512]{1,0:T(8,128)(2,1)S(1)}, u32[]{:S(2)}, u32[]{:S(2)}) collective-permute-start(bf16[784,512]{1,0:T(8,128)(2,1)S(1)} %tie.2.own.own_ref), channel_id=1, source_target_pairs={{0,1},{1,0},{2,3},{3,2},{4,5},{5,4},{6,7},{7,6},{8,9},{9,8},{10,11... | collective-permute-start | bytes 2408456 | tf_op jit(solution)/shard_map/ppermute | solution.py:414
  4.0 7.5 %collective-permute-start.5 = (bf16[784,128]{1,0:T(8,128)(2,1)S(1)}, bf16[784,128]{1,0:T(8,128)(2,1)S(1)}, u32[]{:S(2)}, u32[]{:S(2)}) collective-permute-start(bf16[784,128]{1,0:T(8,128)(2,1)S(1)} %get-tuple-element.12), channel_id=1, source_target_pairs={{0,127},{1,2},{2,1},{3,4},{4,3},{5,6},{6,5},{7,8},{8,7},{9,10},{10... | collective-permute-start | bytes 602120 | tf_op jit(solution)/shard_map/ppermute | solution.py:418
  11.5 8.2 %collective-permute-start.1 = (bf16[784,512]{1,0:T(8,128)(2,1)S(1)}, bf16[784,512]{1,0:T(8,128)(2,1)S(1)}, u32[]{:S(2)}, u32[]{:S(2)}) collective-permute-start(bf16[784,512]{1,0:T(8,128)(2,1)S(1)} %tie.2.own.own_ref), channel_id=1, source_target_pairs={{0,126},{1,3},{2,0},{3,5},{4,2},{5,7},{6,4},{7,9},{8,6},{9,11},{10... | collective-permute-start | bytes 2408456 | tf_op jit(solution)/shard_map/ppermute | solution.py:418
  19.7 1.9 %collective-permute-start = (bf16[784,512]{1,0:T(8,128)(2,1)S(1)}, bf16[784,512]{1,0:T(8,128)(2,1)S(1)}, u32[]{:S(2)}, u32[]{:S(2)}) collective-permute-start(bf16[784,512]{1,0:T(8,128)(2,1)S(1)} %tie.2.own.own_ref), channel_id=1, source_target_pairs={{0,2},{1,127},{2,4},{3,1},{4,6},{5,3},{6,8},{7,5},{8,10},{9,7},{10... | collective-permute-start | bytes 2408456 | tf_op jit(solution)/shard_map/ppermute | solution.py:418
  21.7 0.0 collective-permute-done.5.halo_ref
  21.7 0.0 collective-permute-done.3.pair.pair_ref
  21.7 0.0 copy-start.3
  21.7 0.0 copy-done.4
  21.7 1.4 %pieces.1 = (f32[32,128]{1,0:T(8,128)S(1)}, f32[32,128]{1,0:T(8,128)S(1)}) custom-call(s32[4]{0:T(128)S(1)} %pad_add_fusion.sc, bf16[784,128]{1,0:T(8,128)(2,1)S(1)} %collective-permute-done.5.halo_ref, bf16[784,512]{1,0:T(8,128)(2,1)S(1)} %tie.2.own.own_ref, bf16[784,512]{1,0:T(8,128)(2,1)S(1)} %collective-permute-done.3.pair.pair_ref, ...), custom_call_target="tpu_custom_call" | custom-call | flops 5000000000 | bytes 1000000 | tf_op jit(solution)/shard_map/pieces/pallas_call | solution.py:443
  23.1 0.0 copy-done.2
  23.1 0.0 copy-done.3
  23.2 1.9 %collective-permute-start.6 = (f32[32,128]{1,0:T(8,128)S(1)}, f32[32,128]{1,0:T(8,128)S(1)}, u32[]{:S(2)}, u32[]{:S(2)}) collective-permute-start(f32[32,128]{1,0:T(8,128)S(1)} %get-tuple-element.14), channel_id=1, source_target_pairs={{0,1},{1,0},{2,3},{3,2},{4,5},{5,4},{6,7},{7,6},{8,9},{9,8},{10,11... | collective-permute-start | bytes 49160 | tf_op jit(solution)/shard_map/ppermute | solution.py:414
  25.1 1.1 %collective-permute-done.6 = f32[32,128]{1,0:T(8,128)S(1)} collective-permute-done((f32[32,128]{1,0:T(8,128)S(1)}, f32[32,128]{1,0:T(8,128)S(1)}, u32[]{:S(2)}, u32[]{:S(2)}) %collective-permute-start.6) | collective-permute-done | bytes 16416 | tf_op jit(solution)/shard_map/ppermute | solution.py:414
  26.2 0.7 broadcast_in_dim.3
  27.0 6.8 %all-to-all-start = ((f32[16,32,128]{2,1,0:T(8,128)}), f32[16,32,128]{2,1,0:T(8,128)S(1)}, u32[]{:S(2)}, u32[]{:S(2)}) async-start(f32[16,32,128]{2,1,0:T(8,128)} %broadcast_in_dim.3), calls=%async_computation | async-start | bytes 524288 | tf_op jit(solution)/shard_map/all_to_all | solution.py:421
  33.7 0.1 collective-permute-done.1.far_z.refs_2_
  33.8 0.0 copy-start.1
  33.8 1.9 %collective-permute-start.2 = (bf16[784,512]{1,0:T(8,128)(2,1)S(1)}, bf16[784,512]{1,0:T(8,128)(2,1)}, u32[]{:S(2)}, u32[]{:S(2)}) collective-permute-start(bf16[784,512]{1,0:T(8,128)(2,1)S(1)} %collective-permute-done.1.far_z.refs_2_), channel_id=1, source_target_pairs={{0,1},{1,0},{2,3},{3,2},{4,5},{5,4},{6,7},{7,6},{8,9},{9,8},{10,11... | collective-permute-start | bytes 2408456 | tf_op jit(solution)/shard_map/ppermute | solution.py:414
  35.8 0.0 collective-permute-done.near_z.refs_1_
  35.8 0.0 copy-start
  35.8 2.4 %collective-permute-start.4 = (bf16[784,512]{1,0:T(8,128)(2,1)S(1)}, bf16[784,512]{1,0:T(8,128)(2,1)}, u32[]{:S(2)}, u32[]{:S(2)}) collective-permute-start(bf16[784,512]{1,0:T(8,128)(2,1)S(1)} %collective-permute-done.near_z.refs_1_), channel_id=1, source_target_pairs={{0,1},{1,0},{2,3},{3,2},{4,5},{5,4},{6,7},{7,6},{8,9},{9,8},{10,11... | collective-permute-start | bytes 2408456 | tf_op jit(solution)/shard_map/ppermute | solution.py:414
  38.2 2.9 %side.1 = (bf16[3,64,512]{2,1,0:T(8,128)(2,1)S(1)}, bf16[512,384]{1,0:T(8,128)(2,1)S(1)}) custom-call(s32[4]{0:T(128)S(1)} %pad_add_fusion.sc, s32[16]{0:T(128)} %bitcast.22, s32[16]{0:T(128)} %bitcast.23, f32[16]{0:T(128)} %bitcast.24, bf16[16,32,32]{2,1,0:T(8,128)(2,1)} %bitcast.20, bf16[784,512]{1,0:T(8,128)(2,1)} %copy-done.2, ...), custom_call_target="tpu_custom_call" | custom-call | tf_op jit(solution)/shard_map/side/pallas_call | solution.py:454
  41.1 11.4 %all-to-all-done.refs_0_ = f32[16,32,128]{2,1,0:T(8,128)S(1)} async-done(((f32[16,32,128]{2,1,0:T(8,128)}), f32[16,32,128]{2,1,0:T(8,128)S(1)}, u32[]{:S(2)}, u32[]{:S(2)}) %all-to-all-start) | async-done | bytes 262176 | tf_op jit(solution)/shard_map/all_to_all | solution.py:421
  52.5 0.9 reduce.1
  53.4 0.0 copy-done.1
  53.4 0.0 copy-done
  53.4 7.5 %all-to-all-start.1 = ((f32[32,32,128]{2,1,0:T(8,128)}), f32[32,32,128]{2,1,0:T(8,128)S(1)}, u32[]{:S(2)}, u32[]{:S(2)}) async-start(f32[32,32,128]{2,1,0:T(8,128)} %reduce.1), calls=%async_computation.1 | async-start | bytes 1048576 | tf_op jit(solution)/shard_map/all_to_all | solution.py:421
  61.0 8.3 %collective-permute-start.7 = (bf16[3,64,512]{2,1,0:T(8,128)(2,1)S(1)}, bf16[3,64,512]{2,1,0:T(8,128)(2,1)}, u32[]{:S(2)}, u32[]{:S(2)}) collective-permute-start(bf16[3,64,512]{2,1,0:T(8,128)(2,1)S(1)} %get-tuple-element.15.refs_3_), channel_id=1, source_target_pairs={{0,125},{1,4},{2,127},{3,6},{4,1},{5,8},{6,3},{7,10},{8,5},{9,12},... | collective-permute-start | bytes 589832 | tf_op jit(solution)/shard_map/ppermute | solution.py:418
  69.3 0.0 collective-permute-done.2.pair_far
  69.3 0.0 collective-permute-done.4.pair_near
  69.3 6.6 %near.1 = f32[768,512]{1,0:T(8,128)S(1)} custom-call(s32[4]{0:T(128)S(1)} %pad_add_fusion.sc, s32[2]{0:T(128)} %bitcast.25, bf16[2,768,768]{2,1,0:T(8,128)(2,1)} %bitcast.16, bf16[784,512]{1,0:T(8,128)(2,1)} %copy-done.2, bf16[784,512]{1,0:T(8,128)(2,1)} %copy-done, bf16[784,512]{1,0:T(8,128)(2,1)} %collective-permute-done.2.pair_far, ...), custom_call_target="tpu_custom_call" | custom-call | flops 4000000000 | bytes 1000000 | tf_op jit(solution)/shard_map/near/pallas_call | solution.py:489
  75.9 0.0 collective-permute-done.7.thin
  75.9 0.0 all-to-all-done.1.sums
  75.9 3.0 %mix.1 = bf16[4,768,128]{2,1,0:T(8,128)(2,1)S(1)} custom-call(s32[4]{0:T(128)S(1)} %pad_add_fusion.sc, s32[2]{0:T(128)} %bitcast.26, f32[768,512]{1,0:T(8,128)S(1)} %near.1, f32[32,32,128]{2,1,0:T(8,128)S(1)} %all-to-all-done.1.sums, bf16[512,768]{1,0:T(8,128)(2,1)} %bitcast.19, bf16[512,384]{1,0:T(8,128)(2,1)S(1)} %get-tuple-element.16.refs_4_.mixed, ...), custom_call_target="tpu_custom_call" | custom-call | tf_op jit(solution)/shard_map/mix/pallas_call | solution.py:512
  78.9 15.1 %all_to_all.15.arrived_ref = bf16[4,768,128]{2,1,0:T(8,128)(2,1)S(1)} all-to-all(bf16[4,768,128]{2,1,0:T(8,128)(2,1)S(1)} %mix.1), channel_id=1, replica_groups=mesh['grp'=4,'clu_0'=4,'clu_1'=16,'clu_2'=2] {'grp'}, dimensions={0} | all-to-all | bytes 1572864 | tf_op jit(solution)/shard_map/all_to_all | solution.py:421
  94.0 0.8 last.1
  (3 shorter events, 0.0 us)
Async XLA Ops:
  1.9 19.8 %copy-start.4 = (bf16[2,32,3,256]{3,1,2,0:T(8,128)(2,1)S(1)}, bf16[2,32,3,256]{3,1,2,0:T(8,128)(2,1)}, u32[]{:S(2)}) copy-start(bf16[2,32,3,256]{3,1,2,0:T(8,128)(2,1)} %param.12) | copy-start | bytes 294916
  1.9 21.2 %copy-start.2 = (bf16[784,512]{1,0:T(8,128)(2,1)}, bf16[784,512]{1,0:T(8,128)(2,1)S(1)}, u32[]{:S(2)}) copy-start(bf16[784,512]{1,0:T(8,128)(2,1)S(1)} %tie.2.own.own_ref) | copy-start | bytes 2408452
  2.0 19.7 %collective-permute-start.3 = (bf16[784,512]{1,0:T(8,128)(2,1)S(1)}, bf16[784,512]{1,0:T(8,128)(2,1)S(1)}, u32[]{:S(2)}, u32[]{:S(2)}) collective-permute-start(bf16[784,512]{1,0:T(8,128)(2,1)S(1)} %tie.2.own.own_ref), channel_id=1, source_target_pairs={{0,1},{1,0},{2,3},{3,2},{4,5},{5,4},{6,7},{7,6},{8,9},{9,8},{10,11... | collective-permute-start | bytes 2408456 | tf_op jit(solution)/shard_map/ppermute | solution.py:414
  4.0 17.7 %collective-permute-start.5 = (bf16[784,128]{1,0:T(8,128)(2,1)S(1)}, bf16[784,128]{1,0:T(8,128)(2,1)S(1)}, u32[]{:S(2)}, u32[]{:S(2)}) collective-permute-start(bf16[784,128]{1,0:T(8,128)(2,1)S(1)} %get-tuple-element.12), channel_id=1, source_target_pairs={{0,127},{1,2},{2,1},{3,4},{4,3},{5,6},{6,5},{7,8},{8,7},{9,10},{10... | collective-permute-start | bytes 602120 | tf_op jit(solution)/shard_map/ppermute | solution.py:418
  11.5 22.3 %collective-permute-start.1 = (bf16[784,512]{1,0:T(8,128)(2,1)S(1)}, bf16[784,512]{1,0:T(8,128)(2,1)S(1)}, u32[]{:S(2)}, u32[]{:S(2)}) collective-permute-start(bf16[784,512]{1,0:T(8,128)(2,1)S(1)} %tie.2.own.own_ref), channel_id=1, source_target_pairs={{0,126},{1,3},{2,0},{3,5},{4,2},{5,7},{6,4},{7,9},{8,6},{9,11},{10... | collective-permute-start | bytes 2408456 | tf_op jit(solution)/shard_map/ppermute | solution.py:418
  19.7 16.0 %collective-permute-start = (bf16[784,512]{1,0:T(8,128)(2,1)S(1)}, bf16[784,512]{1,0:T(8,128)(2,1)S(1)}, u32[]{:S(2)}, u32[]{:S(2)}) collective-permute-start(bf16[784,512]{1,0:T(8,128)(2,1)S(1)} %tie.2.own.own_ref), channel_id=1, source_target_pairs={{0,2},{1,127},{2,4},{3,1},{4,6},{5,3},{6,8},{7,5},{8,10},{9,7},{10... | collective-permute-start | bytes 2408456 | tf_op jit(solution)/shard_map/ppermute | solution.py:418
  21.7 1.4 %copy-start.3 = (bf16[784,512]{1,0:T(8,128)(2,1)}, bf16[784,512]{1,0:T(8,128)(2,1)S(1)}, u32[]{:S(2)}) copy-start(bf16[784,512]{1,0:T(8,128)(2,1)S(1)} %collective-permute-done.3.pair.pair_ref) | copy-start | bytes 2408452
  23.2 3.1 %collective-permute-start.6 = (f32[32,128]{1,0:T(8,128)S(1)}, f32[32,128]{1,0:T(8,128)S(1)}, u32[]{:S(2)}, u32[]{:S(2)}) collective-permute-start(f32[32,128]{1,0:T(8,128)S(1)} %get-tuple-element.14), channel_id=1, source_target_pairs={{0,1},{1,0},{2,3},{3,2},{4,5},{5,4},{6,7},{7,6},{8,9},{9,8},{10,11... | collective-permute-start | bytes 49160 | tf_op jit(solution)/shard_map/ppermute | solution.py:414
  27.0 25.5 %all-to-all-start = ((f32[16,32,128]{2,1,0:T(8,128)}), f32[16,32,128]{2,1,0:T(8,128)S(1)}, u32[]{:S(2)}, u32[]{:S(2)}) async-start(f32[16,32,128]{2,1,0:T(8,128)} %broadcast_in_dim.3), calls=%async_computation | async-start | bytes 524288 | tf_op jit(solution)/shard_map/all_to_all | solution.py:421
  33.8 19.6 %copy-start.1 = (bf16[784,512]{1,0:T(8,128)(2,1)}, bf16[784,512]{1,0:T(8,128)(2,1)S(1)}, u32[]{:S(2)}) copy-start(bf16[784,512]{1,0:T(8,128)(2,1)S(1)} %collective-permute-done.1.far_z.refs_2_) | copy-start | bytes 2408452
  33.8 35.4 %collective-permute-start.2 = (bf16[784,512]{1,0:T(8,128)(2,1)S(1)}, bf16[784,512]{1,0:T(8,128)(2,1)}, u32[]{:S(2)}, u32[]{:S(2)}) collective-permute-start(bf16[784,512]{1,0:T(8,128)(2,1)S(1)} %collective-permute-done.1.far_z.refs_2_), channel_id=1, source_target_pairs={{0,1},{1,0},{2,3},{3,2},{4,5},{5,4},{6,7},{7,6},{8,9},{9,8},{10,11... | collective-permute-start | bytes 2408456 | tf_op jit(solution)/shard_map/ppermute | solution.py:414
  35.8 17.6 %copy-start = (bf16[784,512]{1,0:T(8,128)(2,1)}, bf16[784,512]{1,0:T(8,128)(2,1)S(1)}, u32[]{:S(2)}) copy-start(bf16[784,512]{1,0:T(8,128)(2,1)S(1)} %collective-permute-done.near_z.refs_1_) | copy-start | bytes 2408452
  35.8 33.5 %collective-permute-start.4 = (bf16[784,512]{1,0:T(8,128)(2,1)S(1)}, bf16[784,512]{1,0:T(8,128)(2,1)}, u32[]{:S(2)}, u32[]{:S(2)}) collective-permute-start(bf16[784,512]{1,0:T(8,128)(2,1)S(1)} %collective-permute-done.near_z.refs_1_), channel_id=1, source_target_pairs={{0,1},{1,0},{2,3},{3,2},{4,5},{5,4},{6,7},{7,6},{8,9},{9,8},{10,11... | collective-permute-start | bytes 2408456 | tf_op jit(solution)/shard_map/ppermute | solution.py:414
  53.4 22.5 %all-to-all-start.1 = ((f32[32,32,128]{2,1,0:T(8,128)}), f32[32,32,128]{2,1,0:T(8,128)S(1)}, u32[]{:S(2)}, u32[]{:S(2)}) async-start(f32[32,32,128]{2,1,0:T(8,128)} %reduce.1), calls=%async_computation.1 | async-start | bytes 1048576 | tf_op jit(solution)/shard_map/all_to_all | solution.py:421
  61.0 14.9 %collective-permute-start.7 = (bf16[3,64,512]{2,1,0:T(8,128)(2,1)S(1)}, bf16[3,64,512]{2,1,0:T(8,128)(2,1)}, u32[]{:S(2)}, u32[]{:S(2)}) collective-permute-start(bf16[3,64,512]{2,1,0:T(8,128)(2,1)S(1)} %get-tuple-element.15.refs_3_), channel_id=1, source_target_pairs={{0,125},{1,4},{2,127},{3,6},{4,1},{5,8},{6,3},{7,10},{8,5},{9,12},... | collective-permute-start | bytes 589832 | tf_op jit(solution)/shard_map/ppermute | solution.py:418

commit v8 on v7

--- a/solution.py
+++ b/solution.py
@@ -503,7 +503,7 @@
             pltpu.SemaphoreType.DMA((3,)),
         ],
         compiler_params=params(48),
-        cost_estimate=cost_of(4 * 10**9),
+        cost_estimate=cost_of(12 * 10**9),
         name="near",
     )(
         sc, *in_hbm(near_col[0], near_tiles[0]),

time: 95.5 us -> 99.7 us (1.044)
  starting transfers between devices: 48.5 us -> 57.3 us
  waiting for transfers between devices: 12.7 us -> 6.34 us
  blocking collectives: 15.1 us -> 16.7 us
    ppermute x4, starting transfers between devices: 25.9 us -> 37.4 us  [sent(): return lax.ppermute(v, CLU, pairs)]
    all_to_all x2, waiting for transfers between devices: 11.4 us -> 5.07 us  [exchanged(): return lax.all_to_all(v, axis, split_axis=0, concat_axis=0, tiled=True)]
    all_to_all x2, starting transfers between devices: 14.3 us -> 11.6 us  [exchanged(): return lax.all_to_all(v, axis, split_axis=0, concat_axis=0, tiled=True)]
    all_to_all x1, blocking collectives: 15.1 us -> 16.7 us  [exchanged(): return lax.all_to_all(v, axis, split_axis=0, concat_axis=0, tiled=True)]
where the time goes in v8:
time: 99.7 us; the launch traced here: 99 us
  starting transfers between devices  57.3 us (57%)
  Pallas kernels  17.5 us (18%)
  blocking collectives  16.7 us (17%)
  waiting for transfers between devices  6.34 us (6%)
    ppermute x4, starting transfers between devices, sent(): return lax.ppermute(v, CLU, pairs)  37.4 us
    all_to_all x1, blocking collectives, exchanged(): return lax.all_to_all(v, axis, split_axis=0, concat_axis=0, tiled=True)  16.7 us
    all_to_all x2, starting transfers between devices, exchanged(): return lax.all_to_all(v, axis, split_axis=0, concat_axis=0, tiled=True)  11.6 us
    ppermute x4, starting transfers between devices, swapped(): return lax.ppermute(v, 'clu_2', [(0, 1), (1, 0)])  8.29 us
    pallas_call x1, Pallas kernels, on_device(): pl.pallas_call(functools.partial(near_kernel, clusters), out_shape=shape_...  6.65 us
    all_to_all x2, waiting for transfers between devices, exchanged(): return lax.all_to_all(v, axis, split_axis=0, concat_axis=0, tiled=True)  5.07 us
    pallas_call x1, Pallas kernels, on_device(): pl.pallas_call(functools.partial(mix_kernel, clusters, planes), out_shape...  2.98 us
    pallas_call x1, Pallas kernels, on_device(): pl.pallas_call(functools.partial(side_kernel, planes), out_shape=(shape_o...  2.9 us
  transfers between devices with their start and end apart: 10, of which 3 were waited for; matrix products, arithmetic and copies ran while one was open for 1% of the time, Pallas kernels for 12%

profile of v8, /device:TPU:32, one launch (start us, length us, event | category | flops | bytes accessed | tf_op | source)
XLA Modules:
  0.0 99.0 jit_solution(7900949403385854756)
XLA Ops:
  0.0 0.1 pad_add_fusion.sc
  0.1 1.8 %dress.1 = (bf16[784,128]{1,0:T(8,128)(2,1)S(1)}, bf16[784,512]{1,0:T(8,128)(2,1)S(1)}) custom-call(s32[4]{0:T(128)S(1)} %pad_add_fusion.sc, s32[1,256]{1,0:T(1,128)} %bitcast.21, bf16[768,512]{1,0:T(8,128)(2,1)} %bitcast.18), custom_call_target="tpu_custom_call" | custom-call | tf_op jit(solution)/shard_map/dress/pallas_call | solution.py:424
  1.9 0.0 copy-start.4
  1.9 0.0 copy-start.2
  2.0 2.1 %collective-permute-start.3 = (bf16[784,512]{1,0:T(8,128)(2,1)S(1)}, bf16[784,512]{1,0:T(8,128)(2,1)S(1)}, u32[]{:S(2)}, u32[]{:S(2)}) collective-permute-start(bf16[784,512]{1,0:T(8,128)(2,1)S(1)} %tie.2.own.own_ref), channel_id=1, source_target_pairs={{0,1},{1,0},{2,3},{3,2},{4,5},{5,4},{6,7},{7,6},{8,9},{9,8},{10,11... | collective-permute-start | bytes 2408456 | tf_op jit(solution)/shard_map/ppermute | solution.py:414
  4.0 7.5 %collective-permute-start.5 = (bf16[784,128]{1,0:T(8,128)(2,1)S(1)}, bf16[784,128]{1,0:T(8,128)(2,1)S(1)}, u32[]{:S(2)}, u32[]{:S(2)}) collective-permute-start(bf16[784,128]{1,0:T(8,128)(2,1)S(1)} %get-tuple-element.12), channel_id=1, source_target_pairs={{0,127},{1,2},{2,1},{3,4},{4,3},{5,6},{6,5},{7,8},{8,7},{9,10},{10... | collective-permute-start | bytes 602120 | tf_op jit(solution)/shard_map/ppermute | solution.py:418
  11.5 8.2 %collective-permute-start.1 = (bf16[784,512]{1,0:T(8,128)(2,1)S(1)}, bf16[784,512]{1,0:T(8,128)(2,1)S(1)}, u32[]{:S(2)}, u32[]{:S(2)}) collective-permute-start(bf16[784,512]{1,0:T(8,128)(2,1)S(1)} %tie.2.own.own_ref), channel_id=1, source_target_pairs={{0,126},{1,3},{2,0},{3,5},{4,2},{5,7},{6,4},{7,9},{8,6},{9,11},{10... | collective-permute-start | bytes 2408456 | tf_op jit(solution)/shard_map/ppermute | solution.py:418
  19.7 1.9 %collective-permute-start = (bf16[784,512]{1,0:T(8,128)(2,1)S(1)}, bf16[784,512]{1,0:T(8,128)(2,1)S(1)}, u32[]{:S(2)}, u32[]{:S(2)}) collective-permute-start(bf16[784,512]{1,0:T(8,128)(2,1)S(1)} %tie.2.own.own_ref), channel_id=1, source_target_pairs={{0,2},{1,127},{2,4},{3,1},{4,6},{5,3},{6,8},{7,5},{8,10},{9,7},{10... | collective-permute-start | bytes 2408456 | tf_op jit(solution)/shard_map/ppermute | solution.py:418
  21.7 0.0 collective-permute-done.5.halo_ref
  21.7 0.0 collective-permute-done.3.pair.pair_ref
  21.7 0.0 copy-start.3
  21.7 0.0 copy-done.4
  21.7 1.4 %pieces.1 = (f32[32,128]{1,0:T(8,128)S(1)}, f32[32,128]{1,0:T(8,128)S(1)}) custom-call(s32[4]{0:T(128)S(1)} %pad_add_fusion.sc, bf16[784,128]{1,0:T(8,128)(2,1)S(1)} %collective-permute-done.5.halo_ref, bf16[784,512]{1,0:T(8,128)(2,1)S(1)} %tie.2.own.own_ref, bf16[784,512]{1,0:T(8,128)(2,1)S(1)} %collective-permute-done.3.pair.pair_ref, ...), custom_call_target="tpu_custom_call" | custom-call | flops 5000000000 | bytes 1000000 | tf_op jit(solution)/shard_map/pieces/pallas_call | solution.py:443
  23.1 0.0 copy-done.2
  23.1 0.0 copy-done.3
  23.2 1.9 %collective-permute-start.6 = (f32[32,128]{1,0:T(8,128)S(1)}, f32[32,128]{1,0:T(8,128)S(1)}, u32[]{:S(2)}, u32[]{:S(2)}) collective-permute-start(f32[32,128]{1,0:T(8,128)S(1)} %get-tuple-element.14), channel_id=1, source_target_pairs={{0,1},{1,0},{2,3},{3,2},{4,5},{5,4},{6,7},{7,6},{8,9},{9,8},{10,11... | collective-permute-start | bytes 49160 | tf_op jit(solution)/shard_map/ppermute | solution.py:414
  25.1 1.1 %collective-permute-done.6 = f32[32,128]{1,0:T(8,128)S(1)} collective-permute-done((f32[32,128]{1,0:T(8,128)S(1)}, f32[32,128]{1,0:T(8,128)S(1)}, u32[]{:S(2)}, u32[]{:S(2)}) %collective-permute-start.6) | collective-permute-done | bytes 16416 | tf_op jit(solution)/shard_map/ppermute | solution.py:414
  26.2 0.7 broadcast_in_dim.3
  27.0 6.8 %all-to-all-start = ((f32[16,32,128]{2,1,0:T(8,128)}), f32[16,32,128]{2,1,0:T(8,128)S(1)}, u32[]{:S(2)}, u32[]{:S(2)}) async-start(f32[16,32,128]{2,1,0:T(8,128)} %broadcast_in_dim.3), calls=%async_computation | async-start | bytes 524288 | tf_op jit(solution)/shard_map/all_to_all | solution.py:421
  33.7 0.1 collective-permute-done.1.far_z.refs_2_
  33.8 0.0 copy-start.1
  33.8 1.9 %collective-permute-start.2 = (bf16[784,512]{1,0:T(8,128)(2,1)S(1)}, bf16[784,512]{1,0:T(8,128)(2,1)}, u32[]{:S(2)}, u32[]{:S(2)}) collective-permute-start(bf16[784,512]{1,0:T(8,128)(2,1)S(1)} %collective-permute-done.1.far_z.refs_2_), channel_id=1, source_target_pairs={{0,1},{1,0},{2,3},{3,2},{4,5},{5,4},{6,7},{7,6},{8,9},{9,8},{10,11... | collective-permute-start | bytes 2408456 | tf_op jit(solution)/shard_map/ppermute | solution.py:414
  35.8 0.0 collective-permute-done.near_z.refs_1_
  35.8 0.0 copy-start
  35.8 2.4 %collective-permute-start.4 = (bf16[784,512]{1,0:T(8,128)(2,1)S(1)}, bf16[784,512]{1,0:T(8,128)(2,1)}, u32[]{:S(2)}, u32[]{:S(2)}) collective-permute-start(bf16[784,512]{1,0:T(8,128)(2,1)S(1)} %collective-permute-done.near_z.refs_1_), channel_id=1, source_target_pairs={{0,1},{1,0},{2,3},{3,2},{4,5},{5,4},{6,7},{7,6},{8,9},{9,8},{10,11... | collective-permute-start | bytes 2408456 | tf_op jit(solution)/shard_map/ppermute | solution.py:414
  38.2 2.9 %side.1 = (bf16[3,64,512]{2,1,0:T(8,128)(2,1)S(1)}, bf16[512,384]{1,0:T(8,128)(2,1)S(1)}) custom-call(s32[4]{0:T(128)S(1)} %pad_add_fusion.sc, s32[16]{0:T(128)} %bitcast.22, s32[16]{0:T(128)} %bitcast.23, f32[16]{0:T(128)} %bitcast.24, bf16[16,32,32]{2,1,0:T(8,128)(2,1)} %bitcast.20, bf16[784,512]{1,0:T(8,128)(2,1)} %copy-done.2, ...), custom_call_target="tpu_custom_call" | custom-call | tf_op jit(solution)/shard_map/side/pallas_call | solution.py:454
  41.1 19.8 %collective-permute-start.7 = (bf16[3,64,512]{2,1,0:T(8,128)(2,1)S(1)}, bf16[3,64,512]{2,1,0:T(8,128)(2,1)}, u32[]{:S(2)}, u32[]{:S(2)}) collective-permute-start(bf16[3,64,512]{2,1,0:T(8,128)(2,1)S(1)} %get-tuple-element.15.refs_3_), channel_id=1, source_target_pairs={{0,125},{1,4},{2,127},{3,6},{4,1},{5,8},{6,3},{7,10},{8,5},{9,12},... | collective-permute-start | bytes 589832 | tf_op jit(solution)/shard_map/ppermute | solution.py:418
  60.9 0.0 all-to-all-done.refs_0_
  60.9 0.9 reduce.1
  61.8 0.0 copy-done.1
  61.8 0.0 copy-done
  61.8 4.9 %all-to-all-start.1 = ((f32[32,32,128]{2,1,0:T(8,128)}), f32[32,32,128]{2,1,0:T(8,128)S(1)}, u32[]{:S(2)}, u32[]{:S(2)}) async-start(f32[32,32,128]{2,1,0:T(8,128)} %reduce.1), calls=%async_computation.1 | async-start | bytes 1048576 | tf_op jit(solution)/shard_map/all_to_all | solution.py:421
  66.7 0.0 collective-permute-done.2.pair_far
  66.7 0.0 collective-permute-done.4.pair_near
  66.7 6.7 %near.1 = f32[768,512]{1,0:T(8,128)S(1)} custom-call(s32[4]{0:T(128)S(1)} %pad_add_fusion.sc, s32[2]{0:T(128)} %bitcast.25, bf16[2,768,768]{2,1,0:T(8,128)(2,1)} %bitcast.16, bf16[784,512]{1,0:T(8,128)(2,1)} %copy-done.2, bf16[784,512]{1,0:T(8,128)(2,1)} %copy-done, bf16[784,512]{1,0:T(8,128)(2,1)} %collective-permute-done.2.pair_far, ...), custom_call_target="tpu_custom_call" | custom-call | flops 12000000000 | bytes 1000000 | tf_op jit(solution)/shard_map/near/pallas_call | solution.py:489
  73.4 0.0 collective-permute-done.7.thin
  73.4 5.1 %all-to-all-done.1.sums = f32[32,32,128]{2,1,0:T(8,128)S(1)} async-done(((f32[32,32,128]{2,1,0:T(8,128)}), f32[32,32,128]{2,1,0:T(8,128)S(1)}, u32[]{:S(2)}, u32[]{:S(2)}) %all-to-all-start.1) | async-done | bytes 524320 | tf_op jit(solution)/shard_map/all_to_all | solution.py:421
  78.4 3.0 %mix.1 = bf16[4,768,128]{2,1,0:T(8,128)(2,1)S(1)} custom-call(s32[4]{0:T(128)S(1)} %pad_add_fusion.sc, s32[2]{0:T(128)} %bitcast.26, f32[768,512]{1,0:T(8,128)S(1)} %near.1, f32[32,32,128]{2,1,0:T(8,128)S(1)} %all-to-all-done.1.sums, bf16[512,768]{1,0:T(8,128)(2,1)} %bitcast.19, bf16[512,384]{1,0:T(8,128)(2,1)S(1)} %get-tuple-element.16.refs_4_.mixed, ...), custom_call_target="tpu_custom_call" | custom-call | tf_op jit(solution)/shard_map/mix/pallas_call | solution.py:512
  81.4 16.7 %all_to_all.15.arrived_ref = bf16[4,768,128]{2,1,0:T(8,128)(2,1)S(1)} all-to-all(bf16[4,768,128]{2,1,0:T(8,128)(2,1)S(1)} %mix.1), channel_id=1, replica_groups=mesh['grp'=4,'clu_0'=4,'clu_1'=16,'clu_2'=2] {'grp'}, dimensions={0} | all-to-all | bytes 1572864 | tf_op jit(solution)/shard_map/all_to_all | solution.py:421
  98.2 0.8 last.1
  (3 shorter events, 0.0 us)
Async XLA Ops:
  1.9 19.8 %copy-start.4 = (bf16[2,32,3,256]{3,1,2,0:T(8,128)(2,1)S(1)}, bf16[2,32,3,256]{3,1,2,0:T(8,128)(2,1)}, u32[]{:S(2)}) copy-start(bf16[2,32,3,256]{3,1,2,0:T(8,128)(2,1)} %param.12) | copy-start | bytes 294916
  1.9 21.2 %copy-start.2 = (bf16[784,512]{1,0:T(8,128)(2,1)}, bf16[784,512]{1,0:T(8,128)(2,1)S(1)}, u32[]{:S(2)}) copy-start(bf16[784,512]{1,0:T(8,128)(2,1)S(1)} %tie.2.own.own_ref) | copy-start | bytes 2408452
  2.0 19.7 %collective-permute-start.3 = (bf16[784,512]{1,0:T(8,128)(2,1)S(1)}, bf16[784,512]{1,0:T(8,128)(2,1)S(1)}, u32[]{:S(2)}, u32[]{:S(2)}) collective-permute-start(bf16[784,512]{1,0:T(8,128)(2,1)S(1)} %tie.2.own.own_ref), channel_id=1, source_target_pairs={{0,1},{1,0},{2,3},{3,2},{4,5},{5,4},{6,7},{7,6},{8,9},{9,8},{10,11... | collective-permute-start | bytes 2408456 | tf_op jit(solution)/shard_map/ppermute | solution.py:414
  4.0 17.7 %collective-permute-start.5 = (bf16[784,128]{1,0:T(8,128)(2,1)S(1)}, bf16[784,128]{1,0:T(8,128)(2,1)S(1)}, u32[]{:S(2)}, u32[]{:S(2)}) collective-permute-start(bf16[784,128]{1,0:T(8,128)(2,1)S(1)} %get-tuple-element.12), channel_id=1, source_target_pairs={{0,127},{1,2},{2,1},{3,4},{4,3},{5,6},{6,5},{7,8},{8,7},{9,10},{10... | collective-permute-start | bytes 602120 | tf_op jit(solution)/shard_map/ppermute | solution.py:418
  11.5 22.3 %collective-permute-start.1 = (bf16[784,512]{1,0:T(8,128)(2,1)S(1)}, bf16[784,512]{1,0:T(8,128)(2,1)S(1)}, u32[]{:S(2)}, u32[]{:S(2)}) collective-permute-start(bf16[784,512]{1,0:T(8,128)(2,1)S(1)} %tie.2.own.own_ref), channel_id=1, source_target_pairs={{0,126},{1,3},{2,0},{3,5},{4,2},{5,7},{6,4},{7,9},{8,6},{9,11},{10... | collective-permute-start | bytes 2408456 | tf_op jit(solution)/shard_map/ppermute | solution.py:418
  19.7 16.0 %collective-permute-start = (bf16[784,512]{1,0:T(8,128)(2,1)S(1)}, bf16[784,512]{1,0:T(8,128)(2,1)S(1)}, u32[]{:S(2)}, u32[]{:S(2)}) collective-permute-start(bf16[784,512]{1,0:T(8,128)(2,1)S(1)} %tie.2.own.own_ref), channel_id=1, source_target_pairs={{0,2},{1,127},{2,4},{3,1},{4,6},{5,3},{6,8},{7,5},{8,10},{9,7},{10... | collective-permute-start | bytes 2408456 | tf_op jit(solution)/shard_map/ppermute | solution.py:418
  21.7 1.4 %copy-start.3 = (bf16[784,512]{1,0:T(8,128)(2,1)}, bf16[784,512]{1,0:T(8,128)(2,1)S(1)}, u32[]{:S(2)}) copy-start(bf16[784,512]{1,0:T(8,128)(2,1)S(1)} %collective-permute-done.3.pair.pair_ref) | copy-start | bytes 2408452
  23.2 3.1 %collective-permute-start.6 = (f32[32,128]{1,0:T(8,128)S(1)}, f32[32,128]{1,0:T(8,128)S(1)}, u32[]{:S(2)}, u32[]{:S(2)}) collective-permute-start(f32[32,128]{1,0:T(8,128)S(1)} %get-tuple-element.14), channel_id=1, source_target_pairs={{0,1},{1,0},{2,3},{3,2},{4,5},{5,4},{6,7},{7,6},{8,9},{9,8},{10,11... | collective-permute-start | bytes 49160 | tf_op jit(solution)/shard_map/ppermute | solution.py:414
  27.0 33.9 %all-to-all-start = ((f32[16,32,128]{2,1,0:T(8,128)}), f32[16,32,128]{2,1,0:T(8,128)S(1)}, u32[]{:S(2)}, u32[]{:S(2)}) async-start(f32[16,32,128]{2,1,0:T(8,128)} %broadcast_in_dim.3), calls=%async_computation | async-start | bytes 524288 | tf_op jit(solution)/shard_map/all_to_all | solution.py:421
  33.8 27.9 %copy-start.1 = (bf16[784,512]{1,0:T(8,128)(2,1)}, bf16[784,512]{1,0:T(8,128)(2,1)S(1)}, u32[]{:S(2)}) copy-start(bf16[784,512]{1,0:T(8,128)(2,1)S(1)} %collective-permute-done.1.far_z.refs_2_) | copy-start | bytes 2408452
  33.8 32.8 %collective-permute-start.2 = (bf16[784,512]{1,0:T(8,128)(2,1)S(1)}, bf16[784,512]{1,0:T(8,128)(2,1)}, u32[]{:S(2)}, u32[]{:S(2)}) collective-permute-start(bf16[784,512]{1,0:T(8,128)(2,1)S(1)} %collective-permute-done.1.far_z.refs_2_), channel_id=1, source_target_pairs={{0,1},{1,0},{2,3},{3,2},{4,5},{5,4},{6,7},{7,6},{8,9},{9,8},{10,11... | collective-permute-start | bytes 2408456 | tf_op jit(solution)/shard_map/ppermute | solution.py:414
  35.8 26.0 %copy-start = (bf16[784,512]{1,0:T(8,128)(2,1)}, bf16[784,512]{1,0:T(8,128)(2,1)S(1)}, u32[]{:S(2)}) copy-start(bf16[784,512]{1,0:T(8,128)(2,1)S(1)} %collective-permute-done.near_z.refs_1_) | copy-start | bytes 2408452
  35.8 30.9 %collective-permute-start.4 = (bf16[784,512]{1,0:T(8,128)(2,1)S(1)}, bf16[784,512]{1,0:T(8,128)(2,1)}, u32[]{:S(2)}, u32[]{:S(2)}) collective-permute-start(bf16[784,512]{1,0:T(8,128)(2,1)S(1)} %collective-permute-done.near_z.refs_1_), channel_id=1, source_target_pairs={{0,1},{1,0},{2,3},{3,2},{4,5},{5,4},{6,7},{7,6},{8,9},{9,8},{10,11... | collective-permute-start | bytes 2408456 | tf_op jit(solution)/shard_map/ppermute | solution.py:414
  41.1 32.3 %collective-permute-start.7 = (bf16[3,64,512]{2,1,0:T(8,128)(2,1)S(1)}, bf16[3,64,512]{2,1,0:T(8,128)(2,1)}, u32[]{:S(2)}, u32[]{:S(2)}) collective-permute-start(bf16[3,64,512]{2,1,0:T(8,128)(2,1)S(1)} %get-tuple-element.15.refs_3_), channel_id=1, source_target_pairs={{0,125},{1,4},{2,127},{3,6},{4,1},{5,8},{6,3},{7,10},{8,5},{9,12},... | collective-permute-start | bytes 589832 | tf_op jit(solution)/shard_map/ppermute | solution.py:418
  61.8 16.6 %all-to-all-start.1 = ((f32[32,32,128]{2,1,0:T(8,128)}), f32[32,32,128]{2,1,0:T(8,128)S(1)}, u32[]{:S(2)}, u32[]{:S(2)}) async-start(f32[32,32,128]{2,1,0:T(8,128)} %reduce.1), calls=%async_computation.1 | async-start | bytes 1048576 | tf_op jit(solution)/shard_map/all_to_all | solution.py:421

commit v9 on v7

--- a/solution.py
+++ b/solution.py
@@ -471,7 +471,9 @@
     )(
         sc, *in_hbm(far_target[0], far_rank[0], far_scale[0], far_coupling[0], block), halo, level_sum,
     )
-    many = tied(many, near_z, far_z, thin, mixed)
+    near_z = tied(near_z, thin, mixed)
+    far_z = tied(far_z, thin, mixed)
+    many = tied(many, near_z, far_z)
     thin = sent(thin, 3)
     pair_near = swapped(near_z)
     pair_far = swapped(far_z)
@@ -512,7 +514,7 @@
     split = pl.pallas_call(
         functools.partial(mix_kernel, clusters, planes),
         out_shape=shape_of((groups, rows, part), BF16),
-        in_specs=[SMEM, SMEM, ANY, ANY, HBM, ANY, HBM, HBM, HBM],
+        in_specs=[SMEM, SMEM, HBM, ANY, HBM, ANY, HBM, HBM, HBM],
         out_specs=HBM,
         scratch_shapes=[
             pltpu.VMEM((rows, columns), F32),
@@ -535,7 +537,7 @@
         compiler_params=params(24),
         name="mix",
     )(
-        sc, *in_hbm(near_col[0]), near, sums, *in_hbm(far_basis.reshape(far_count * rank, rows)), mixed,
+        sc, *in_hbm(near_col[0], near), sums, *in_hbm(far_basis.reshape(far_count * rank, rows)), mixed,
         *in_hbm(near_tiles[0], thin, near_z),
     )
     arrived = exchanged(split, "grp")

time: 95.5 us -> 96.5 us (1.010)
  local copies, waits for them, and re-layouts: 0.75 us -> 1.9 us
    unnamed x10 -> x12, local copies, waits for them, and re-layouts: 0.02 us -> 1.17 us
  transfers between devices with their start and end apart: 10 -> 10, of which waited for: 3 -> 2; matrix products, arithmetic and copies ran while one was open for 1% -> 1% of each run, Pallas kernels for 12% -> 12%
where the time goes in v9:
time: 96.5 us; the launch traced here: 96.4 us
  starting transfers between devices  47.8 us (50%)
  Pallas kernels  17.9 us (19%)
  blocking collectives  15.8 us (16%)
  waiting for transfers between devices  12.6 us (13%)
  local copies, waits for them, and re-layouts  1.9 us (2%)
    ppermute x4, starting transfers between devices, sent(): return lax.ppermute(v, CLU, pairs)  25.2 us
    all_to_all x1, blocking collectives, exchanged(): return lax.all_to_all(v, axis, split_axis=0, concat_axis=0, tiled=True)  15.8 us
    all_to_all x2, starting transfers between devices, exchanged(): return lax.all_to_all(v, axis, split_axis=0, concat_axis=0, tiled=True)  14.3 us
    all_to_all x2, waiting for transfers between devices, exchanged(): return lax.all_to_all(v, axis, split_axis=0, concat_axis=0, tiled=True)  11.5 us
    ppermute x4, starting transfers between devices, swapped(): return lax.ppermute(v, 'clu_2', [(0, 1), (1, 0)])  8.3 us
    pallas_call x1, Pallas kernels, on_device(): pl.pallas_call(functools.partial(near_kernel, clusters), out_shape=shape_...  6.58 us
    pallas_call x1, Pallas kernels, on_device(): pl.pallas_call(functools.partial(mix_kernel, clusters, planes), out_shape...  3.5 us
    pallas_call x1, Pallas kernels, on_device(): pl.pallas_call(functools.partial(side_kernel, planes), out_shape=(shape_o...  2.9 us
  transfers between devices with their start and end apart: 10, of which 2 were waited for; matrix products, arithmetic and copies ran while one was open for 1% of the time, Pallas kernels for 12%

profile of v9, /device:TPU:32, one launch (start us, length us, event | category | flops | bytes accessed | tf_op | source)
XLA Modules:
  0.0 96.4 jit_solution(5161057780043471774)
XLA Ops:
  0.0 0.1 pad_add_fusion.sc
  0.1 1.8 %dress.1 = (bf16[784,128]{1,0:T(8,128)(2,1)S(1)}, bf16[784,512]{1,0:T(8,128)(2,1)S(1)}) custom-call(s32[4]{0:T(128)S(1)} %pad_add_fusion.sc, s32[1,256]{1,0:T(1,128)} %bitcast.21, bf16[768,512]{1,0:T(8,128)(2,1)} %bitcast.18), custom_call_target="tpu_custom_call" | custom-call | tf_op jit(solution)/shard_map/dress/pallas_call | solution.py:424
  1.9 0.0 copy-start.5
  1.9 0.0 copy-start.3
  2.0 2.1 %collective-permute-start.2 = (bf16[784,512]{1,0:T(8,128)(2,1)S(1)}, bf16[784,512]{1,0:T(8,128)(2,1)S(1)}, u32[]{:S(2)}, u32[]{:S(2)}) collective-permute-start(bf16[784,512]{1,0:T(8,128)(2,1)S(1)} %tie.4.own_ref.own), channel_id=1, source_target_pairs={{0,1},{1,0},{2,3},{3,2},{4,5},{5,4},{6,7},{7,6},{8,9},{9,8},{10,11... | collective-permute-start | bytes 2408456 | tf_op jit(solution)/shard_map/ppermute | solution.py:414
  4.0 7.5 %collective-permute-start.1 = (bf16[784,128]{1,0:T(8,128)(2,1)S(1)}, bf16[784,128]{1,0:T(8,128)(2,1)S(1)}, u32[]{:S(2)}, u32[]{:S(2)}) collective-permute-start(bf16[784,128]{1,0:T(8,128)(2,1)S(1)} %get-tuple-element.12), channel_id=1, source_target_pairs={{0,127},{1,2},{2,1},{3,4},{4,3},{5,6},{6,5},{7,8},{8,7},{9,10},{10... | collective-permute-start | bytes 602120 | tf_op jit(solution)/shard_map/ppermute | solution.py:418
  11.5 8.2 %collective-permute-start.4 = (bf16[784,512]{1,0:T(8,128)(2,1)S(1)}, bf16[784,512]{1,0:T(8,128)(2,1)S(1)}, u32[]{:S(2)}, u32[]{:S(2)}) collective-permute-start(bf16[784,512]{1,0:T(8,128)(2,1)S(1)} %tie.4.own_ref.own), channel_id=1, source_target_pairs={{0,126},{1,3},{2,0},{3,5},{4,2},{5,7},{6,4},{7,9},{8,6},{9,11},{10... | collective-permute-start | bytes 2408456 | tf_op jit(solution)/shard_map/ppermute | solution.py:418
  19.7 1.9 %collective-permute-start = (bf16[784,512]{1,0:T(8,128)(2,1)S(1)}, bf16[784,512]{1,0:T(8,128)(2,1)S(1)}, u32[]{:S(2)}, u32[]{:S(2)}) collective-permute-start(bf16[784,512]{1,0:T(8,128)(2,1)S(1)} %tie.4.own_ref.own), channel_id=1, source_target_pairs={{0,2},{1,127},{2,4},{3,1},{4,6},{5,3},{6,8},{7,5},{8,10},{9,7},{10... | collective-permute-start | bytes 2408456 | tf_op jit(solution)/shard_map/ppermute | solution.py:418
  21.7 0.0 collective-permute-done.1.halo_ref
  21.7 0.0 collective-permute-done.2.pair_ref.pair
  21.7 0.0 copy-start.4
  21.7 0.0 copy-done.5
  21.7 1.4 %pieces.1 = (f32[32,128]{1,0:T(8,128)S(1)}, f32[32,128]{1,0:T(8,128)S(1)}) custom-call(s32[4]{0:T(128)S(1)} %pad_add_fusion.sc, bf16[784,128]{1,0:T(8,128)(2,1)S(1)} %collective-permute-done.1.halo_ref, bf16[784,512]{1,0:T(8,128)(2,1)S(1)} %tie.4.own_ref.own, bf16[784,512]{1,0:T(8,128)(2,1)S(1)} %collective-permute-done.2.pair_ref.pair, ...), custom_call_target="tpu_custom_call" | custom-call | flops 5000000000 | bytes 1000000 | tf_op jit(solution)/shard_map/pieces/pallas_call | solution.py:443
  23.1 0.0 copy-done.3
  23.1 0.0 copy-done.4
  23.2 1.9 %collective-permute-start.3 = (f32[32,128]{1,0:T(8,128)S(1)}, f32[32,128]{1,0:T(8,128)S(1)}, u32[]{:S(2)}, u32[]{:S(2)}) collective-permute-start(f32[32,128]{1,0:T(8,128)S(1)} %get-tuple-element.14), channel_id=1, source_target_pairs={{0,1},{1,0},{2,3},{3,2},{4,5},{5,4},{6,7},{7,6},{8,9},{9,8},{10,11... | collective-permute-start | bytes 49160 | tf_op jit(solution)/shard_map/ppermute | solution.py:414
  25.1 1.1 %collective-permute-done.3 = f32[32,128]{1,0:T(8,128)S(1)} collective-permute-done((f32[32,128]{1,0:T(8,128)S(1)}, f32[32,128]{1,0:T(8,128)S(1)}, u32[]{:S(2)}, u32[]{:S(2)}) %collective-permute-start.3) | collective-permute-done | bytes 16416 | tf_op jit(solution)/shard_map/ppermute | solution.py:414
  26.2 0.7 broadcast_in_dim.3
  27.0 6.8 %all-to-all-start = ((f32[16,32,128]{2,1,0:T(8,128)}), f32[16,32,128]{2,1,0:T(8,128)S(1)}, u32[]{:S(2)}, u32[]{:S(2)}) async-start(f32[16,32,128]{2,1,0:T(8,128)} %broadcast_in_dim.3), calls=%async_computation | async-start | bytes 524288 | tf_op jit(solution)/shard_map/all_to_all | solution.py:421
  33.7 2.9 %side.1 = (bf16[3,64,512]{2,1,0:T(8,128)(2,1)S(1)}, bf16[512,384]{1,0:T(8,128)(2,1)S(1)}) custom-call(s32[4]{0:T(128)S(1)} %pad_add_fusion.sc, s32[16]{0:T(128)} %bitcast.22, s32[16]{0:T(128)} %bitcast.23, f32[16]{0:T(128)} %bitcast.24, bf16[16,32,32]{2,1,0:T(8,128)(2,1)} %bitcast.20, bf16[784,512]{1,0:T(8,128)(2,1)} %copy-done.3, ...), custom_call_target="tpu_custom_call" | custom-call | tf_op jit(solution)/shard_map/side/pallas_call | solution.py:454
  36.6 0.0 collective-permute-done.4.refs_0_
  36.7 0.0 copy-start.1
  36.7 1.9 %collective-permute-start.5 = (bf16[784,512]{1,0:T(8,128)(2,1)S(1)}, bf16[784,512]{1,0:T(8,128)(2,1)}, u32[]{:S(2)}, u32[]{:S(2)}) collective-permute-start(bf16[784,512]{1,0:T(8,128)(2,1)S(1)} %tie.6.far_z.refs_2_), channel_id=1, source_target_pairs={{0,1},{1,0},{2,3},{3,2},{4,5},{5,4},{6,7},{7,6},{8,9},{9,8},{10,11... | collective-permute-start | bytes 2408456 | tf_op jit(solution)/shard_map/ppermute | solution.py:414
  38.6 0.0 collective-permute-done.refs_0_
  38.6 0.0 copy-start
  38.6 2.4 %collective-permute-start.6 = (bf16[784,512]{1,0:T(8,128)(2,1)S(1)}, bf16[784,512]{1,0:T(8,128)(2,1)S(1)}, u32[]{:S(2)}, u32[]{:S(2)}) collective-permute-start(bf16[784,512]{1,0:T(8,128)(2,1)S(1)} %tie.5.near_z.refs_1_), channel_id=1, source_target_pairs={{0,1},{1,0},{2,3},{3,2},{4,5},{5,4},{6,7},{7,6},{8,9},{9,8},{10,11... | collective-permute-start | bytes 2408456 | tf_op jit(solution)/shard_map/ppermute | solution.py:414
  41.0 11.5 %all-to-all-done.refs_0_ = f32[16,32,128]{2,1,0:T(8,128)S(1)} async-done(((f32[16,32,128]{2,1,0:T(8,128)}), f32[16,32,128]{2,1,0:T(8,128)S(1)}, u32[]{:S(2)}, u32[]{:S(2)}) %all-to-all-start) | async-done | bytes 262176 | tf_op jit(solution)/shard_map/all_to_all | solution.py:421
  52.5 0.9 reduce.1
  53.4 0.0 copy-done.1
  53.4 7.5 %all-to-all-start.1 = ((f32[32,32,128]{2,1,0:T(8,128)}), f32[32,32,128]{2,1,0:T(8,128)S(1)}, u32[]{:S(2)}, u32[]{:S(2)}) async-start(f32[32,32,128]{2,1,0:T(8,128)} %reduce.1), calls=%async_computation.1 | async-start | bytes 1048576 | tf_op jit(solution)/shard_map/all_to_all | solution.py:421
  60.9 7.5 %collective-permute-start.7 = (bf16[3,64,512]{2,1,0:T(8,128)(2,1)S(1)}, bf16[3,64,512]{2,1,0:T(8,128)(2,1)}, u32[]{:S(2)}, u32[]{:S(2)}) collective-permute-start(bf16[3,64,512]{2,1,0:T(8,128)(2,1)S(1)} %get-tuple-element.15.refs_1_), channel_id=1, source_target_pairs={{0,125},{1,4},{2,127},{3,6},{4,1},{5,8},{6,3},{7,10},{8,5},{9,12},... | collective-permute-start | bytes 589832 | tf_op jit(solution)/shard_map/ppermute | solution.py:418
  68.5 0.0 collective-permute-done.5.pair_far
  68.5 0.0 collective-permute-done.6.pair_near
  68.5 0.0 copy-done
  68.5 6.6 %near.1 = f32[768,512]{1,0:T(8,128)S(1)} custom-call(s32[4]{0:T(128)S(1)} %pad_add_fusion.sc, s32[2]{0:T(128)} %bitcast.25, bf16[2,768,768]{2,1,0:T(8,128)(2,1)} %bitcast.16, bf16[784,512]{1,0:T(8,128)(2,1)} %copy-done.3, bf16[784,512]{1,0:T(8,128)(2,1)} %copy-done, bf16[784,512]{1,0:T(8,128)(2,1)} %collective-permute-done.5.pair_far, ...), custom_call_target="tpu_custom_call" | custom-call | flops 4000000000 | bytes 1000000 | tf_op jit(solution)/shard_map/near/pallas_call | solution.py:491
  75.1 0.0 copy-start.2
  75.1 1.1 %copy-done.2 = f32[768,512]{1,0:T(8,128)} copy-done((f32[768,512]{1,0:T(8,128)}, f32[768,512]{1,0:T(8,128)S(1)}, u32[]{:S(2)}) %copy-start.2) | copy-done | bytes 1572888
  76.3 0.0 collective-permute-done.7.thin
  76.3 0.0 all-to-all-done.1.sums
  76.3 3.5 %mix.1 = bf16[4,768,128]{2,1,0:T(8,128)(2,1)S(1)} custom-call(s32[4]{0:T(128)S(1)} %pad_add_fusion.sc, s32[2]{0:T(128)} %bitcast.26, f32[768,512]{1,0:T(8,128)} %copy-done.2, f32[32,32,128]{2,1,0:T(8,128)S(1)} %all-to-all-done.1.sums, bf16[512,768]{1,0:T(8,128)(2,1)} %bitcast.19, bf16[512,384]{1,0:T(8,128)(2,1)S(1)} %get-tuple-element.16.refs_2_.mixed, ...), custom_call_target="tpu_custom_call" | custom-call | tf_op jit(solution)/shard_map/mix/pallas_call | solution.py:514
  79.8 15.8 %all_to_all.15.arrived_ref = bf16[4,768,128]{2,1,0:T(8,128)(2,1)S(1)} all-to-all(bf16[4,768,128]{2,1,0:T(8,128)(2,1)S(1)} %mix.1), channel_id=1, replica_groups=mesh['grp'=4,'clu_0'=4,'clu_1'=16,'clu_2'=2] {'grp'}, dimensions={0} | all-to-all | bytes 1572864 | tf_op jit(solution)/shard_map/all_to_all | solution.py:421
  95.6 0.8 last.1
  (5 shorter events, 0.0 us)
Async XLA Ops:
  1.9 19.8 %copy-start.5 = (bf16[2,32,3,256]{3,1,2,0:T(8,128)(2,1)S(1)}, bf16[2,32,3,256]{3,1,2,0:T(8,128)(2,1)}, u32[]{:S(2)}) copy-start(bf16[2,32,3,256]{3,1,2,0:T(8,128)(2,1)} %param.12) | copy-start | bytes 294916
  1.9 21.2 %copy-start.3 = (bf16[784,512]{1,0:T(8,128)(2,1)}, bf16[784,512]{1,0:T(8,128)(2,1)S(1)}, u32[]{:S(2)}) copy-start(bf16[784,512]{1,0:T(8,128)(2,1)S(1)} %tie.4.own_ref.own) | copy-start | bytes 2408452
  2.0 19.7 %collective-permute-start.2 = (bf16[784,512]{1,0:T(8,128)(2,1)S(1)}, bf16[784,512]{1,0:T(8,128)(2,1)S(1)}, u32[]{:S(2)}, u32[]{:S(2)}) collective-permute-start(bf16[784,512]{1,0:T(8,128)(2,1)S(1)} %tie.4.own_ref.own), channel_id=1, source_target_pairs={{0,1},{1,0},{2,3},{3,2},{4,5},{5,4},{6,7},{7,6},{8,9},{9,8},{10,11... | collective-permute-start | bytes 2408456 | tf_op jit(solution)/shard_map/ppermute | solution.py:414
  4.0 17.7 %collective-permute-start.1 = (bf16[784,128]{1,0:T(8,128)(2,1)S(1)}, bf16[784,128]{1,0:T(8,128)(2,1)S(1)}, u32[]{:S(2)}, u32[]{:S(2)}) collective-permute-start(bf16[784,128]{1,0:T(8,128)(2,1)S(1)} %get-tuple-element.12), channel_id=1, source_target_pairs={{0,127},{1,2},{2,1},{3,4},{4,3},{5,6},{6,5},{7,8},{8,7},{9,10},{10... | collective-permute-start | bytes 602120 | tf_op jit(solution)/shard_map/ppermute | solution.py:418
  11.5 25.1 %collective-permute-start.4 = (bf16[784,512]{1,0:T(8,128)(2,1)S(1)}, bf16[784,512]{1,0:T(8,128)(2,1)S(1)}, u32[]{:S(2)}, u32[]{:S(2)}) collective-permute-start(bf16[784,512]{1,0:T(8,128)(2,1)S(1)} %tie.4.own_ref.own), channel_id=1, source_target_pairs={{0,126},{1,3},{2,0},{3,5},{4,2},{5,7},{6,4},{7,9},{8,6},{9,11},{10... | collective-permute-start | bytes 2408456 | tf_op jit(solution)/shard_map/ppermute | solution.py:418
  19.7 18.9 %collective-permute-start = (bf16[784,512]{1,0:T(8,128)(2,1)S(1)}, bf16[784,512]{1,0:T(8,128)(2,1)S(1)}, u32[]{:S(2)}, u32[]{:S(2)}) collective-permute-start(bf16[784,512]{1,0:T(8,128)(2,1)S(1)} %tie.4.own_ref.own), channel_id=1, source_target_pairs={{0,2},{1,127},{2,4},{3,1},{4,6},{5,3},{6,8},{7,5},{8,10},{9,7},{10... | collective-permute-start | bytes 2408456 | tf_op jit(solution)/shard_map/ppermute | solution.py:418
  21.7 1.4 %copy-start.4 = (bf16[784,512]{1,0:T(8,128)(2,1)}, bf16[784,512]{1,0:T(8,128)(2,1)S(1)}, u32[]{:S(2)}) copy-start(bf16[784,512]{1,0:T(8,128)(2,1)S(1)} %collective-permute-done.2.pair_ref.pair) | copy-start | bytes 2408452
  23.2 3.1 %collective-permute-start.3 = (f32[32,128]{1,0:T(8,128)S(1)}, f32[32,128]{1,0:T(8,128)S(1)}, u32[]{:S(2)}, u32[]{:S(2)}) collective-permute-start(f32[32,128]{1,0:T(8,128)S(1)} %get-tuple-element.14), channel_id=1, source_target_pairs={{0,1},{1,0},{2,3},{3,2},{4,5},{5,4},{6,7},{7,6},{8,9},{9,8},{10,11... | collective-permute-start | bytes 49160 | tf_op jit(solution)/shard_map/ppermute | solution.py:414
  27.0 25.5 %all-to-all-start = ((f32[16,32,128]{2,1,0:T(8,128)}), f32[16,32,128]{2,1,0:T(8,128)S(1)}, u32[]{:S(2)}, u32[]{:S(2)}) async-start(f32[16,32,128]{2,1,0:T(8,128)} %broadcast_in_dim.3), calls=%async_computation | async-start | bytes 524288 | tf_op jit(solution)/shard_map/all_to_all | solution.py:421
  36.7 16.7 %copy-start.1 = (bf16[784,512]{1,0:T(8,128)(2,1)}, bf16[784,512]{1,0:T(8,128)(2,1)S(1)}, u32[]{:S(2)}) copy-start(bf16[784,512]{1,0:T(8,128)(2,1)S(1)} %tie.6.far_z.refs_2_) | copy-start | bytes 2408452
  36.7 31.8 %collective-permute-start.5 = (bf16[784,512]{1,0:T(8,128)(2,1)S(1)}, bf16[784,512]{1,0:T(8,128)(2,1)}, u32[]{:S(2)}, u32[]{:S(2)}) collective-permute-start(bf16[784,512]{1,0:T(8,128)(2,1)S(1)} %tie.6.far_z.refs_2_), channel_id=1, source_target_pairs={{0,1},{1,0},{2,3},{3,2},{4,5},{5,4},{6,7},{7,6},{8,9},{9,8},{10,11... | collective-permute-start | bytes 2408456 | tf_op jit(solution)/shard_map/ppermute | solution.py:414
  38.6 29.9 %copy-start = (bf16[784,512]{1,0:T(8,128)(2,1)}, bf16[784,512]{1,0:T(8,128)(2,1)S(1)}, u32[]{:S(2)}) copy-start(bf16[784,512]{1,0:T(8,128)(2,1)S(1)} %tie.5.near_z.refs_1_) | copy-start | bytes 2408452
  38.6 29.9 %collective-permute-start.6 = (bf16[784,512]{1,0:T(8,128)(2,1)S(1)}, bf16[784,512]{1,0:T(8,128)(2,1)S(1)}, u32[]{:S(2)}, u32[]{:S(2)}) collective-permute-start(bf16[784,512]{1,0:T(8,128)(2,1)S(1)} %tie.5.near_z.refs_1_), channel_id=1, source_target_pairs={{0,1},{1,0},{2,3},{3,2},{4,5},{5,4},{6,7},{7,6},{8,9},{9,8},{10,11... | collective-permute-start | bytes 2408456 | tf_op jit(solution)/shard_map/ppermute | solution.py:414
  53.4 22.9 %all-to-all-start.1 = ((f32[32,32,128]{2,1,0:T(8,128)}), f32[32,32,128]{2,1,0:T(8,128)S(1)}, u32[]{:S(2)}, u32[]{:S(2)}) async-start(f32[32,32,128]{2,1,0:T(8,128)} %reduce.1), calls=%async_computation.1 | async-start | bytes 1048576 | tf_op jit(solution)/shard_map/all_to_all | solution.py:421
  60.9 15.3 %collective-permute-start.7 = (bf16[3,64,512]{2,1,0:T(8,128)(2,1)S(1)}, bf16[3,64,512]{2,1,0:T(8,128)(2,1)}, u32[]{:S(2)}, u32[]{:S(2)}) collective-permute-start(bf16[3,64,512]{2,1,0:T(8,128)(2,1)S(1)} %get-tuple-element.15.refs_1_), channel_id=1, source_target_pairs={{0,125},{1,4},{2,127},{3,6},{4,1},{5,8},{6,3},{7,10},{8,5},{9,12},... | collective-permute-start | bytes 589832 | tf_op jit(solution)/shard_map/ppermute | solution.py:418
  75.1 1.2 %copy-start.2 = (f32[768,512]{1,0:T(8,128)}, f32[768,512]{1,0:T(8,128)S(1)}, u32[]{:S(2)}) copy-start(f32[768,512]{1,0:T(8,128)S(1)} %near.1) | copy-start | bytes 4718596
